TPU v7x, 32 devices: a whole 2x2x4 slice. The times are simulated.
32 devices in a mesh: dp: 32 (over z, y, x, core).
Axes of the slice: x: 2, y: 2, z: 4, core: 2. Of those that a mesh axis runs over, the one named last changes fastest.
Arguments:
- images: float32 [192, 196, 768], P('dp'), may hold values from -6 to 6
- mask: int32 [192], P('dp'), may hold values 0 or 1
- cotangent: float32 [192, 196, 768], P('dp'), may hold values from -6 to 6
- w_token_in: float32 [75264], P('dp'), may hold values from -0.4375 to 0.4375
- w_token_out: float32 [75264], P('dp'), may hold values from -0.3125 to 0.3125
- bias_token_in: float32 [384], replicated, may hold values from -3 to 3
- bias_token_out: float32 [196], replicated, may hold values from -3 to 3
- gain_one: float32 [768], P('dp'), may hold values from 0.1 to 1.9
- shift_one: float32 [768], P('dp'), may hold values from -3 to 3
- gain_two: float32 [768], P('dp'), may hold values from 0.1 to 1.9
- shift_two: float32 [768], P('dp'), may hold values from -3 to 3
- w_expand: float32 [3072, 768], P('dp'), may hold values from -0.21875 to 0.21875
- bias_expand: float32 [3072], P('dp'), may hold values from -3 to 3
- w_reduce: float32 [3072, 768], P('dp'), may hold values from -0.109375 to 0.109375
- bias_reduce: float32 [768], P('dp'), may hold values from -3 to 3
Outputs:
- block_output: float32 [192, 196, 768], P('dp')
- image_grad: float32 [192, 196, 768], P('dp')
- grad_token_in: float32 [75264], P('dp')
- grad_token_out: float32 [75264], P('dp')
- grad_bias_token_in: float32 [384], replicated
- grad_bias_token_out: float32 [196], replicated
- grad_gain_one: float32 [768], P('dp')
- grad_shift_one: float32 [768], P('dp')
- grad_gain_two: float32 [768], P('dp')
- grad_shift_two: float32 [768], P('dp')
- grad_expand: float32 [3072, 768], P('dp')
- grad_bias_expand: float32 [3072], P('dp')
- grad_reduce: float32 [3072, 768], P('dp')
- grad_bias_reduce: float32 [768], P('dp')
All inputs are finite; a program needn't handle non-finite values. No bound on the sum of `mask` on one device may be relied on, other than what follows from the above.
Results may differ from a plain program's by a relative error of at most 0.0095.
Values may be sent and summed in bfloat16 or wider, within the bound.
A program may use at most 192 MiB of HBM per device.

v0:
```python
import jax
import jax.numpy as jnp
from jax import lax
from jax.sharding import PartitionSpec as P

EPS = 1e-06


def gelu_exact(v):
    return 0.5 * v * (1.0 + lax.erf(v * 0.7071067811865476))


def gelu_slope(v):
    return 0.5 * (1.0 + lax.erf(v * 0.7071067811865476)) + v * 0.3989422804014327 * jnp.exp(
        -0.5 * v * v
    )


def normalize(v):
    centered = v - jnp.mean(v, axis=-1, keepdims=True)
    scale = lax.rsqrt(jnp.mean(centered * centered, axis=-1, keepdims=True) + EPS)
    return (centered * scale, scale)


def norm_back(grad_in, normed, scale, gain):
    scaled = grad_in * gain
    return scale * (
        scaled
        - jnp.mean(scaled, axis=-1, keepdims=True)
        - normed * jnp.mean(scaled * normed, axis=-1, keepdims=True)
    )


def shards(
    images,
    mask,
    cotangent,
    w_token_in,
    w_token_out,
    bias_token_in,
    bias_token_out,
    gain_one,
    shift_one,
    gain_two,
    shift_two,
    w_expand,
    bias_expand,
    w_reduce,
    bias_reduce,
):
    low_type = jnp.bfloat16
    wide = jnp.float32
    count, patches, width = images.shape
    hidden_tok = bias_token_in.shape[0]
    rows = count * patches
    keep = mask.astype(wide)[:, None, None]
    small_local = (
        w_token_in.astype(low_type),
        w_token_out.astype(low_type),
        gain_one.astype(low_type),
        shift_one.astype(low_type),
        gain_two.astype(low_type),
        shift_two.astype(low_type),
        bias_reduce.astype(low_type),
    )
    channel_local = (
        w_expand.astype(low_type),
        w_reduce.astype(low_type),
        bias_expand.astype(low_type),
    )
    small_all = (
        lax.all_gather(small_local[0], "dp", axis=0, tiled=True),
        lax.all_gather(small_local[1], "dp", axis=0, tiled=True),
        lax.all_gather(small_local[2], "dp", axis=0, tiled=True),
        lax.all_gather(small_local[3], "dp", axis=0, tiled=True),
        lax.all_gather(small_local[4], "dp", axis=0, tiled=True),
        lax.all_gather(small_local[5], "dp", axis=0, tiled=True),
        lax.all_gather(small_local[6], "dp", axis=0, tiled=True),
    )
    tin = small_all[0].reshape(patches, hidden_tok)
    tout = small_all[1].reshape(hidden_tok, patches)
    g_one, b_one, g_two, b_two, c_four = [piece.astype(wide) for piece in small_all[2:]]
    normed_one, scale_one = normalize(images)
    mixed_in = (normed_one * g_one + b_one).astype(low_type)
    pre_t = (
        jnp.einsum("ps,bpd->bsd", tin, mixed_in, preferred_element_type=wide)
        + bias_token_in[None, :, None]
    )
    act_t = gelu_exact(pre_t).astype(low_type)
    middle = (
        images
        + jnp.einsum("sp,bsd->bpd", tout, act_t, preferred_element_type=wide)
        + bias_token_out[None, :, None]
    )
    normed_two, scale_two = normalize(middle.reshape(rows, width))
    zed = (normed_two * g_two + b_two).astype(low_type)
    whole_channel = (
        lax.all_gather(channel_local[0], "dp", axis=0, tiled=True),
        lax.all_gather(channel_local[1], "dp", axis=0, tiled=True),
        lax.all_gather(channel_local[2], "dp", axis=0, tiled=True),
    )
    w_in, w_out, c_in = whole_channel
    pre = (
        jnp.einsum("td,fd->tf", zed, w_in, preferred_element_type=wide) + c_in.astype(wide)[None, :]
    )
    act = gelu_exact(pre).astype(low_type)
    reduced = jnp.dot(act, w_out, preferred_element_type=wide)
    block_output = (middle + (reduced + c_four).reshape(count, patches, width)) * keep
    grad_top = cotangent * keep
    grad_branch = grad_top.reshape(rows, width).astype(low_type)
    grad_c_four = jnp.sum(grad_branch.astype(wide), axis=0)
    small_all = (
        lax.all_gather(small_local[0], "dp", axis=0, tiled=True),
        lax.all_gather(small_local[1], "dp", axis=0, tiled=True),
        lax.all_gather(small_local[2], "dp", axis=0, tiled=True),
        lax.all_gather(small_local[3], "dp", axis=0, tiled=True),
        lax.all_gather(small_local[4], "dp", axis=0, tiled=True),
        lax.all_gather(small_local[5], "dp", axis=0, tiled=True),
        lax.all_gather(small_local[6], "dp", axis=0, tiled=True),
    )
    tin = small_all[0].reshape(patches, hidden_tok)
    tout = small_all[1].reshape(hidden_tok, patches)
    g_one, b_one, g_two, b_two, c_four = [piece.astype(wide) for piece in small_all[2:]]
    whole_channel = (
        lax.all_gather(channel_local[0], "dp", axis=0, tiled=True),
        lax.all_gather(channel_local[1], "dp", axis=0, tiled=True),
        lax.all_gather(channel_local[2], "dp", axis=0, tiled=True),
    )
    w_in, w_out, c_in = whole_channel
    pre = (
        jnp.einsum("td,fd->tf", zed, w_in, preferred_element_type=wide) + c_in.astype(wide)[None, :]
    )
    act = gelu_exact(pre).astype(low_type)
    grad_act = jnp.einsum("td,fd->tf", grad_branch, w_out, preferred_element_type=wide)
    grad_pre = (grad_act * gelu_slope(pre)).astype(low_type)
    grad_zed = jnp.dot(grad_pre, w_in, preferred_element_type=wide)
    grad_in = jnp.einsum("tf,td->fd", grad_pre, zed, preferred_element_type=wide)
    grad_out = jnp.einsum("tf,td->fd", act, grad_branch, preferred_element_type=wide)
    grad_cin = jnp.sum(grad_pre.astype(wide), axis=0)
    grad_zed, grad_win, grad_wout, grad_cin = (grad_zed, grad_in, grad_out, grad_cin)
    grad_g_two = jnp.sum(grad_zed * normed_two, axis=0)
    grad_b_two = jnp.sum(grad_zed, axis=0)
    grad_mid = grad_top + norm_back(grad_zed, normed_two, scale_two, g_two).reshape(
        count, patches, width
    )
    grad_back = grad_mid.astype(low_type)
    grad_c_two = jnp.sum(grad_back.astype(wide), axis=(0, 2))
    grad_tout = jnp.einsum("bsd,bpd->sp", act_t, grad_back, preferred_element_type=wide)
    grad_act_t = jnp.einsum("sp,bpd->bsd", tout, grad_back, preferred_element_type=wide)
    grad_pre_t = (grad_act_t * gelu_slope(pre_t)).astype(low_type)
    grad_c_one = jnp.sum(grad_pre_t.astype(wide), axis=(0, 2))
    grad_tin = jnp.einsum("bpd,bsd->ps", mixed_in, grad_pre_t, preferred_element_type=wide)
    grad_mixed = jnp.einsum("ps,bsd->bpd", tin, grad_pre_t, preferred_element_type=wide)
    grad_g_one = jnp.sum(grad_mixed * normed_one, axis=(0, 1))
    grad_b_one = jnp.sum(grad_mixed, axis=(0, 1))
    image_grad = grad_mid + norm_back(grad_mixed, normed_one, scale_one, g_one)
    bias_sums = lax.psum((grad_c_one, grad_c_two), "dp")
    flat_tin = grad_tin.reshape(patches * hidden_tok)
    flat_tout = grad_tout.reshape(hidden_tok * patches)
    owned = (
        lax.psum_scatter(flat_tin, "dp", scatter_dimension=0, tiled=True),
        lax.psum_scatter(flat_tout, "dp", scatter_dimension=0, tiled=True),
        lax.psum_scatter(grad_g_one, "dp", scatter_dimension=0, tiled=True),
        lax.psum_scatter(grad_b_one, "dp", scatter_dimension=0, tiled=True),
        lax.psum_scatter(grad_g_two, "dp", scatter_dimension=0, tiled=True),
        lax.psum_scatter(grad_b_two, "dp", scatter_dimension=0, tiled=True),
        lax.psum_scatter(grad_win, "dp", scatter_dimension=0, tiled=True),
        lax.psum_scatter(grad_cin, "dp", scatter_dimension=0, tiled=True),
        lax.psum_scatter(grad_wout, "dp", scatter_dimension=0, tiled=True),
        lax.psum_scatter(grad_c_four, "dp", scatter_dimension=0, tiled=True),
    )
    (
        own_tin,
        own_tout,
        own_g_one,
        own_b_one,
        own_g_two,
        own_b_two,
        own_win,
        own_cin,
        own_wout,
        own_c_four,
    ) = owned
    return (
        block_output,
        image_grad,
        own_tin,
        own_tout,
        bias_sums[0],
        bias_sums[1],
        own_g_one,
        own_b_one,
        own_g_two,
        own_b_two,
        own_win,
        own_cin,
        own_wout,
        own_c_four,
    )


def solution(mesh):
    placed = (
        P("dp", None, None),
        P("dp"),
        P("dp", None, None),
        P("dp"),
        P("dp"),
        P(),
        P(),
        P("dp"),
        P("dp"),
        P("dp"),
        P("dp"),
        P("dp", None),
        P("dp"),
        P("dp", None),
        P("dp"),
    )
    return jax.shard_map(
        shards,
        mesh=mesh,
        in_specs=placed,
        out_specs=(
            P("dp", None, None),
            P("dp", None, None),
            P("dp"),
            P("dp"),
            P(),
            P(),
            P("dp"),
            P("dp"),
            P("dp"),
            P("dp"),
            P("dp", None),
            P("dp"),
            P("dp", None),
            P("dp"),
        ),
        check_vma=False,
    )
```

profile of v0, /device:TPU:0, one launch (start us, length us, event | category | flops | bytes accessed | tf_op | source)
XLA Modules:
  0.0 742.0 jit_solution(6735220830884729459)
XLA Ops:
  7.2 0.7 convert_element_type.101
  7.9 0.7 convert_element_type.103
  10.0 1.6 convert_element_type.109
  11.8 1.6 convert_element_type.113
  13.5 0.7 convert_element_type.98
  14.1 0.7 convert_element_type.96
  14.8 0.7 convert_element_type.110
  15.5 0.7 convert_element_type.106
  16.1 0.7 convert_element_type.104
  16.8 0.7 convert_element_type.114
  18.7 42.4 %all-reduce.18 = (bf16[768]{0:T(1024)(128)(2,1)S(1)}, bf16[768]{0:T(1024)(128)(2,1)S(1)}, bf16[3072]{0:T(1024)(128)(2,1)S(1)}, bf16[768]{0:T(1024)(128)(2,1)S(1)...) all-reduce(bf16[768]{0:T(1024)(128)(2,1)S(1)} %dynamic-update-slice.1, ...), channel_id=1, replica_groups=mesh['dp'=32] {'dp'}, use_global_device_ids=true, to_apply=%add.1 | all-reduce | flops 6912 | bytes 27648
  61.1 0.6 convert_element_type.97
  61.7 0.6 convert_element_type.99
  62.3 0.6 convert_element_type.105
  62.9 0.6 convert_element_type.111
  63.5 0.6 convert_element_type.107
  64.0 0.7 convert_element_type.116
  65.3 3.2 convert_reduce_fusion.2
  68.5 1.9 convert_element_type.118
  70.4 2.3 reduce_sum.144
  72.7 2.6 multiply_reduce_fusion.2
  75.3 67.5 %all-reduce.25.cloned.1.call-done = (bf16[75264]{0:T(1024)(128)(2,1)}, bf16[75264]{0:T(1024)(128)(2,1)}) async-done(((bf16[75264]{0:T(1024)(128)(2,1)}, bf16[75264]{0:T(1024)(128)(2,1)}), (bf16[75264]{0:T(1024)(128)(2,1)}, bf16[75264]{0:T(1024)(128)(2,1)})) %all-reduce.25.cloned.1.call-update) | async-done | bytes 301072
  142.8 1.6 reshape.145
  144.5 2.2 reshape.123
  146.7 6.1 fusion.11
  152.8 4.0 fusion.23
  156.8 4.8 reshape.124
  161.6 0.7 broadcast_multiply_fusion.4
  162.3 0.7 div.29
  163.0 2.6 multiply_reduce_fusion.1
  165.6 0.7 rsqrt.21
  166.3 45.2 %all-gather.3.cloned.1.call-done = bf16[3072,768]{1,0:T(8,128)(2,1)} async-done(((bf16[96,768]{1,0:T(8,128)(2,1)}), bf16[3072,768]{1,0:T(8,128)(2,1)}) %all-gather.3.cloned.1.call-update) | async-done | bytes 4718608 | tf_op jit(solution)/shard_map/all_gather | solution.py:98
  211.4 13.3 %multiply_convert_fusion = (bf16[1176,3072]{1,0:T(8,128)(2,1)}, f32[1176,3072]{1,0:T(8,128)}) fusion(f32[3072]{0:T(1024)} %convert_element_type.111, bf16[3072,768]{1,0:T(8,128)(2,1)} %all-gather.3.cloned.1.call-done, f32[1176,768]{1,0:T(8,128)} %reshape.124, f32[768]{0:T(1024)} %convert_element_type.107, f32[768]{0:T(1024)} %convert_element_type.105, ...), kind=kOutput, calls=%fused_computation.7 | convolution fusion | flops 5575256064 | bytes 30035136 | tf_op jit(solution)/shard_map/td,fd->tf/dot_general | solution.py:104
  224.7 52.5 %all-gather.5.cloned.1.call-done = bf16[3072,768]{1,0:T(8,128)(2,1)} async-done(((bf16[96,768]{1,0:T(8,128)(2,1)}), bf16[3072,768]{1,0:T(8,128)(2,1)}) %all-gather.5.cloned.1.call-update) | async-done | bytes 4718608 | tf_op jit(solution)/shard_map/all_gather | solution.py:99
  277.2 13.9 %convert_reduce_fusion = (f32[3072]{0:T(1024)}, bf16[1176,3072]{1,0:T(8,128)(2,1)S(1)}) fusion(f32[1176,3072]{1,0:T(8,128)} %get-tuple-element.52, bf16[1176,768]{1,0:T(8,128)(2,1)} %convert_element_type.118, bf16[3072,768]{1,0:T(8,128)(2,1)} %all-gather.5.cloned.1.call-done), kind=kOutput, calls=%fused_computation.6 | convolution fusion | flops 5592413184 | bytes 28213248 | tf_op jit(solution)/shard_map/td,fd->tf/dot_general | solution.py:134
  291.1 7.4 %multiply_reduce_fusion.3 = (f32[768]{0:T(1024)}, f32[1176]{0:T(1024)S(1)}, f32[1176]{0:T(1024)S(1)}, f32[768]{0:T(1024)}, f32[1176,768]{1,0:T(8,128)S(1)}) fusion(f32[1176,768]{1,0:T(8,128)S(1)} %copy-done.2, f32[1176]{0:T(1024)S(1)} %copy-done.13, f32[1176]{0:T(1024)S(1)} %copy-done.12, f32[768]{0:T(1024)S(1)} %copy-done.17, ...), kind=kOutput, calls=%fused_computation.38 | convolution fusion | flops 5557188608 | bytes 19197312 | tf_op jit(solution)/shard_map/dot_general | solution.py:136
  298.6 2.4 subtract_multiply_fusion
  300.9 4.8 reshape.126
  305.7 4.4 convert_reduce_fusion.3
  310.1 1.9 convolution_bitcast_fusion
  312.0 6.4 convert_reduce_fusion.1
  318.5 1.8 copy-done.31
  320.4 1.3 convolution_bitcast_fusion.1
  321.7 0.7 reshape.127
  322.4 1.1 reshape.128
  323.6 12.9 %fusion.21 = f32[3072,768]{1,0:T(8,128)} fusion(bf16[1176,3072]{1,0:T(8,128)(2,1)} %copy-done.32, f32[1176,768]{1,0:T(8,128)} %reshape.124, f32[768]{0:T(1024)S(1)} %copy-done.25, f32[768]{0:T(1024)S(1)} %copy-done.18, f32[1176]{0:T(1024)S(1)} %copy-done.14, f32[1176]{0:T(1024)S(1)} %copy-done.12), kind=kOutput, calls=%fused_computation.62 | convolution fusion | flops 5553580032 | bytes 20290752 | tf_op jit(solution)/shard_map/tf,td->fd/dot_general | solution.py:137
  336.6 1.4 copy-done.3
  338.0 10.8 %fusion.24 = f32[3072,768]{1,0:T(8,128)} fusion(bf16[1176,3072]{1,0:T(8,128)(2,1)} %get-tuple-element.51, bf16[1176,768]{1,0:T(8,128)(2,1)S(1)} %copy-done.3), kind=kOutput, calls=%fused_computation.64 | convolution fusion | flops 5549064192 | bytes 18468864 | tf_op jit(solution)/shard_map/tf,td->fd/dot_general | solution.py:138
  348.8 0.6 copy-done.27
  349.5 10.7 %convolution_add_fusion.1 = f32[1176,768]{1,0:T(8,128)} fusion(bf16[1176,3072]{1,0:T(8,128)(2,1)} %get-tuple-element.51, bf16[3072,768]{1,0:T(8,128)(2,1)} %all-gather.5.cloned.1.call-done, f32[768]{0:T(1024)S(1)} %convert_element_type.115), kind=kOutput, calls=%fused_computation.24 | convolution fusion | flops 5549967360 | bytes 15559680 | tf_op jit(solution)/shard_map/dot_general | solution.py:107
  360.1 4.8 reshape.125
  365.0 6.9 fusion.14
  371.9 2.4 reduce_sum.155
  374.3 40.3 %all-reduce.16 = (f32[384]{0:T(512)}, f32[196]{0:T(256)}, f32[768]{0:T(1024)S(1)}, f32[768]{0:T(1024)S(1)}, f32[768]{0:T(1024)S(1)}, /*index=5*/f32[768]{0:T(1024)S(1)}, f32[3072]{0:T(1024)S(1)}, f32[768]{0:T(1024)S(1)}) all-reduce(f32[384]{0:T(512)S(1)} %get-tuple-element.53, ...), channel_id=1, replica_groups=mesh['dp'=32] {'dp'}, use_global_device_ids=true, to_apply=%region_11.0 | all-reduce | flops 7492 | bytes 59936 | tf_op jit(solution)/shard_map/psum | solution.py:157
  414.6 0.6 dynamic-slice.2
  415.8 0.6 dynamic-slice.4
  417.0 0.6 dynamic-slice.7
  417.6 0.6 dynamic-slice.6
  418.2 11.5 %multiply_add_fusion = (f32[6,196,768]{2,1,0:T(8,128)}, f32[6,196,768]{2,1,0:T(8,128)}) fusion(f32[6,768,196]{1,2,0:T(8,128)} %get-tuple-element.50, f32[6,196,768]{2,1,0:T(8,128)} %param.15, f32[6,196]{1,0:T(8,128)S(1)} %broadcast_multiply_fusion.2, f32[6,196]{1,0:T(8,128)S(1)} %broadcast_multiply_fusion.3, f32[768]{0:T(1024)S(1)} %copy-done.16, ...), kind=kLoop, calls=%fused_computation.32 | loop fusion | flops 10838016 | bytes 28923288 | tf_op jit(solution)/shard_map/add | solution.py:156
  429.7 20.8 %all-reduce.23.cloned.1.call-done = (f32[75264]{0:T(1024)}, f32[75264]{0:T(1024)}) async-done(((f32[75264]{0:T(1024)}, f32[75264]{0:T(1024)}), (f32[75264]{0:T(1024)}, f32[75264]{0:T(1024)})) %all-reduce.23.cloned.1.call-update) | async-done | bytes 602128
  450.5 1.4 dynamic-slice
  451.9 1.4 dynamic-slice.1
  453.3 139.3 %reduce-scatter.3.cloned.1.call-done = f32[96,768]{1,0:T(8,128)} async-done(((f32[3072,768]{1,0:T(8,128)}), f32[96,768]{1,0:T(8,128)}) %reduce-scatter.3.cloned.1.call-update) | async-done | bytes 294928 | tf_op jit(solution)/shard_map/reduce_scatter | solution.py:167
  592.6 142.1 %reduce-scatter.5.cloned.1.call-done = f32[96,768]{1,0:T(8,128)} async-done(((f32[3072,768]{1,0:T(8,128)}), f32[96,768]{1,0:T(8,128)}) %reduce-scatter.5.cloned.1.call-update) | async-done | bytes 294928 | tf_op jit(solution)/shard_map/reduce_scatter | solution.py:169
  (100 shorter events, 4.8 us)
Async XLA Ops:
  7.2 135.7 %all-reduce.25.cloned.1.call-start = ((), (), s32[]{:S(2)}) async-start(), calls=%async_computation.7 | async-start | bytes 606208
  9.0 0.7 copy-start.7
  9.3 0.7 copy-start.6
  10.0 201.4 %all-gather.3.cloned.1.call-start = ((), (), s32[]{:S(2)}) async-start(), calls=%async_computation.2 | async-start | bytes 4866048 | tf_op jit(solution)/shard_map/all_gather | solution.py:98
  11.7 265.4 %all-gather.5.cloned.1.call-start = ((), (), s32[]{:S(2)}) async-start(), calls=%async_computation.3 | async-start | bytes 4866048 | tf_op jit(solution)/shard_map/all_gather | solution.py:99
  13.4 437.1 %all-reduce.23.cloned.1.call-start = ((), (), s32[]{:S(2)}) async-start(), calls=%async_computation.6 | async-start | bytes 1212416
  64.7 0.6 copy-start.20
  75.3 77.4 %copy-start.10 = (f32[6,196]{1,0:T(8,128)}, f32[6,196]{1,0:T(8,128)S(1)}, u32[]{:S(2)}) copy-start(f32[6,196]{1,0:T(8,128)S(1)} %add_rsqrt_fusion.1) | copy-start | bytes 14116
  146.7 6.1 copy-start
  146.7 6.1 copy-start.4
  146.7 6.1 copy-start.28
  277.2 13.9 %copy-start.2 = (f32[1176,768]{1,0:T(8,128)S(1)}, f32[1176,768]{1,0:T(8,128)}, u32[]{:S(2)}) copy-start(f32[1176,768]{1,0:T(8,128)} %reshape.124) | copy-start | bytes 10838020
  277.2 13.9 %copy-start.12 = (f32[1176]{0:T(1024)S(1)}, f32[1176]{0:T(1024)}, u32[]{:S(2)}) copy-start(f32[1176]{0:T(1024)} %div.29) | copy-start | bytes 14116
  277.2 13.9 %copy-start.13 = (f32[1176]{0:T(1024)S(1)}, f32[1176]{0:T(1024)}, u32[]{:S(2)}) copy-start(f32[1176]{0:T(1024)} %rsqrt.21) | copy-start | bytes 14116
  277.2 13.9 %copy-start.17 = (f32[768]{0:T(1024)S(1)}, f32[768]{0:T(1024)}, u32[]{:S(2)}) copy-start(f32[768]{0:T(1024)} %convert_element_type.105) | copy-start | bytes 9220
  277.2 13.9 %copy-start.29 = (bf16[3072,768]{1,0:T(8,128)(2,1)S(1)}, bf16[3072,768]{1,0:T(8,128)(2,1)}, u32[]{:S(2)}) copy-start(bf16[3072,768]{1,0:T(8,128)(2,1)} %all-gather.3.cloned.1.call-done) | copy-start | bytes 14155780
  291.1 7.5 %copy-start.32 = (bf16[1176,3072]{1,0:T(8,128)(2,1)}, bf16[1176,3072]{1,0:T(8,128)(2,1)S(1)}, u32[]{:S(2)}) copy-start(bf16[1176,3072]{1,0:T(8,128)(2,1)S(1)} %get-tuple-element.56) | copy-start | bytes 21676036
  310.1 1.9 copy-start.5
  310.1 1.9 copy-start.30
  312.0 8.3 %copy-start.1 = (f32[6,196,768]{2,1,0:T(8,128)S(1)}, f32[6,196,768]{2,1,0:T(8,128)}, u32[]{:S(2)}) copy-start(f32[6,196,768]{2,1,0:T(8,128)} %param.15) | copy-start | bytes 10838020
  312.0 8.3 %copy-start.11 = (f32[6,196]{1,0:T(8,128)S(1)}, f32[6,196]{1,0:T(8,128)}, u32[]{:S(2)}) copy-start(f32[6,196]{1,0:T(8,128)} %copy-done.10) | copy-start | bytes 14116
  312.0 8.3 %copy-start.16 = (f32[768]{0:T(1024)S(1)}, f32[768]{0:T(1024)}, u32[]{:S(2)}) copy-start(f32[768]{0:T(1024)} %convert_element_type.97) | copy-start | bytes 9220
  312.0 8.3 %copy-start.26 = (f32[768]{0:T(1024)S(1)}, f32[768]{0:T(1024)}, u32[]{:S(2)}) copy-start(f32[768]{0:T(1024)} %convert_element_type.99) | copy-start | bytes 9220
  318.5 1.8 copy-start.31
  320.4 2.1 copy-start.8
  320.4 3.2 copy-start.14
  320.4 3.2 copy-start.18
  320.4 3.2 copy-start.25
  323.5 269.0 %reduce-scatter.3.cloned.1.call-start = ((), (), s32[]{:S(2)}) async-start(), calls=%async_computation.4 | async-start | bytes 9732096 | tf_op jit(solution)/shard_map/reduce_scatter | solution.py:167
  336.5 1.5 copy-start.3
  336.5 398.1 %reduce-scatter.5.cloned.1.call-start = ((), (), s32[]{:S(2)}) async-start(), calls=%async_computation.5 | async-start | bytes 9732096 | tf_op jit(solution)/shard_map/reduce_scatter | solution.py:169
  348.8 0.7 copy-start.27
  360.1 4.8 copy-start.9
  371.9 2.4 copy-start.15
  371.9 2.4 copy-start.19
  371.9 2.4 copy-start.22
  371.9 2.4 copy-start.23
  371.9 2.4 copy-start.24
  371.9 46.3 %copy-start.21 = (f32[6]{0:T(128)S(1)}, f32[6]{0:T(128)}, u32[]{:S(2)}) copy-start(f32[6]{0:T(128)} %copy-done.20) | copy-start | bytes 76
Sparse Core Ops, SparseCore 0:
  14.0 128.7 all-reduce.24
  146.7 64.6 all-gather.2
  214.7 62.3 all-gather.4
  323.7 126.7 all-reduce.22
  456.8 135.7 reduce-scatter.2
  599.9 134.7 reduce-scatter.4
where the time goes:
time: 745 us; the launch traced here: 742 us
  waiting for transfers between devices  467 us (63%)
  matrix products  95.7 us (13%)
  blocking collectives  82.7 us (11%)
  other arithmetic  44.3 us (6%)
  local copies, waits for them, and re-layouts  36.7 us (5%)
  between operations  14.9 us (2%)
    reduce_scatter x1, waiting for transfers between devices, shards(): lax.psum_scatter(grad_wout, 'dp', scatter_dimension=0, tiled=True)  142 us
    reduce_scatter x1, waiting for transfers between devices, shards(): lax.psum_scatter(grad_win, 'dp', scatter_dimension=0, tiled=True)  139 us
    unnamed x8, waiting for transfers between devices  88.4 us
    all_gather x1, waiting for transfers between devices, shards(): lax.all_gather(channel_local[1], 'dp', axis=0, tiled=True)  52.5 us
    all_gather x1, waiting for transfers between devices, shards(): lax.all_gather(channel_local[0], 'dp', axis=0, tiled=True)  45.2 us
    unnamed x1, blocking collectives  42.4 us
    psum x1, blocking collectives, shards(): bias_sums = lax.psum((grad_c_one, grad_c_two), 'dp')  40.3 us
  transfers between devices with their start and end apart: 6, of which 6 were waited for; matrix products, arithmetic and copies ran while one was open for 17% of the time, Pallas kernels for 0%

commit v1 on v0

--- a/solution.py
+++ b/solution.py
@@ -1,6 +1,8 @@
 import jax
 import jax.numpy as jnp
 from jax import lax
+from jax.experimental import pallas as pl
+from jax.experimental.pallas import tpu as pltpu
 from jax.sharding import PartitionSpec as P
 
 EPS = 1e-06
@@ -29,6 +31,623 @@
         - jnp.mean(scaled, axis=-1, keepdims=True)
         - normed * jnp.mean(scaled * normed, axis=-1, keepdims=True)
     )
+
+
+WIDE = jnp.float32
+LOW = jnp.bfloat16
+MESH = pl.DeviceIdType.MESH
+NT = (((1,), (1,)), ((), ()))
+TN = (((0,), (0,)), ((), ()))
+NN = (((1,), (0,)), ((), ()))
+PLANE = 8
+
+
+def dot(a, b, dims):
+    return lax.dot_general(a, b, dims, preferred_element_type=WIDE)
+
+
+def gelu_parts(v):
+    cdf = 0.5 * (1.0 + lax.erf(v * 0.7071067811865476))
+    return v * cdf, cdf + v * 0.3989422804014327 * jnp.exp(-0.5 * v * v)
+
+
+def padded(v, rows):
+    return jnp.concatenate([v, jnp.zeros((rows - v.shape[0], v.shape[1]), v.dtype)], axis=0)
+
+
+def block_kernel(
+    mask,
+    images,
+    cotangent,
+    w_in,
+    w_out,
+    tin,
+    tin_t,
+    tout,
+    tout_t,
+    vecs,
+    c_one,
+    c_two,
+    c_in,
+    block_out,
+    image_grad,
+    grad_in,
+    grad_out,
+    grad_tin,
+    grad_tout,
+    grad_c_one,
+    grad_c_two,
+    grad_vecs,
+    grad_c_in,
+    im,
+    cot,
+    mixed,
+    act_t,
+    slope_t,
+    mid,
+    total,
+    grad_zed,
+    zed,
+    top,
+    weights,
+    act,
+    grad_pre,
+    c_in_rel,
+    own_sum,
+    keep_sum,
+    send_one,
+    recv_one,
+    send_two,
+    recv_two,
+    send_three,
+    recv_three,
+    send_four,
+    recv_four,
+    in_sem,
+    out_sem,
+    ag_send,
+    ag_recv,
+    rs_send,
+    rs_recv,
+):
+    count, patches, width = im.shape
+    planes = weights.shape[1]
+    shard = w_in.shape[0]
+    half = 4 * shard
+    chunk = 8 * shard
+    pad = mixed.shape[1]
+    pair = zed.shape[1]
+    lot = pair // 2
+    blocks = count // 2
+    me = lax.axis_index("dp")
+    core = me % 2
+    col = (me // 2) % 2
+    row = (me // 4) % 2
+    z = me // PLANE
+    by_core = me + 1 - 2 * core
+    by_x = me + 2 - 4 * col
+    by_y = me + 4 - 8 * row
+
+    def plane_of(k):
+        out, bit = z, 1
+        while bit < planes:
+            out = out + bit * ((k // bit) % 2) * (1 - 2 * ((z // bit) % 2))
+            bit *= 2
+        return out
+
+    def by_z(k):
+        return me + PLANE * (plane_of(k) - z)
+
+    def ag(stage, k, mat):
+        near, far = (by_x, by_y) if mat == 0 else (by_y, by_x)
+        step = 1 if mat == 0 else 2
+        if stage == 0:
+            src, dst, size, to = 0, 0, shard, by_z(k)
+            source = weights.at[mat, 0, pl.ds(src, size)]
+        else:
+            src, dst, size, to = {
+                1: (0, step * shard, shard, near),
+                2: (0, (3 - step) * shard, shard, far),
+                3: (step * shard, 3 * shard, shard, far),
+                4: (0, half, half, by_core),
+            }[stage]
+            source = weights.at[mat, k, pl.ds(src, size)]
+        return pltpu.make_async_remote_copy(
+            src_ref=source,
+            dst_ref=weights.at[mat, k, pl.ds(dst, size)],
+            send_sem=ag_send.at[stage, k, mat],
+            recv_sem=ag_recv.at[stage, k, mat],
+            device_id=(to,),
+            device_id_type=MESH,
+        )
+
+    def rs(stage, k, mat):
+        slot = k % 2
+        near, far = (by_x, by_y) if mat == 0 else (by_y, by_x)
+        src, dst, to = [
+            lambda: (send_one.at[mat], recv_one.at[slot, mat], by_core),
+            lambda: (send_two.at[mat], recv_two.at[slot, mat], near),
+            lambda: (send_three.at[mat], recv_three.at[slot, mat], far),
+            lambda: (send_four.at[slot, mat], recv_four.at[k, mat], by_z(k)),
+        ][stage]()
+        return pltpu.make_async_remote_copy(
+            src_ref=src,
+            dst_ref=dst,
+            send_sem=rs_send.at[stage, k, mat],
+            recv_sem=rs_recv.at[stage, k, mat],
+            device_id=(to,),
+            device_id_type=MESH,
+        )
+
+    def load(b):
+        return (
+            pltpu.make_async_copy(images.at[b], im.at[b], in_sem.at[0, b]),
+            pltpu.make_async_copy(cotangent.at[b], cot.at[b], in_sem.at[1, b]),
+        )
+
+    for b in range(count):
+        for copy in load(b):
+            copy.start()
+    weights[0, 0, 0:shard] = w_in[...].astype(LOW)
+    weights[1, 0, 0:shard] = w_out[...].astype(LOW)
+
+    barrier = pltpu.get_barrier_semaphore()
+    peers = [by_core, by_x, by_y] + [by_z(k) for k in range(1, planes)]
+    for peer in peers:
+        pl.semaphore_signal(barrier, inc=1, device_id=(peer,), device_id_type=MESH)
+    pl.semaphore_wait(barrier, len(peers))
+
+    mats = (0, 1)
+
+    def ag_direct(k):
+        for mat in mats:
+            ag(1, k, mat).start()
+        for mat in mats:
+            ag(2, k, mat).start()
+
+    def ag_forward(k):
+        for mat in mats:
+            ag(1, k, mat).wait_recv()
+            ag(3, k, mat).start()
+
+    def ag_core(k):
+        for mat in mats:
+            ag(2, k, mat).wait_recv()
+            ag(3, k, mat).wait_recv()
+            ag(4, k, mat).start()
+
+    def ag_plane(k):
+        for mat in mats:
+            ag(0, k, mat).wait_recv()
+        ag_direct(k)
+
+    def ag_plane_next(k):
+        for mat in mats:
+            ag(0, k, mat).start()
+
+    def ag_ready(k):
+        for mat in mats:
+            ag(4, k, mat).wait_recv()
+
+    ag_direct(0)
+    ag_plane_next(1)
+
+    gain_one, shift_one = vecs[0:1, :], vecs[1:2, :]
+    gain_two, shift_two, c_four = vecs[2:3, :], vecs[3:4, :], vecs[4:5, :]
+    for k in range(planes):
+        for place in range(PLANE):
+            near = plane_of(k) * PLANE + (
+                (row + (place // 2) % 2) % 2 * 4 + (col + place % 2) % 2 * 2 + (core + place // 4) % 2
+            )
+            c_in_rel[k, :, place * shard : (place + 1) * shard] = c_in[near]
+
+    grad_vecs[...] = jnp.zeros_like(grad_vecs)
+    grad_tin[...] = jnp.zeros_like(grad_tin)
+    grad_tout[...] = jnp.zeros_like(grad_tout)
+    grad_c_one[...] = jnp.zeros_like(grad_c_one)
+    grad_c_two[...] = jnp.zeros_like(grad_c_two)
+
+    def token_forward(b, carry):
+        for copy in load(b):
+            copy.wait()
+        x = im[b]
+        normed, _ = normalize(x)
+        mixed[b] = padded(normed * gain_one + shift_one, pad).astype(LOW)
+        pre_t = dot(tin_t[...], mixed[b], NN) + c_one[...]
+        value, slope = gelu_parts(pre_t)
+        act_t[b] = value.astype(LOW)
+        slope_t[b] = slope.astype(LOW)
+        mid[b] = x + dot(tout_t[...], act_t[b], NN)[0:patches] + c_two[...]
+        return carry
+
+    def channel_inputs(r, carry):
+        parts, tops = [], []
+        for h in range(2):
+            b = 2 * r + h
+            keep = mask[b].astype(WIDE)
+            normed, _ = normalize(mid[b])
+            parts.append(padded(normed * gain_two + shift_two, lot))
+            tops.append(padded(cot[b] * keep, lot))
+        zed[r] = jnp.concatenate(parts, axis=0).astype(LOW)
+        top[r] = jnp.concatenate(tops, axis=0).astype(LOW)
+        grad_vecs[4:5, :] += jnp.sum(top[r].astype(WIDE), axis=0, keepdims=True)
+        return carry
+
+    lax.fori_loop(0, 2, token_forward, 0)
+    ag_forward(0)
+    lax.fori_loop(2, 4, token_forward, 0)
+    ag_plane(1)
+    ag_plane_next(2)
+    lax.fori_loop(4, count, token_forward, 0)
+    ag_core(0)
+    ag_forward(1)
+    lax.fori_loop(0, blocks, channel_inputs, 0)
+    total[...] = jnp.zeros_like(total)
+    grad_zed[...] = jnp.zeros_like(grad_zed)
+
+    def rs_two(k):
+        for mat in mats:
+            rs(0, k, mat).wait_recv()
+            own_sum[mat] += recv_one[k % 2, mat].astype(WIDE)
+            if mat == 0:
+                first, second = (1, 2), (3, 4)
+            else:
+                first, second = (2, 3), (3, 4)
+
+            @pl.when(k > 0)
+            def _():
+                rs(1, k - 1, mat).wait_send()
+
+            send_two[mat, 0:shard] = own_sum[mat, first[0] * shard : first[1] * shard].astype(LOW)
+            send_two[mat, shard : 2 * shard] = own_sum[mat, second[0] * shard : second[1] * shard].astype(LOW)
+            rs(1, k, mat).start()
+
+    def rs_three(k):
+        for mat in mats:
+            rs(1, k, mat).wait_recv()
+            other = 2 if mat == 0 else 1
+
+            @pl.when(k > 0)
+            def _():
+                rs(2, k - 1, mat).wait_send()
+
+            keep_sum[mat] = own_sum[mat, 0:shard] + recv_two[k % 2, mat, 0:shard].astype(WIDE)
+            send_three[mat] = (
+                own_sum[mat, other * shard : (other + 1) * shard]
+                + recv_two[k % 2, mat, shard : 2 * shard].astype(WIDE)
+            ).astype(LOW)
+            rs(2, k, mat).start()
+
+    def rs_four(k):
+        for mat in mats:
+            rs(2, k, mat).wait_recv()
+            summed = keep_sum[mat] + recv_three[k % 2, mat].astype(WIDE)
+            result = grad_in if mat == 0 else grad_out
+
+            @pl.when(k == 0)
+            def _():
+                result[...] = summed
+
+            @pl.when(k > 0)
+            def _():
+                @pl.when(k > 2)
+                def _():
+                    rs(3, k - 2, mat).wait_send()
+
+                send_four[k % 2, mat] = summed.astype(LOW)
+                rs(3, k, mat).start()
+
+    def rs_last():
+        for mat in mats:
+            result = grad_in if mat == 0 else grad_out
+            for k in range(1, planes):
+                rs(3, k, mat).wait_recv()
+                result[...] += recv_four[k, mat].astype(WIDE)
+
+    tile = chunk // 3
+
+    def channel_chunk(k, carry):
+        ag_ready(k)
+
+        def rows(r, inner):
+            for s in range(3):
+                part = slice(s * tile, (s + 1) * tile)
+                pre = dot(zed[r], weights[0, k, part], NT) + c_in_rel[k, :, part]
+                value, slope = gelu_parts(pre)
+                act[pl.ds(r * pair, pair), part] = value.astype(LOW)
+                back = (dot(top[r], weights[1, k, part], NT) * slope).astype(LOW)
+                grad_pre[pl.ds(r * pair, pair), part] = back
+            up = dot(act[pl.ds(r * pair, pair), :], weights[1, k], NN)
+            down = dot(grad_pre[pl.ds(r * pair, pair), :], weights[0, k], NN)
+            for h in range(2):
+                total[2 * r + h] += up[h * lot : h * lot + patches]
+                grad_zed[2 * r + h] += down[h * lot : h * lot + patches]
+
+            @pl.when((r == 0) & (k + 1 < planes) & (k > 0))
+            def _():
+                ag_forward(k + 1)
+
+            @pl.when((r == 2) & (k > 0))
+            def _():
+                rs_three(k - 1)
+
+            return inner
+
+        lax.fori_loop(0, blocks, rows, 0)
+
+        @pl.when(k + 1 < planes)
+        def _():
+            ag_core(k + 1)
+
+        @pl.when(k + 2 < planes)
+        def _():
+            ag_plane(k + 2)
+
+        @pl.when(k + 3 < planes)
+        def _():
+            ag_plane_next(k + 3)
+
+        back_sum = jnp.sum(grad_pre[...].astype(WIDE), axis=0, keepdims=True)
+        for place in range(PLANE):
+            near = plane_of(k) * PLANE + (
+                (row + (place // 2) % 2) % 2 * 4 + (col + place % 2) % 2 * 2 + (core + place // 4) % 2
+            )
+            grad_c_in[near] = back_sum[:, place * shard : (place + 1) * shard]
+
+        flat_top = top[...].reshape(blocks * pair, width)
+        flat_zed = zed[...].reshape(blocks * pair, width)
+        for mat, left, right in ((1, act, flat_top), (0, grad_pre, flat_zed)):
+            @pl.when(k > 0)
+            def _():
+                rs(0, k - 1, mat).wait_send()
+
+            send_one[mat] = dot(left[:, half:chunk], right, TN).astype(LOW)
+            rs(0, k, mat).start()
+
+        @pl.when(k > 0)
+        def _():
+            rs_four(k - 1)
+
+        for mat, left, right in ((1, act, flat_top), (0, grad_pre, flat_zed)):
+            own_sum[mat] = dot(left[:, 0:half], right, TN)
+        rs_two(k)
+        return carry
+
+    lax.fori_loop(0, planes, channel_chunk, 0)
+
+    def store(b):
+        return (
+            pltpu.make_async_copy(total.at[b], block_out.at[b], out_sem.at[0, b]),
+            pltpu.make_async_copy(grad_zed.at[b], image_grad.at[b], out_sem.at[1, b]),
+        )
+
+    def token_backward(b, carry):
+        keep = mask[b].astype(WIDE)
+        total[b] = (mid[b] + total[b] + c_four) * keep
+        store(b)[0].start()
+        normed, scale = normalize(mid[b])
+        down = grad_zed[b]
+        grad_vecs[2:3, :] += jnp.sum(down * normed, axis=0, keepdims=True)
+        grad_vecs[3:4, :] += jnp.sum(down, axis=0, keepdims=True)
+        grad_mid = cot[b] * keep + norm_back(down, normed, scale, gain_two)
+        back = padded(grad_mid, pad).astype(LOW)
+        grad_c_two[...] += jnp.sum(back.astype(WIDE), axis=1, keepdims=True)
+        grad_tout[...] += dot(act_t[b], back, NT)
+        back_t = (dot(tout[...], back, NN) * slope_t[b].astype(WIDE)).astype(LOW)
+        grad_c_one[...] += jnp.sum(back_t.astype(WIDE), axis=1, keepdims=True)
+        grad_tin[...] += dot(mixed[b], back_t, NT)
+        grad_mixed = dot(tin[...], back_t, NN)[0:patches]
+        normed, scale = normalize(im[b])
+        grad_vecs[0:1, :] += jnp.sum(grad_mixed * normed, axis=0, keepdims=True)
+        grad_vecs[1:2, :] += jnp.sum(grad_mixed, axis=0, keepdims=True)
+        grad_zed[b] = grad_mid + norm_back(grad_mixed, normed, scale, gain_one)
+        store(b)[1].start()
+
+        @pl.when(b == count // 2)
+        def _():
+            rs_three(planes - 1)
+
+        return carry
+
+    lax.fori_loop(0, count, token_backward, 0)
+    rs_four(planes - 1)
+    rs_last()
+
+    for mat in mats:
+        for k in range(planes):
+            for stage in range(5):
+                if stage > 0 or k > 0:
+                    ag(stage, k, mat).wait_send()
+        for stage in range(3):
+            rs(stage, planes - 1, mat).wait_send()
+        for k in range(max(1, planes - 2), planes):
+            rs(3, k, mat).wait_send()
+    for b in range(count):
+        for copy in store(b):
+            copy.wait()
+
+
+def fast_shards(
+    images,
+    mask,
+    cotangent,
+    w_token_in,
+    w_token_out,
+    bias_token_in,
+    bias_token_out,
+    gain_one,
+    shift_one,
+    gain_two,
+    shift_two,
+    w_expand,
+    bias_expand,
+    w_reduce,
+    bias_reduce,
+):
+    devices = lax.axis_size("dp")
+    planes = devices // PLANE
+    count, patches, width = images.shape
+    hidden_tok = bias_token_in.shape[0]
+    shard = w_expand.shape[0]
+    pad = -(-patches // 16) * 16
+    lot = -(-patches // 8) * 8
+    pair = 2 * lot
+    blocks = count // 2
+    chunk = 8 * shard
+    half = 4 * shard
+
+    small = [w_token_in, w_token_out, gain_one, shift_one, gain_two, shift_two, bias_reduce, bias_expand]
+    sizes = [piece.shape[0] for piece in small]
+    packed = jnp.concatenate([piece.astype(LOW) for piece in small])
+    gathered = lax.all_gather(packed, "dp", axis=0)
+    ends = [sum(sizes[: i + 1]) for i in range(len(sizes))]
+    pieces = [gathered[:, end - size : end].reshape(-1) for end, size in zip(ends, sizes)]
+    tin = jnp.pad(pieces[0].reshape(patches, hidden_tok), ((0, pad - patches), (0, 0)))
+    tout = jnp.pad(pieces[1].reshape(hidden_tok, patches), ((0, 0), (0, pad - patches)))
+    vecs = jnp.concatenate([jnp.stack(pieces[2:7]), jnp.zeros((3, width), LOW)]).astype(WIDE)
+    c_in = pieces[7].reshape(devices, 1, shard).astype(WIDE)
+
+    vmem = pl.BlockSpec(memory_space=pltpu.VMEM)
+    hbm = pl.BlockSpec(memory_space=pl.ANY)
+    shape = jax.ShapeDtypeStruct
+    outs = pl.pallas_call(
+        block_kernel,
+        out_shape=(
+            shape(images.shape, WIDE),
+            shape(images.shape, WIDE),
+            shape(w_expand.shape, WIDE),
+            shape(w_reduce.shape, WIDE),
+            shape((pad, hidden_tok), WIDE),
+            shape((hidden_tok, pad), WIDE),
+            shape((hidden_tok, 1), WIDE),
+            shape((pad, 1), WIDE),
+            shape((8, width), WIDE),
+            shape((devices, 1, shard), WIDE),
+        ),
+        in_specs=[pl.BlockSpec(memory_space=pltpu.SMEM), hbm, hbm] + [vmem] * 10,
+        out_specs=[hbm, hbm] + [vmem] * 8,
+        scratch_shapes=[
+            pltpu.VMEM(images.shape, WIDE),
+            pltpu.VMEM(images.shape, WIDE),
+            pltpu.VMEM((count, pad, width), LOW),
+            pltpu.VMEM((count, hidden_tok, width), LOW),
+            pltpu.VMEM((count, hidden_tok, width), LOW),
+            pltpu.VMEM(images.shape, WIDE),
+            pltpu.VMEM(images.shape, WIDE),
+            pltpu.VMEM(images.shape, WIDE),
+            pltpu.VMEM((blocks, pair, width), LOW),
+            pltpu.VMEM((blocks, pair, width), LOW),
+            pltpu.VMEM((2, planes, chunk, width), LOW),
+            pltpu.VMEM((blocks * pair, chunk), LOW),
+            pltpu.VMEM((blocks * pair, chunk), LOW),
+            pltpu.VMEM((planes, 1, chunk), WIDE),
+            pltpu.VMEM((2, half, width), WIDE),
+            pltpu.VMEM((2, shard, width), WIDE),
+            pltpu.VMEM((2, half, width), LOW),
+            pltpu.VMEM((2, 2, half, width), LOW),
+            pltpu.VMEM((2, 2 * shard, width), LOW),
+            pltpu.VMEM((2, 2, 2 * shard, width), LOW),
+            pltpu.VMEM((2, shard, width), LOW),
+            pltpu.VMEM((2, 2, shard, width), LOW),
+            pltpu.VMEM((2, 2, shard, width), LOW),
+            pltpu.VMEM((planes, 2, shard, width), LOW),
+            pltpu.SemaphoreType.DMA((2, count)),
+            pltpu.SemaphoreType.DMA((2, count)),
+            pltpu.SemaphoreType.DMA((5, planes, 2)),
+            pltpu.SemaphoreType.DMA((5, planes, 2)),
+            pltpu.SemaphoreType.DMA((4, planes, 2)),
+            pltpu.SemaphoreType.DMA((4, planes, 2)),
+        ],
+        compiler_params=pltpu.CompilerParams(
+            collective_id=0, has_side_effects=True, vmem_limit_bytes=63 * 2**20
+        ),
+    )(
+        mask,
+        images,
+        cotangent,
+        w_expand,
+        w_reduce,
+        tin,
+        tin.T,
+        tout,
+        tout.T,
+        vecs,
+        bias_token_in[:, None],
+        bias_token_out[:, None],
+        c_in,
+    )
+    block_output, image_grad, own_win, own_wout, g_tin, g_tout, g_c1, g_c2, g_vecs, g_cin = outs
+    bias_sums = lax.psum((g_c1[:, 0], g_c2[:patches, 0]), "dp")
+    flat = [
+        g_tin[:patches].reshape(devices, -1),
+        g_tout[:, :patches].reshape(devices, -1),
+        *[g_vecs[i].reshape(devices, -1) for i in range(5)],
+        g_cin.reshape(devices, -1),
+    ]
+    mine = lax.psum_scatter(jnp.concatenate(flat, axis=1), "dp", scatter_dimension=0, tiled=True)[0]
+    own = [mine[end - size : end] for end, size in zip(ends, sizes)]
+    return (
+        block_output,
+        image_grad,
+        own[0],
+        own[1],
+        bias_sums[0],
+        bias_sums[1],
+        own[2],
+        own[3],
+        own[4],
+        own[5],
+        own_win,
+        own[7],
+        own_wout,
+        own[6],
+    )
+
+
+def fits(devices):
+    planes = devices // PLANE
+    return devices % PLANE == 0 and planes & (planes - 1) == 0 and planes >= 2
+
+
+def choose(
+    images,
+    mask,
+    cotangent,
+    w_token_in,
+    w_token_out,
+    bias_token_in,
+    bias_token_out,
+    gain_one,
+    shift_one,
+    gain_two,
+    shift_two,
+    w_expand,
+    bias_expand,
+    w_reduce,
+    bias_reduce,
+):
+    args = (
+        images,
+        mask,
+        cotangent,
+        w_token_in,
+        w_token_out,
+        bias_token_in,
+        bias_token_out,
+        gain_one,
+        shift_one,
+        gain_two,
+        shift_two,
+        w_expand,
+        bias_expand,
+        w_reduce,
+        bias_reduce,
+    )
+    shard = w_expand.shape[0]
+    whole = shard % 16 == 0 and (4 * shard) % 128 == 0 and images.shape[0] % 2 == 0
+    if fits(lax.axis_size("dp")) and whole:
+        return fast_shards(*args)
+    return shards(*args)
 
 
 def shards(
@@ -218,7 +837,7 @@
         P("dp"),
     )
     return jax.shard_map(
-        shards,
+        choose,
         mesh=mesh,
         in_specs=placed,
         out_specs=(

time: 745 us -> 415 us (0.56)
  waiting for transfers between devices: 467 us -> 214 us
  Pallas kernels: 0 us -> 108 us
  matrix products: 95.7 us -> 0 us
  blocking collectives: 82.7 us -> 43.8 us
  other arithmetic: 44.3 us -> 6.78 us
  local copies, waits for them, and re-layouts: 36.7 us -> 28 us
    reduce_scatter x2 -> x0, waiting for transfers between devices: 281 us -> none  [the longest x1 142 us: shards(): lax.psum_scatter(grad_wout, 'dp', scatter_dimension=0, tiled=True)]
    unnamed x8 -> x4, waiting for transfers between devices: 88.4 us -> 214 us
    pallas_call x0 -> x1, Pallas kernels: none -> 108 us  [fast_shards(): pl.pallas_call(block_kernel, out_shape=(shape(images.shape, WIDE), shape(...]
    all_gather x2 -> x0, waiting for transfers between devices: 97.6 us -> none  [the longest x1 52.5 us: shards(): lax.all_gather(channel_local[1], 'dp', axis=0, tiled=True)]
    dot_general x12 -> x0, matrix products: 95.7 us -> none  [the longest x1 13.9 us: shards(): jnp.einsum('td,fd->tf', grad_branch, w_out, preferred_element_type=wide)]
    unnamed x1 -> x0, blocking collectives: 42.4 us -> none
    reshape x7 -> x2, local copies, waits for them, and re-layouts: 20 us -> 1.44 us  [the longest x1 1.19 us: fast_shards(): g_tout[:, :patches].reshape(devices, -1)]
    reduce_sum x6 -> x0, other arithmetic: 17.4 us -> none  [the longest x2 5.17 us: normalize(): jnp.mean(centered * centered, axis=-1, keepdims=True) + EPS]
  transfers between devices with their start and end apart: 6 -> 2, of which waited for: 6 -> 2; matrix products, arithmetic and copies ran while one was open for 17% -> 1% of each run, Pallas kernels for 0% -> 0%
where the time goes in v1:
time: 415 us; the launch traced here: 414 us
  waiting for transfers between devices  214 us (52%)
  Pallas kernels  108 us (26%)
  blocking collectives  43.8 us (11%)
  local copies, waits for them, and re-layouts  28 us (7%)
  between operations  14.3 us (3%)
  other arithmetic  6.78 us (2%)
    unnamed x4, waiting for transfers between devices  214 us
    pallas_call x1, Pallas kernels, fast_shards(): pl.pallas_call(block_kernel, out_shape=(shape(images.shape, WIDE), shape(...  108 us
    psum x1, blocking collectives, fast_shards(): bias_sums = lax.psum((g_c1[:, 0], g_c2[:patches, 0]), 'dp')  43.8 us
    unnamed x20, local copies, waits for them, and re-layouts  8.95 us
  transfers between devices with their start and end apart: 2, of which 2 were waited for; matrix products, arithmetic and copies ran while one was open for 1% of the time, Pallas kernels for 0%

profile of v1, /device:TPU:0, one launch (start us, length us, event | category | flops | bytes accessed | tf_op | source)
XLA Modules:
  0.0 414.4 jit_solution(16279296733181357891)
XLA Ops:
  7.2 0.0 all-reduce.8.cloned.1.call-start
  7.2 0.7 convert_element_type.36
  7.9 0.7 convert_element_type.37
  8.7 0.7 convert_element_type.38
  9.3 0.7 convert_element_type.39
  10.0 0.7 convert_element_type.40
  10.6 0.7 convert_element_type.41
  11.3 0.7 convert_element_type.42
  11.9 0.7 convert_element_type.43
  12.6 0.1 concatenate.9
  12.7 0.4 dynamic-update-slice
  13.1 0.0 copy-start.1
  13.1 0.7 copy-done.1
  13.8 0.0 all-reduce.8.cloned.1.call-update
  13.8 0.0 all-reduce.10.cloned.1.call-start
  13.9 1.5 broadcast_in_dim.12.c_one
  15.4 1.4 copy.44.c_two
  16.8 125.5 %all-reduce.8.cloned.1.call-done = bf16[157440]{0:T(1024)(128)(2,1)} async-done(((bf16[157440]{0:T(1024)(128)(2,1)}), bf16[157440]{0:T(1024)(128)(2,1)}) %all-reduce.8.cloned.1.call-update) | async-done | bytes 314896
  142.3 1.4 reshape.51
  143.8 0.1 fusion
  143.9 0.1 fusion.1
  144.0 0.3 reshape_reshape.7
  144.3 0.1 copy.39
  144.5 0.1 copy.45
  144.6 0.7 pad_bitcast_fusion.1.tin_t
  145.3 0.3 reshape_reshape.8
  145.6 0.1 copy.40
  145.7 0.1 copy.46
  145.9 0.7 pad_bitcast_fusion.tout_t
  146.6 0.7 slice_convert_fusion
  147.3 0.1 stack_reshape.15
  147.4 0.1 stack_reshape.16
  147.5 0.1 stack_reshape.17
  147.6 0.1 stack_reshape.18
  147.7 0.1 stack_reshape.19
  147.8 0.6 convert_element_type.44.vecs
  148.4 0.7 pad.9.clone.tout
  149.1 0.7 pad.8.clone.tin
  149.8 108.0 %shard_map.254 = (f32[6,196,768]{2,1,0:T(8,128)}, f32[6,196,768]{2,1,0:T(8,128)}, f32[96,768]{1,0:T(8,128)}, f32[96,768]{1,0:T(8,128)}, f32[208,384]{1,0:T(8,128...) custom-call(s32[6]{0:T(128)} %mask.1, ...), custom_call_target="tpu_custom_call" | custom-call | tf_op jit(solution)/shard_map/pallas_call | solution.py:513
  257.8 0.0 copy-start.4
  257.8 0.0 copy-start.5
  257.8 1.0 slice_reduce_fusion.1
  258.8 0.1 reshape_squeeze.15
  258.9 0.1 reshape_squeeze.16
  259.0 0.1 reshape_squeeze.17
  259.1 0.1 reshape_squeeze.18
  259.2 0.1 reshape_squeeze.19
  259.3 1.0 slice.104
  260.3 0.3 reshape.47
  260.5 1.2 reshape.48
  261.7 1.8 concatenate.11
  263.5 0.0 all-reduce.10.cloned.1.call-update
  263.5 0.0 copy-done.4
  263.5 0.1 reduce.7
  263.7 0.1 slice_reduce_fusion
  263.8 43.8 %all-reduce.4 = (f32[384]{0:T(512)}, f32[196]{0:T(256)}) all-reduce(f32[384]{0:T(512)S(1)} %reduce.7, f32[196]{0:T(256)S(1)} %slice_reduce_fusion), channel_id=1, replica_groups=mesh['dp'=32] {'dp'}, use_global_device_ids=true, to_apply=%region_1.2 | all-reduce | flops 580 | bytes 4640 | tf_op jit(solution)/shard_map/psum | solution.py:580
  307.6 88.0 %all-reduce.10.cloned.1.call-done = f32[32,4920]{1,0:T(8,128)} async-done(((f32[32,4920]{1,0:T(8,128)}), f32[32,4920]{1,0:T(8,128)}) %all-reduce.10.cloned.1.call-update) | async-done | bytes 629776
  395.6 1.7 dynamic-slice_reduce_fusion
  397.2 1.3 dynamic-slice_bitcast_fusion.1
  398.5 1.5 dynamic-slice_bitcast_fusion
  400.0 4.3 %copy.54 = f32[6,196,768]{2,1,0:T(8,128)} copy(f32[6,196,768]{2,1,0:T(8,128)} %get-tuple-element.69) | data formatting | bytes 7225344
  404.3 1.8 copy.55
  406.1 0.7 copy.56
  406.9 0.7 copy.57
  (10 shorter events, 0.1 us)
Async XLA Ops:
  7.2 135.2 %all-reduce.8.cloned.1.call-start = ((), (), s32[]{:S(2)}) async-start(), calls=%async_computation | async-start | bytes 630784
  13.1 0.7 copy-start.1
  13.8 381.7 %all-reduce.10.cloned.1.call-start = ((), (), s32[]{:S(2)}) async-start(), calls=%async_computation.1 | async-start | bytes 1277952
  257.8 5.7 %copy-start.4 = (f32[384,1]{1,0:T(8,128)S(1)}, f32[384,1]{1,0:T(8,128)}, u32[]{:S(2)}) copy-start(f32[384,1]{1,0:T(8,128)} %get-tuple-element.30) | copy-start | bytes 4612
  257.8 5.9 %copy-start.5 = (f32[208,1]{1,0:T(8,128)S(1)}, f32[208,1]{1,0:T(8,128)}, u32[]{:S(2)}) copy-start(f32[208,1]{1,0:T(8,128)} %get-tuple-element.31) | copy-start | bytes 2500
  400.0 4.3 %copy-start = (f32[6,196,768]{2,1,0:T(8,128)S(1)}, f32[6,196,768]{2,1,0:T(8,128)}, u32[]{:S(2)}) copy-start(f32[6,196,768]{2,1,0:T(8,128)} %get-tuple-element.70) | copy-start | bytes 10838020
  404.3 1.8 copy-start.3
  404.3 2.6 copy-start.2
Sparse Core Ops, SparseCore 0:
  14.0 128.3 all-reduce.7
  263.6 131.9 all-reduce.9

commit v2 on v1

--- a/solution.py
+++ b/solution.py
@@ -1,3 +1,5 @@
+import math
+
 import jax
 import jax.numpy as jnp
 from jax import lax
@@ -61,24 +63,22 @@
     cotangent,
     w_in,
     w_out,
-    tin,
-    tin_t,
-    tout,
-    tout_t,
-    vecs,
+    tin_own,
+    tout_own,
+    gain_one_own,
+    shift_one_own,
+    gain_two_own,
+    shift_two_own,
+    c_four_own,
+    c_in_own,
     c_one,
     c_two,
-    c_in,
     block_out,
     image_grad,
     grad_in,
     grad_out,
-    grad_tin,
-    grad_tout,
-    grad_c_one,
-    grad_c_two,
-    grad_vecs,
-    grad_c_in,
+    small_out,
+    biases_out,
     im,
     cot,
     mixed,
@@ -103,12 +103,37 @@
     recv_three,
     send_four,
     recv_four,
+    tin,
+    tin_t,
+    tout,
+    tout_t,
+    vecs,
+    c_in,
+    lines,
+    small_own,
+    small_all,
+    grad_tin,
+    grad_tout,
+    grad_vecs,
+    grad_c_in,
+    small_sum,
+    small_core,
+    small_plane,
+    small_z,
+    biases,
+    biases_in,
     in_sem,
     out_sem,
     ag_send,
     ag_recv,
     rs_send,
     rs_recv,
+    sg_send,
+    sg_recv,
+    ss_send,
+    ss_recv,
+    bs_send,
+    bs_recv,
 ):
     count, patches, width = im.shape
     planes = weights.shape[1]
@@ -127,6 +152,7 @@
     by_core = me + 1 - 2 * core
     by_x = me + 2 - 4 * col
     by_y = me + 4 - 8 * row
+    by_both = by_x + by_y - me
 
     def plane_of(k):
         out, bit = z, 1
@@ -179,20 +205,91 @@
             device_id_type=MESH,
         )
 
+    def small_gather(stage, k):
+        src, dst, to = [
+            lambda: (small_all.at[0, 0], small_all.at[0, k], by_z(k)),
+            lambda: (small_all.at[0], small_all.at[k], (me, by_x, by_y, by_both)[k]),
+            lambda: (small_all.at[pl.ds(0, 4)], small_all.at[pl.ds(4, 4)], by_core),
+        ][stage]()
+        return pltpu.make_async_remote_copy(
+            src_ref=src,
+            dst_ref=dst,
+            send_sem=sg_send.at[stage, k],
+            recv_sem=sg_recv.at[stage, k],
+            device_id=(to,),
+            device_id_type=MESH,
+        )
+
+    def small_reduce(stage, k):
+        src, dst, to = [
+            lambda: (small_all.at[pl.ds(4, 4)], small_core, by_core),
+            lambda: (small_all.at[k], small_plane.at[k], (me, by_x, by_y, by_both)[k]),
+            lambda: (small_all.at[0, k], small_z.at[k], by_z(k)),
+        ][stage]()
+        return pltpu.make_async_remote_copy(
+            src_ref=src,
+            dst_ref=dst,
+            send_sem=ss_send.at[stage, k],
+            recv_sem=ss_recv.at[stage, k],
+            device_id=(to,),
+            device_id_type=MESH,
+        )
+
+    def bias_reduce(stage, k):
+        to = [lambda: by_core, lambda: (me, by_x, by_y, by_both)[k], lambda: by_z(k)][stage]()
+        return pltpu.make_async_remote_copy(
+            src_ref=biases.at[stage],
+            dst_ref=biases_in.at[stage, k],
+            send_sem=bs_send.at[stage, k],
+            recv_sem=bs_recv.at[stage, k],
+            device_id=(to,),
+            device_id_type=MESH,
+        )
+
+    unit = tin_own.shape[1]
+    lines_in = tin_own.shape[0]
+    first_lines = (lines_in + 1) // 2
+    lines_out = tout_own.shape[0]
+    own_vec = gain_one_own.shape[1]
+    hidden_tok = c_one.shape[1]
+    turns = hidden_tok // unit
+    devices = planes * PLANE
+
+    def place_of(d):
+        dz, dy, dx, dc = d // PLANE, (d // 4) % 2, (d // 2) % 2, d % 2
+        far = (dc + core) % 2 * 4 + (dy + row) % 2 * 2 + (dx + col) % 2
+        k, bit = 0, 1
+        while bit < planes:
+            k = k + bit * ((dz // bit + z // bit) % 2)
+            bit *= 2
+        return far, k
+
     def load(b):
         return (
             pltpu.make_async_copy(images.at[b], im.at[b], in_sem.at[0, b]),
-            pltpu.make_async_copy(cotangent.at[b], cot.at[b], in_sem.at[1, b]),
+            pltpu.make_async_copy(cotangent.at[b], total.at[b], in_sem.at[1, b]),
         )
+
+    def reload(b):
+        return pltpu.make_async_copy(cotangent.at[b], cot.at[b % 2], in_sem.at[2, b])
 
     for b in range(count):
         for copy in load(b):
             copy.start()
+    small_own[...] = jnp.zeros_like(small_own)
+    small_own[0:first_lines, 0:unit] = tin_own[0:first_lines, :]
+    small_own[0 : lines_in - first_lines, 64 : 64 + unit] = tin_own[first_lines:lines_in, :]
+    for i, piece in enumerate((gain_one_own, shift_one_own, gain_two_own, shift_two_own, c_four_own)):
+        small_own[24 + i : 25 + i, 64 : 64 + own_vec] = piece[...]
+    small_own[31:32, 0:shard] = c_in_own[...]
+    small_own[32 : 32 + lines_out, :] = tout_own[:, 0:128]
+    small_own[48 : 48 + lines_out, 0 : patches - 128] = tout_own[:, 128:patches]
+    small_all[0, 0] = small_own[...].astype(LOW)
     weights[0, 0, 0:shard] = w_in[...].astype(LOW)
     weights[1, 0, 0:shard] = w_out[...].astype(LOW)
 
     barrier = pltpu.get_barrier_semaphore()
-    peers = [by_core, by_x, by_y] + [by_z(k) for k in range(1, planes)]
+    peers = [by_core, by_x, by_y, by_both] + [by_z(k) for k in range(1, planes)]
     for peer in peers:
         pl.semaphore_signal(barrier, inc=1, device_id=(peer,), device_id_type=MESH)
     pl.semaphore_wait(barrier, len(peers))
@@ -229,8 +326,66 @@
         for mat in mats:
             ag(4, k, mat).wait_recv()
 
-    ag_direct(0)
+    for k in range(1, planes):
+        small_gather(0, k).start()
+    for mat in mats:
+        ag(1, 0, mat).start()
+
+    grad_vecs[...] = jnp.zeros_like(grad_vecs)
+    grad_tin[...] = jnp.zeros_like(grad_tin)
+    grad_tout[...] = jnp.zeros_like(grad_tout)
+
+    def channel_top(r, carry):
+        tops = []
+        for h in range(2):
+            b = 2 * r + h
+            load(b)[1].wait()
+            tops.append(padded(total[b] * mask[b].astype(WIDE), lot))
+        top[r] = jnp.concatenate(tops, axis=0).astype(LOW)
+        grad_vecs[4:5, :] += jnp.sum(top[r].astype(WIDE), axis=0, keepdims=True)
+        return carry
+
+    def first_norm(b, carry):
+        load(b)[0].wait()
+        mid[b] = normalize(im[b])[0]
+        return carry
+
+    lax.fori_loop(0, blocks, channel_top, 0)
+    for k in range(1, planes):
+        small_gather(0, k).wait_recv()
+    for k in range(1, 4):
+        small_gather(1, k).start()
+    for mat in mats:
+        ag(2, 0, mat).start()
     ag_plane_next(1)
+    lax.fori_loop(0, count, first_norm, 0)
+    for k in range(1, 4):
+        small_gather(1, k).wait_recv()
+    small_gather(2, 0).start()
+    small_gather(2, 0).wait_recv()
+
+    tin[...] = jnp.zeros_like(tin)
+    tout[...] = jnp.zeros_like(tout)
+    for d in range(devices):
+        far, k = place_of(d)
+        message = small_all[far, k].astype(WIDE)
+        lines[d * lines_in : d * lines_in + first_lines, :] = message[0:first_lines, :]
+        shifted = jnp.concatenate([message[0:24, 64:128], message[0:24, 0:64]], axis=1)
+        lines[d * lines_in + first_lines : (d + 1) * lines_in, :] = shifted[0 : lines_in - first_lines, :]
+        vecs[:, d * own_vec : (d + 1) * own_vec] = message[24:32, 64 : 64 + own_vec]
+        c_in[d] = message[31:32, 0:shard]
+        tout[d * lines_out : (d + 1) * lines_out, 0:128] = message[32 : 32 + lines_out, :]
+        tout[d * lines_out : (d + 1) * lines_out, 128:patches] = message[48 : 48 + lines_out, 0 : patches - 128]
+    for turn in range(turns):
+        tin[0:patches, turn * unit : (turn + 1) * unit] = lines[pl.ds(turn, patches, stride=turns), :][:, 0:unit]
+    for rest, into, at in ((c_one[...], tin, patches), (c_two[...], tout, hidden_tok)):
+        for i in range(3):
+            term = rest.astype(LOW).astype(WIDE)
+            into[at + i : at + i + 1, 0 : rest.shape[1]] = term
+            rest = rest - term
+    tin_t[...] = tin[...].T.astype(LOW)
+    tout_t[...] = tout[...].T.astype(LOW)
+    ones = jnp.ones((3, width), WIDE)
 
     gain_one, shift_one = vecs[0:1, :], vecs[1:2, :]
     gain_two, shift_two, c_four = vecs[2:3, :], vecs[3:4, :], vecs[4:5, :]
@@ -241,36 +396,21 @@
             )
             c_in_rel[k, :, place * shard : (place + 1) * shard] = c_in[near]
 
-    grad_vecs[...] = jnp.zeros_like(grad_vecs)
-    grad_tin[...] = jnp.zeros_like(grad_tin)
-    grad_tout[...] = jnp.zeros_like(grad_tout)
-    grad_c_one[...] = jnp.zeros_like(grad_c_one)
-    grad_c_two[...] = jnp.zeros_like(grad_c_two)
-
     def token_forward(b, carry):
-        for copy in load(b):
-            copy.wait()
-        x = im[b]
-        normed, _ = normalize(x)
-        mixed[b] = padded(normed * gain_one + shift_one, pad).astype(LOW)
-        pre_t = dot(tin_t[...], mixed[b], NN) + c_one[...]
-        value, slope = gelu_parts(pre_t)
-        act_t[b] = value.astype(LOW)
+        fed = mid[b] * gain_one + shift_one
+        mixed[b] = padded(jnp.concatenate([fed, ones], axis=0), pad).astype(LOW)
+        value, slope = gelu_parts(dot(tin_t[...], mixed[b], NN))
+        act_t[b] = padded(jnp.concatenate([value, ones], axis=0), act_t.shape[1]).astype(LOW)
         slope_t[b] = slope.astype(LOW)
-        mid[b] = x + dot(tout_t[...], act_t[b], NN)[0:patches] + c_two[...]
+        mid[b] = im[b] + dot(tout_t[...], act_t[b], NN)[0:patches]
         return carry
 
     def channel_inputs(r, carry):
-        parts, tops = [], []
+        parts = []
         for h in range(2):
-            b = 2 * r + h
-            keep = mask[b].astype(WIDE)
-            normed, _ = normalize(mid[b])
+            normed, _ = normalize(mid[2 * r + h])
             parts.append(padded(normed * gain_two + shift_two, lot))
-            tops.append(padded(cot[b] * keep, lot))
         zed[r] = jnp.concatenate(parts, axis=0).astype(LOW)
-        top[r] = jnp.concatenate(tops, axis=0).astype(LOW)
-        grad_vecs[4:5, :] += jnp.sum(top[r].astype(WIDE), axis=0, keepdims=True)
         return carry
 
     lax.fori_loop(0, 2, token_forward, 0)
@@ -413,6 +553,8 @@
         rs_two(k)
         return carry
 
+    for b in range(2):
+        reload(b).start()
     lax.fori_loop(0, planes, channel_chunk, 0)
 
     def store(b):
@@ -420,6 +562,9 @@
             pltpu.make_async_copy(total.at[b], block_out.at[b], out_sem.at[0, b]),
             pltpu.make_async_copy(grad_zed.at[b], image_grad.at[b], out_sem.at[1, b]),
         )
+
+    tin_low = tin[...].astype(LOW)
+    tout_low = tout[0:hidden_tok, :].astype(LOW)
 
     def token_backward(b, carry):
         keep = mask[b].astype(WIDE)
@@ -429,14 +574,18 @@
         down = grad_zed[b]
         grad_vecs[2:3, :] += jnp.sum(down * normed, axis=0, keepdims=True)
         grad_vecs[3:4, :] += jnp.sum(down, axis=0, keepdims=True)
-        grad_mid = cot[b] * keep + norm_back(down, normed, scale, gain_two)
+        reload(b).wait()
+        grad_mid = cot[b % 2] * keep + norm_back(down, normed, scale, gain_two)
+
+        @pl.when(b + 2 < count)
+        def _():
+            reload(b + 2).start()
+
         back = padded(grad_mid, pad).astype(LOW)
-        grad_c_two[...] += jnp.sum(back.astype(WIDE), axis=1, keepdims=True)
         grad_tout[...] += dot(act_t[b], back, NT)
-        back_t = (dot(tout[...], back, NN) * slope_t[b].astype(WIDE)).astype(LOW)
-        grad_c_one[...] += jnp.sum(back_t.astype(WIDE), axis=1, keepdims=True)
-        grad_tin[...] += dot(mixed[b], back_t, NT)
-        grad_mixed = dot(tin[...], back_t, NN)[0:patches]
+        back_t = (dot(tout_low, back, NN) * slope_t[b].astype(WIDE)).astype(LOW)
+        grad_tin[:, 0:hidden_tok] += dot(mixed[b], back_t, NT)
+        grad_mixed = dot(tin_low, back_t, NN)[0:patches]
         normed, scale = normalize(im[b])
         grad_vecs[0:1, :] += jnp.sum(grad_mixed * normed, axis=0, keepdims=True)
         grad_vecs[1:2, :] += jnp.sum(grad_mixed, axis=0, keepdims=True)
@@ -450,8 +599,66 @@
         return carry
 
     lax.fori_loop(0, count, token_backward, 0)
+
+    biases[0] = jnp.zeros_like(biases[0])
+    for i in range(hidden_tok // 128):
+        biases[0, i : i + 1, :] = grad_tin[patches : patches + 1, i * 128 : (i + 1) * 128]
+    biases[0, 3:4, :] = grad_tout[hidden_tok : hidden_tok + 1, 0:128]
+    biases[0, 4:5, 0 : patches - 128] = grad_tout[hidden_tok : hidden_tok + 1, 128:patches]
+    bias_reduce(0, 0).start()
+    for turn in range(turns):
+        lines[pl.ds(turn, patches, stride=turns), :] = grad_tin[0:patches, turn * unit : turn * unit + 128]
+    for d in range(devices):
+        far, k = place_of(d)
+        low = lines[d * lines_in : d * lines_in + first_lines, :]
+        high = lines[d * lines_in + first_lines : (d + 1) * lines_in, :]
+        small_sum[far, k, 0:first_lines, 0:64] = low[:, 0:64]
+        small_sum[far, k, 0 : lines_in - first_lines, 64:128] = high[:, 0:64]
+        small_sum[far, k, 24:29, 64 : 64 + own_vec] = grad_vecs[0:5, d * own_vec : (d + 1) * own_vec]
+        small_sum[far, k, 31:32, 0:shard] = grad_c_in[d]
+        small_sum[far, k, 32 : 32 + lines_out, :] = grad_tout[d * lines_out : (d + 1) * lines_out, 0:128]
+        small_sum[far, k, 48 : 48 + lines_out, 0 : patches - 128] = grad_tout[
+            d * lines_out : (d + 1) * lines_out, 128:patches
+        ]
+    for k in range(1, planes):
+        small_gather(0, k).wait_send()
+    for far in range(1, 4):
+        small_gather(1, far).wait_send()
+    small_gather(2, 0).wait_send()
+    for far in range(4, PLANE):
+        small_all[far] = small_sum[far].astype(LOW)
+    small_reduce(0, 0).start()
     rs_four(planes - 1)
+    bias_reduce(0, 0).wait_recv()
+    biases[1] = biases[0] + biases_in[0, 0]
+    small_reduce(0, 0).wait_recv()
+    for far in range(4):
+        small_sum[far] += small_core[far].astype(WIDE)
+    for far in range(1, 4):
+        small_all[far] = small_sum[far].astype(LOW)
+        small_reduce(1, far).start()
+        bias_reduce(1, far).start()
+    for far in range(1, 4):
+        small_reduce(1, far).wait_recv()
+        bias_reduce(1, far).wait_recv()
+        small_sum[0] += small_plane[far].astype(WIDE)
+    biases[2] = (biases[1] + biases_in[1, 1]) + (biases_in[1, 2] + biases_in[1, 3])
+    for k in range(1, planes):
+        small_all[0, k] = small_sum[0, k].astype(LOW)
+        small_reduce(2, k).start()
+        bias_reduce(2, k).start()
     rs_last()
+    summed = small_sum[0, 0]
+    tree = [biases[2]]
+    for k in range(1, planes):
+        small_reduce(2, k).wait_recv()
+        bias_reduce(2, k).wait_recv()
+        summed = summed + small_z[k].astype(WIDE)
+        tree.append(biases_in[2, k])
+    small_out[...] = summed
+    while len(tree) > 1:
+        tree = [tree[i] + tree[i + 1] for i in range(0, len(tree), 2)]
+    biases_out[...] = tree[0]
 
     for mat in mats:
         for k in range(planes):
@@ -462,9 +669,59 @@
             rs(stage, planes - 1, mat).wait_send()
         for k in range(max(1, planes - 2), planes):
             rs(3, k, mat).wait_send()
+    small_reduce(0, 0).wait_send()
+    bias_reduce(0, 0).wait_send()
+    for far in range(1, 4):
+        small_reduce(1, far).wait_send()
+        bias_reduce(1, far).wait_send()
+    for k in range(1, planes):
+        small_reduce(2, k).wait_send()
+        bias_reduce(2, k).wait_send()
     for b in range(count):
         for copy in store(b):
             copy.wait()
+
+
+def finish_kernel(
+    block_in,
+    image_in,
+    w_in,
+    w_out,
+    small,
+    biases,
+    block_out,
+    image_out,
+    w_in_out,
+    w_out_out,
+    tin,
+    tout,
+    gain_one,
+    shift_one,
+    gain_two,
+    shift_two,
+    c_four,
+    c_in,
+    c_one,
+    c_two,
+):
+    block_out[...] = block_in[...]
+    image_out[...] = image_in[...]
+    w_in_out[...] = w_in[...]
+    w_out_out[...] = w_out[...]
+    lines_in, unit = tin.shape
+    first_lines = (lines_in + 1) // 2
+    lines_out, patches = tout.shape
+    tin[0:first_lines, :] = small[0:first_lines, 0:unit]
+    tin[first_lines:lines_in, :] = small[0 : lines_in - first_lines, 64 : 64 + unit]
+    tout[:, 0:128] = small[32 : 32 + lines_out, :]
+    tout[:, 128:patches] = small[48 : 48 + lines_out, 0 : patches - 128]
+    for i, piece in enumerate((gain_one, shift_one, gain_two, shift_two, c_four)):
+        piece[...] = small[24 + i : 25 + i, 64 : 64 + piece.shape[1]]
+    c_in[...] = small[31:32, 0 : c_in.shape[1]]
+    for i in range(c_one.shape[1] // 128):
+        c_one[:, i * 128 : (i + 1) * 128] = biases[i : i + 1, :]
+    c_two[:, 0:128] = biases[3:4, :]
+    c_two[:, 128:patches] = biases[4:5, 0 : patches - 128]
 
 
 def fast_shards(
@@ -496,16 +753,11 @@
     chunk = 8 * shard
     half = 4 * shard
 
-    small = [w_token_in, w_token_out, gain_one, shift_one, gain_two, shift_two, bias_reduce, bias_expand]
-    sizes = [piece.shape[0] for piece in small]
-    packed = jnp.concatenate([piece.astype(LOW) for piece in small])
-    gathered = lax.all_gather(packed, "dp", axis=0)
-    ends = [sum(sizes[: i + 1]) for i in range(len(sizes))]
-    pieces = [gathered[:, end - size : end].reshape(-1) for end, size in zip(ends, sizes)]
-    tin = jnp.pad(pieces[0].reshape(patches, hidden_tok), ((0, pad - patches), (0, 0)))
-    tout = jnp.pad(pieces[1].reshape(hidden_tok, patches), ((0, 0), (0, pad - patches)))
-    vecs = jnp.concatenate([jnp.stack(pieces[2:7]), jnp.zeros((3, width), LOW)]).astype(WIDE)
-    c_in = pieces[7].reshape(devices, 1, shard).astype(WIDE)
+    unit = math.gcd(w_token_in.shape[0], hidden_tok)
+    lines_in = w_token_in.shape[0] // unit
+    lines_out = w_token_out.shape[0] // patches
+    own_vec = gain_one.shape[0]
+    hidden_pad = hidden_tok + 16
 
     vmem = pl.BlockSpec(memory_space=pltpu.VMEM)
     hbm = pl.BlockSpec(memory_space=pl.ANY)
@@ -517,20 +769,16 @@
             shape(images.shape, WIDE),
             shape(w_expand.shape, WIDE),
             shape(w_reduce.shape, WIDE),
-            shape((pad, hidden_tok), WIDE),
-            shape((hidden_tok, pad), WIDE),
-            shape((hidden_tok, 1), WIDE),
-            shape((pad, 1), WIDE),
-            shape((8, width), WIDE),
-            shape((devices, 1, shard), WIDE),
+            shape((64, 128), WIDE),
+            shape((8, 128), WIDE),
         ),
-        in_specs=[pl.BlockSpec(memory_space=pltpu.SMEM), hbm, hbm] + [vmem] * 10,
-        out_specs=[hbm, hbm] + [vmem] * 8,
+        in_specs=[pl.BlockSpec(memory_space=pltpu.SMEM), hbm, hbm] + [vmem] * 12,
+        out_specs=[hbm, hbm] + [vmem] * 4,
         scratch_shapes=[
             pltpu.VMEM(images.shape, WIDE),
-            pltpu.VMEM(images.shape, WIDE),
+            pltpu.VMEM((2,) + images.shape[1:], WIDE),
             pltpu.VMEM((count, pad, width), LOW),
-            pltpu.VMEM((count, hidden_tok, width), LOW),
+            pltpu.VMEM((count, hidden_pad, width), LOW),
             pltpu.VMEM((count, hidden_tok, width), LOW),
             pltpu.VMEM(images.shape, WIDE),
             pltpu.VMEM(images.shape, WIDE),
@@ -551,13 +799,33 @@
             pltpu.VMEM((2, 2, shard, width), LOW),
             pltpu.VMEM((2, 2, shard, width), LOW),
             pltpu.VMEM((planes, 2, shard, width), LOW),
-            pltpu.SemaphoreType.DMA((2, count)),
+            pltpu.VMEM((pad, hidden_tok), WIDE),
+            pltpu.VMEM((hidden_tok, pad), LOW),
+            pltpu.VMEM((hidden_pad, pad), WIDE),
+            pltpu.VMEM((pad, hidden_pad), LOW),
+            pltpu.VMEM((8, width), WIDE),
+            pltpu.VMEM((devices, 1, shard), WIDE),
+            pltpu.VMEM((devices * lines_in, 128), WIDE),
+            pltpu.VMEM((64, 128), WIDE),
+            pltpu.VMEM((PLANE, planes, 64, 128), LOW),
+            pltpu.VMEM((pad, hidden_tok + 128), WIDE),
+            pltpu.VMEM((hidden_pad, pad), WIDE),
+            pltpu.VMEM((8, width), WIDE),
+            pltpu.VMEM((devices, 1, shard), WIDE),
+            pltpu.VMEM((PLANE, planes, 64, 128), WIDE),
+            pltpu.VMEM((4, planes, 64, 128), LOW),
+            pltpu.VMEM((4, planes, 64, 128), LOW),
+            pltpu.VMEM((planes, 64, 128), LOW),
+            pltpu.VMEM((3, 8, 128), WIDE),
+            pltpu.VMEM((3, max(4, planes), 8, 128), WIDE),
+            pltpu.SemaphoreType.DMA((3, count)),
             pltpu.SemaphoreType.DMA((2, count)),
             pltpu.SemaphoreType.DMA((5, planes, 2)),
             pltpu.SemaphoreType.DMA((5, planes, 2)),
             pltpu.SemaphoreType.DMA((4, planes, 2)),
             pltpu.SemaphoreType.DMA((4, planes, 2)),
-        ],
+        ]
+        + [pltpu.SemaphoreType.DMA((3, max(4, planes)))] * 6,
         compiler_params=pltpu.CompilerParams(
             collective_id=0, has_side_effects=True, vmem_limit_bytes=63 * 2**20
         ),
@@ -567,46 +835,78 @@
         cotangent,
         w_expand,
         w_reduce,
-        tin,
-        tin.T,
-        tout,
-        tout.T,
-        vecs,
-        bias_token_in[:, None],
-        bias_token_out[:, None],
-        c_in,
-    )
-    block_output, image_grad, own_win, own_wout, g_tin, g_tout, g_c1, g_c2, g_vecs, g_cin = outs
-    bias_sums = lax.psum((g_c1[:, 0], g_c2[:patches, 0]), "dp")
-    flat = [
-        g_tin[:patches].reshape(devices, -1),
-        g_tout[:, :patches].reshape(devices, -1),
-        *[g_vecs[i].reshape(devices, -1) for i in range(5)],
-        g_cin.reshape(devices, -1),
-    ]
-    mine = lax.psum_scatter(jnp.concatenate(flat, axis=1), "dp", scatter_dimension=0, tiled=True)[0]
-    own = [mine[end - size : end] for end, size in zip(ends, sizes)]
+        w_token_in.reshape(lines_in, unit),
+        w_token_out.reshape(lines_out, patches),
+        gain_one.reshape(1, -1),
+        shift_one.reshape(1, -1),
+        gain_two.reshape(1, -1),
+        shift_two.reshape(1, -1),
+        bias_reduce.reshape(1, -1),
+        bias_expand.reshape(1, -1),
+        bias_token_in.reshape(1, -1),
+        bias_token_out.reshape(1, -1),
+    )
+    image = pl.BlockSpec((1, patches, width), lambda b: (b, 0, 0))
+    flat = pl.pallas_call(
+        finish_kernel,
+        out_shape=(
+            shape(images.shape, WIDE),
+            shape(images.shape, WIDE),
+            shape(w_expand.shape, WIDE),
+            shape(w_reduce.shape, WIDE),
+            shape((lines_in, unit), WIDE),
+            shape((lines_out, patches), WIDE),
+            *[shape((1, own_vec), WIDE)] * 5,
+            shape((1, shard), WIDE),
+            shape((1, hidden_tok), WIDE),
+            shape((1, patches), WIDE),
+        ),
+        grid=(count,),
+        in_specs=[image] * 2 + [vmem] * 4,
+        out_specs=[image] * 2 + [vmem] * 12,
+    )(*outs)
+    block_output, image_grad, own_win, own_wout, *rest = flat
+    g_tin, g_tout, g_one, b_one, g_two, b_two, c_four, c_in, c_one, c_two = [part.reshape(-1) for part in rest]
     return (
         block_output,
         image_grad,
-        own[0],
-        own[1],
-        bias_sums[0],
-        bias_sums[1],
-        own[2],
-        own[3],
-        own[4],
-        own[5],
+        g_tin,
+        g_tout,
+        c_one,
+        c_two,
+        g_one,
+        b_one,
+        g_two,
+        b_two,
         own_win,
-        own[7],
+        c_in,
         own_wout,
-        own[6],
-    )
-
-
-def fits(devices):
+        c_four,
+    )
+
+
+def fits(devices, images, w_token_in, w_token_out, bias_token_in, gain_one, w_expand):
     planes = devices // PLANE
-    return devices % PLANE == 0 and planes & (planes - 1) == 0 and planes >= 2
+    patches = images.shape[1]
+    hidden_tok = bias_token_in.shape[0]
+    shard = w_expand.shape[0]
+    unit = math.gcd(w_token_in.shape[0], hidden_tok)
+    return (
+        devices % PLANE == 0
+        and planes & (planes - 1) == 0
+        and planes >= 2
+        and images.shape[0] % 2 == 0
+        and shard % 16 == 0
+        and shard <= 128
+        and (4 * shard) % 128 == 0
+        and 128 < patches <= 205
+        and unit <= 64
+        and w_token_in.shape[0] // unit <= 49
+        and w_token_out.shape[0] % patches == 0
+        and w_token_out.shape[0] // patches <= 16
+        and gain_one.shape[0] <= 64
+        and hidden_tok == 384
+    )
 
 
 def choose(
@@ -643,9 +943,7 @@
         w_reduce,
         bias_reduce,
     )
-    shard = w_expand.shape[0]
-    whole = shard % 16 == 0 and (4 * shard) % 128 == 0 and images.shape[0] % 2 == 0
-    if fits(lax.axis_size("dp")) and whole:
+    if fits(lax.axis_size("dp"), images, w_token_in, w_token_out, bias_token_in, gain_one, w_expand):
         return fast_shards(*args)
     return shards(*args)
 

time: 415 us -> 141 us (0.34)
  waiting for transfers between devices: 214 us -> 0 us
  blocking collectives: 43.8 us -> 0 us
  Pallas kernels: 108 us -> 132 us
  local copies, waits for them, and re-layouts: 28 us -> 6.87 us
  between operations: 14.3 us -> 0.66 us
  other arithmetic: 6.78 us -> 1.28 us
    unnamed x4 -> x0, waiting for transfers between devices: 214 us -> none
    psum x1 -> x0, blocking collectives: 43.8 us -> none  [fast_shards(): bias_sums = lax.psum((g_c1[:, 0], g_c2[:patches, 0]), 'dp')]
    pallas_call x1, Pallas kernels: 108 us -> 124 us  [fast_shards(): pl.pallas_call(block_kernel, out_shape=(shape(images.shape, WIDE), shape(...]
    unnamed x20 -> x0, local copies, waits for them, and re-layouts: 8.95 us -> none
    pallas_call x0 -> x1, Pallas kernels: none -> 7.79 us  [fast_shards(): pl.pallas_call(finish_kernel, out_shape=(shape(images.shape, WIDE), shape...]
    slice x8 -> x0, local copies, waits for them, and re-layouts: 6.75 us -> none  [the longest x3 4.42 us: fast_shards(): own = [mine[end - size:end] for end, size in zip(ends, sizes)]]
    convert_element_type x10 -> x0, other arithmetic: 6.64 us -> none  [the longest x8 5.36 us: fast_shards(): packed = jnp.concatenate([piece.astype(LOW) for piece in small])]
    reshape x2 -> x5, local copies, waits for them, and re-layouts: 1.44 us -> 6.87 us  [the longest x2 2.83 us: fast_shards(): part.reshape(-1)]
  transfers between devices with their start and end apart: 2 -> 0, of which waited for: 2 -> 0; matrix products, arithmetic and copies ran while one was open for 1% -> 0% of each run, Pallas kernels for 0% -> 0%
where the time goes in v2:
time: 141 us; the launch traced here: 140 us
  Pallas kernels  132 us (94%)
  local copies, waits for them, and re-layouts  6.87 us (5%)
    pallas_call x1, Pallas kernels, fast_shards(): pl.pallas_call(block_kernel, out_shape=(shape(images.shape, WIDE), shape(...  124 us
    pallas_call x1, Pallas kernels, fast_shards(): pl.pallas_call(finish_kernel, out_shape=(shape(images.shape, WIDE), shape...  7.79 us
    reshape x2, local copies, waits for them, and re-layouts, fast_shards(): part.reshape(-1)  2.83 us

profile of v2, /device:TPU:0, one launch (start us, length us, event | category | flops | bytes accessed | tf_op | source)
XLA Modules:
  0.0 140.4 jit_solution(10274219916392538728)
XLA Ops:
  0.6 1.2 reshape.96.c_one
  1.9 1.4 reshape.89.tout_own
  3.3 1.4 reshape.88.tin_own
  4.7 123.8 %shard_map.254 = (f32[6,196,768]{2,1,0:T(8,128)}, f32[6,196,768]{2,1,0:T(8,128)}, f32[96,768]{1,0:T(8,128)}, f32[96,768]{1,0:T(8,128)}, f32[64,128]{1,0:T(8,128)}, /*index=5*/f32[8,128]{1,0:T(8,128)}) custom-call(s32[6]{0:T(128)} %mask.1, f32[6,196,768]{2,1,0:T(8,128)} %images.1, f32[6,196,768]{2,1,0:T(8,128)} %cotangent.1, f32[96,768]{1,0:T(8,128)} %w_in.1, ...), custom_call_target="tpu_custom_call" | custom-call | tf_op jit(solution)/shard_map/pallas_call | solution.py:765
  128.5 7.8 %shard_map.255 = (f32[6,196,768]{2,1,0:T(8,128)}, f32[6,196,768]{2,1,0:T(8,128)}, f32[96,768]{1,0:T(8,128)}, f32[96,768]{1,0:T(8,128)}, f32[49,48]{1,0:T(8,128)}...) custom-call(f32[6,196,768]{2,1,0:T(8,128)} %get-tuple-element.34.blo, ...), custom_call_target="tpu_custom_call" | custom-call | tf_op jit(solution)/shard_map/pallas_call | solution.py:850
  136.3 1.3 reduce
  137.6 1.4 %reshape.98 = f32[2352]{0:T(1024)} reshape(f32[49,48]{1,0:T(8,128)} %get-tuple-element.42) | data formatting | bytes 18816 | tf_op jit(solution)/shard_map/reshape | solution.py:869
  139.0 1.4 %reshape.99 = f32[2352]{0:T(1024)} reshape(f32[12,196]{1,0:T(8,128)} %get-tuple-element.43) | data formatting | bytes 18816 | tf_op jit(solution)/shard_map/reshape | solution.py:869

commit v3 on v2

--- a/solution.py
+++ b/solution.py
@@ -73,20 +73,17 @@
     c_in_own,
     c_one,
     c_two,
-    block_out,
-    image_grad,
+    total,
+    grad_zed,
     grad_in,
     grad_out,
     small_out,
     biases_out,
-    im,
     cot,
     mixed,
     act_t,
     slope_t,
     mid,
-    total,
-    grad_zed,
     zed,
     top,
     weights,
@@ -122,8 +119,9 @@
     small_z,
     biases,
     biases_in,
+    late,
+    late_in,
     in_sem,
-    out_sem,
     ag_send,
     ag_recv,
     rs_send,
@@ -134,8 +132,10 @@
     ss_recv,
     bs_send,
     bs_recv,
+    ls_send,
+    ls_recv,
 ):
-    count, patches, width = im.shape
+    count, patches, width = images.shape
     planes = weights.shape[1]
     shard = w_in.shape[0]
     half = 4 * shard
@@ -187,20 +187,23 @@
             device_id_type=MESH,
         )
 
-    def rs(stage, k, mat):
-        slot = k % 2
+    def plane_at(i):
+        return (i + 1) % planes
+
+    def rs(stage, i, mat):
+        slot, k = i % 2, plane_at(i)
         near, far = (by_x, by_y) if mat == 0 else (by_y, by_x)
         src, dst, to = [
             lambda: (send_one.at[mat], recv_one.at[slot, mat], by_core),
             lambda: (send_two.at[mat], recv_two.at[slot, mat], near),
             lambda: (send_three.at[mat], recv_three.at[slot, mat], far),
-            lambda: (send_four.at[slot, mat], recv_four.at[k, mat], by_z(k)),
+            lambda: (send_four.at[slot, mat], recv_four.at[i, mat], by_z(k)),
         ][stage]()
         return pltpu.make_async_remote_copy(
             src_ref=src,
             dst_ref=dst,
-            send_sem=rs_send.at[stage, k, mat],
-            recv_sem=rs_recv.at[stage, k, mat],
+            send_sem=rs_send.at[stage, i, mat],
+            recv_sem=rs_recv.at[stage, i, mat],
             device_id=(to,),
             device_id_type=MESH,
         )
@@ -246,12 +249,23 @@
             device_id_type=MESH,
         )
 
-    unit = tin_own.shape[1]
-    lines_in = tin_own.shape[0]
+    def late_reduce(stage, k):
+        to = [lambda: by_core, lambda: (me, by_x, by_y, by_both)[k], lambda: by_z(k)][stage]()
+        return pltpu.make_async_remote_copy(
+            src_ref=late.at[stage],
+            dst_ref=late_in.at[stage, k],
+            send_sem=ls_send.at[stage, k],
+            recv_sem=ls_recv.at[stage, k],
+            device_id=(to,),
+            device_id_type=MESH,
+        )
+
+    hidden_tok = c_one.shape[0]
+    unit = math.gcd(tin_own.shape[0], hidden_tok)
+    lines_in = tin_own.shape[0] // unit
     first_lines = (lines_in + 1) // 2
-    lines_out = tout_own.shape[0]
-    own_vec = gain_one_own.shape[1]
-    hidden_tok = c_one.shape[1]
+    lines_out = tout_own.shape[0] // patches
+    own_vec = gain_one_own.shape[0]
     turns = hidden_tok // unit
     devices = planes * PLANE
 
@@ -265,25 +279,32 @@
         return far, k
 
     def load(b):
-        return (
-            pltpu.make_async_copy(images.at[b], im.at[b], in_sem.at[0, b]),
-            pltpu.make_async_copy(cotangent.at[b], total.at[b], in_sem.at[1, b]),
-        )
+        return pltpu.make_async_copy(images.at[b], grad_zed.at[b], in_sem.at[0, b])
+
+    def load_top(b):
+        return pltpu.make_async_copy(cotangent.at[b], total.at[b], in_sem.at[1, b])
+
+    def reload_image(b):
+        return pltpu.make_async_copy(images.at[b], mid.at[b], in_sem.at[3, b])
 
     def reload(b):
         return pltpu.make_async_copy(cotangent.at[b], cot.at[b % 2], in_sem.at[2, b])
 
     for b in range(count):
-        for copy in load(b):
-            copy.start()
+        load_top(b).start()
+    for b in range(count):
+        load(b).start()
     small_own[...] = jnp.zeros_like(small_own)
-    small_own[0:first_lines, 0:unit] = tin_own[0:first_lines, :]
-    small_own[0 : lines_in - first_lines, 64 : 64 + unit] = tin_own[first_lines:lines_in, :]
+    for i in range(lines_in):
+        at, lane = (i, 0) if i < first_lines else (i - first_lines, 64)
+        small_own[at : at + 1, lane : lane + unit] = tin_own[i * unit : (i + 1) * unit].reshape(1, unit)
     for i, piece in enumerate((gain_one_own, shift_one_own, gain_two_own, shift_two_own, c_four_own)):
-        small_own[24 + i : 25 + i, 64 : 64 + own_vec] = piece[...]
-    small_own[31:32, 0:shard] = c_in_own[...]
-    small_own[32 : 32 + lines_out, :] = tout_own[:, 0:128]
-    small_own[48 : 48 + lines_out, 0 : patches - 128] = tout_own[:, 128:patches]
+        small_own[24 + i : 25 + i, 64 : 64 + own_vec] = piece[...].reshape(1, own_vec)
+    small_own[31:32, 0:shard] = c_in_own[...].reshape(1, shard)
+    for i in range(lines_out):
+        line = tout_own[i * patches : (i + 1) * patches].reshape(1, patches)
+        small_own[32 + i : 33 + i, :] = line[:, 0:128]
+        small_own[48 + i : 49 + i, 0 : patches - 128] = line[:, 128:patches]
     small_all[0, 0] = small_own[...].astype(LOW)
     weights[0, 0, 0:shard] = w_in[...].astype(LOW)
     weights[1, 0, 0:shard] = w_out[...].astype(LOW)
@@ -296,7 +317,18 @@
 
     mats = (0, 1)
 
+    def ag_planes(distance):
+        for k in range(1, planes):
+            away = plane_of(k) - z
+
+            @pl.when((away == distance) | (away == -distance))
+            def _():
+                for mat in mats:
+                    ag(0, k, mat).start()
+
     def ag_direct(k):
+        for mat in mats:
+            ag(0, k, mat).wait_recv()
         for mat in mats:
             ag(1, k, mat).start()
         for mat in mats:
@@ -313,15 +345,6 @@
             ag(3, k, mat).wait_recv()
             ag(4, k, mat).start()
 
-    def ag_plane(k):
-        for mat in mats:
-            ag(0, k, mat).wait_recv()
-        ag_direct(k)
-
-    def ag_plane_next(k):
-        for mat in mats:
-            ag(0, k, mat).start()
-
     def ag_ready(k):
         for mat in mats:
             ag(4, k, mat).wait_recv()
@@ -330,6 +353,7 @@
         small_gather(0, k).start()
     for mat in mats:
         ag(1, 0, mat).start()
+    ag_planes(1)
 
     grad_vecs[...] = jnp.zeros_like(grad_vecs)
     grad_tin[...] = jnp.zeros_like(grad_tin)
@@ -339,15 +363,15 @@
         tops = []
         for h in range(2):
             b = 2 * r + h
-            load(b)[1].wait()
+            load_top(b).wait()
             tops.append(padded(total[b] * mask[b].astype(WIDE), lot))
         top[r] = jnp.concatenate(tops, axis=0).astype(LOW)
-        grad_vecs[4:5, :] += jnp.sum(top[r].astype(WIDE), axis=0, keepdims=True)
+        grad_vecs[2:3, :] += jnp.sum(top[r].astype(WIDE), axis=0, keepdims=True)
         return carry
 
     def first_norm(b, carry):
-        load(b)[0].wait()
-        mid[b] = normalize(im[b])[0]
+        load(b).wait()
+        mid[b] = normalize(grad_zed[b])[0]
         return carry
 
     lax.fori_loop(0, blocks, channel_top, 0)
@@ -357,11 +381,15 @@
         small_gather(1, k).start()
     for mat in mats:
         ag(2, 0, mat).start()
-    ag_plane_next(1)
+    ag_planes(2)
     lax.fori_loop(0, count, first_norm, 0)
+    ag_forward(0)
+    for distance in range(3, planes):
+        ag_planes(distance)
     for k in range(1, 4):
         small_gather(1, k).wait_recv()
     small_gather(2, 0).start()
+    ag_direct(plane_at(0))
     small_gather(2, 0).wait_recv()
 
     tin[...] = jnp.zeros_like(tin)
@@ -378,7 +406,8 @@
         tout[d * lines_out : (d + 1) * lines_out, 128:patches] = message[48 : 48 + lines_out, 0 : patches - 128]
     for turn in range(turns):
         tin[0:patches, turn * unit : (turn + 1) * unit] = lines[pl.ds(turn, patches, stride=turns), :][:, 0:unit]
-    for rest, into, at in ((c_one[...], tin, patches), (c_two[...], tout, hidden_tok)):
+    for rest, into, at in ((c_one, tin, patches), (c_two, tout, hidden_tok)):
+        rest = rest[...].reshape(1, rest.shape[0])
         for i in range(3):
             term = rest.astype(LOW).astype(WIDE)
             into[at + i : at + i + 1, 0 : rest.shape[1]] = term
@@ -402,7 +431,7 @@
         value, slope = gelu_parts(dot(tin_t[...], mixed[b], NN))
         act_t[b] = padded(jnp.concatenate([value, ones], axis=0), act_t.shape[1]).astype(LOW)
         slope_t[b] = slope.astype(LOW)
-        mid[b] = im[b] + dot(tout_t[...], act_t[b], NN)[0:patches]
+        mid[b] = grad_zed[b] + dot(tout_t[...], act_t[b], NN)[0:patches]
         return carry
 
     def channel_inputs(r, carry):
@@ -413,80 +442,75 @@
         zed[r] = jnp.concatenate(parts, axis=0).astype(LOW)
         return carry
 
-    lax.fori_loop(0, 2, token_forward, 0)
-    ag_forward(0)
-    lax.fori_loop(2, 4, token_forward, 0)
-    ag_plane(1)
-    ag_plane_next(2)
-    lax.fori_loop(4, count, token_forward, 0)
+    first, second = count // 3, 2 * count // 3
+    lax.fori_loop(0, first, token_forward, 0)
     ag_core(0)
-    ag_forward(1)
+    lax.fori_loop(first, second, token_forward, 0)
+    ag_forward(plane_at(0))
+    lax.fori_loop(second, count, token_forward, 0)
+    if planes > 2:
+        ag_direct(plane_at(1))
     lax.fori_loop(0, blocks, channel_inputs, 0)
+    ag_core(plane_at(0))
     total[...] = jnp.zeros_like(total)
     grad_zed[...] = jnp.zeros_like(grad_zed)
 
-    def rs_two(k):
+    def rs_two(i):
         for mat in mats:
-            rs(0, k, mat).wait_recv()
-            own_sum[mat] += recv_one[k % 2, mat].astype(WIDE)
-            if mat == 0:
-                first, second = (1, 2), (3, 4)
-            else:
-                first, second = (2, 3), (3, 4)
-
-            @pl.when(k > 0)
+            rs(0, i, mat).wait_recv()
+            own_sum[mat] += recv_one[i % 2, mat].astype(WIDE)
+            first, second = (1, 3) if mat == 0 else (2, 3)
+
+            @pl.when(i > 0)
             def _():
-                rs(1, k - 1, mat).wait_send()
-
-            send_two[mat, 0:shard] = own_sum[mat, first[0] * shard : first[1] * shard].astype(LOW)
-            send_two[mat, shard : 2 * shard] = own_sum[mat, second[0] * shard : second[1] * shard].astype(LOW)
-            rs(1, k, mat).start()
-
-    def rs_three(k):
+                rs(1, i - 1, mat).wait_send()
+
+            send_two[mat, 0:shard] = own_sum[mat, first * shard : (first + 1) * shard].astype(LOW)
+            send_two[mat, shard : 2 * shard] = own_sum[mat, second * shard : (second + 1) * shard].astype(LOW)
+            rs(1, i, mat).start()
+
+    def rs_three(i):
         for mat in mats:
-            rs(1, k, mat).wait_recv()
+            rs(1, i, mat).wait_recv()
             other = 2 if mat == 0 else 1
 
-            @pl.when(k > 0)
+            @pl.when(i > 0)
             def _():
-                rs(2, k - 1, mat).wait_send()
-
-            keep_sum[mat] = own_sum[mat, 0:shard] + recv_two[k % 2, mat, 0:shard].astype(WIDE)
+                rs(2, i - 1, mat).wait_send()
+
+            keep_sum[mat] = own_sum[mat, 0:shard] + recv_two[i % 2, mat, 0:shard].astype(WIDE)
             send_three[mat] = (
                 own_sum[mat, other * shard : (other + 1) * shard]
-                + recv_two[k % 2, mat, shard : 2 * shard].astype(WIDE)
+                + recv_two[i % 2, mat, shard : 2 * shard].astype(WIDE)
             ).astype(LOW)
-            rs(2, k, mat).start()
-
-    def rs_four(k):
+            rs(2, i, mat).start()
+
+    def rs_four(i):
         for mat in mats:
-            rs(2, k, mat).wait_recv()
-            summed = keep_sum[mat] + recv_three[k % 2, mat].astype(WIDE)
-            result = grad_in if mat == 0 else grad_out
-
-            @pl.when(k == 0)
+            rs(2, i, mat).wait_recv()
+
+            @pl.when(i > 1)
             def _():
-                result[...] = summed
-
-            @pl.when(k > 0)
-            def _():
-                @pl.when(k > 2)
-                def _():
-                    rs(3, k - 2, mat).wait_send()
-
-                send_four[k % 2, mat] = summed.astype(LOW)
-                rs(3, k, mat).start()
+                rs(3, i - 2, mat).wait_send()
+
+            send_four[i % 2, mat] = (keep_sum[mat] + recv_three[i % 2, mat].astype(WIDE)).astype(LOW)
+            rs(3, i, mat).start()
 
     def rs_last():
+        last = planes - 1
         for mat in mats:
             result = grad_in if mat == 0 else grad_out
-            for k in range(1, planes):
-                rs(3, k, mat).wait_recv()
-                result[...] += recv_four[k, mat].astype(WIDE)
+            rs(2, last, mat).wait_recv()
+            summed = keep_sum[mat] + recv_three[last % 2, mat].astype(WIDE)
+            for i in range(last):
+                rs(3, i, mat).wait_recv()
+                summed = summed + recv_four[i, mat].astype(WIDE)
+            result[...] = summed
 
     tile = chunk // 3
 
-    def channel_chunk(k, carry):
+    def channel_chunk(i, carry):
+        k = plane_at(i)
         ag_ready(k)
 
         def rows(r, inner):
@@ -503,29 +527,25 @@
                 total[2 * r + h] += up[h * lot : h * lot + patches]
                 grad_zed[2 * r + h] += down[h * lot : h * lot + patches]
 
-            @pl.when((r == 0) & (k + 1 < planes) & (k > 0))
+            @pl.when((r == 0) & (i + 2 < planes))
             def _():
-                ag_forward(k + 1)
-
-            @pl.when((r == 2) & (k > 0))
+                ag_forward(i + 2)
+
+            @pl.when((r == 1) & (i + 3 < planes))
             def _():
-                rs_three(k - 1)
+                ag_direct(i + 3)
+
+            @pl.when((r == 1) & (i > 1))
+            def _():
+                rs_four(i - 2)
 
             return inner
 
         lax.fori_loop(0, blocks, rows, 0)
 
-        @pl.when(k + 1 < planes)
+        @pl.when(i + 2 < planes)
         def _():
-            ag_core(k + 1)
-
-        @pl.when(k + 2 < planes)
-        def _():
-            ag_plane(k + 2)
-
-        @pl.when(k + 3 < planes)
-        def _():
-            ag_plane_next(k + 3)
+            ag_core(i + 2)
 
         back_sum = jnp.sum(grad_pre[...].astype(WIDE), axis=0, keepdims=True)
         for place in range(PLANE):
@@ -537,43 +557,36 @@
         flat_top = top[...].reshape(blocks * pair, width)
         flat_zed = zed[...].reshape(blocks * pair, width)
         for mat, left, right in ((1, act, flat_top), (0, grad_pre, flat_zed)):
-            @pl.when(k > 0)
+            @pl.when(i > 0)
             def _():
-                rs(0, k - 1, mat).wait_send()
+                rs(0, i - 1, mat).wait_send()
 
             send_one[mat] = dot(left[:, half:chunk], right, TN).astype(LOW)
-            rs(0, k, mat).start()
-
-        @pl.when(k > 0)
+            rs(0, i, mat).start()
+
+        @pl.when(i > 0)
         def _():
-            rs_four(k - 1)
+            rs_three(i - 1)
 
         for mat, left, right in ((1, act, flat_top), (0, grad_pre, flat_zed)):
             own_sum[mat] = dot(left[:, 0:half], right, TN)
-        rs_two(k)
+        rs_two(i)
         return carry
 
     for b in range(2):
         reload(b).start()
     lax.fori_loop(0, planes, channel_chunk, 0)
 
-    def store(b):
-        return (
-            pltpu.make_async_copy(total.at[b], block_out.at[b], out_sem.at[0, b]),
-            pltpu.make_async_copy(grad_zed.at[b], image_grad.at[b], out_sem.at[1, b]),
-        )
-
     tin_low = tin[...].astype(LOW)
     tout_low = tout[0:hidden_tok, :].astype(LOW)
 
     def token_backward(b, carry):
         keep = mask[b].astype(WIDE)
         total[b] = (mid[b] + total[b] + c_four) * keep
-        store(b)[0].start()
         normed, scale = normalize(mid[b])
         down = grad_zed[b]
-        grad_vecs[2:3, :] += jnp.sum(down * normed, axis=0, keepdims=True)
-        grad_vecs[3:4, :] += jnp.sum(down, axis=0, keepdims=True)
+        grad_vecs[0:1, :] += jnp.sum(down * normed, axis=0, keepdims=True)
+        grad_vecs[1:2, :] += jnp.sum(down, axis=0, keepdims=True)
         reload(b).wait()
         grad_mid = cot[b % 2] * keep + norm_back(down, normed, scale, gain_two)
 
@@ -583,21 +596,37 @@
 
         back = padded(grad_mid, pad).astype(LOW)
         grad_tout[...] += dot(act_t[b], back, NT)
-        back_t = (dot(tout_low, back, NN) * slope_t[b].astype(WIDE)).astype(LOW)
-        grad_tin[:, 0:hidden_tok] += dot(mixed[b], back_t, NT)
-        grad_mixed = dot(tin_low, back_t, NN)[0:patches]
-        normed, scale = normalize(im[b])
-        grad_vecs[0:1, :] += jnp.sum(grad_mixed * normed, axis=0, keepdims=True)
-        grad_vecs[1:2, :] += jnp.sum(grad_mixed, axis=0, keepdims=True)
-        grad_zed[b] = grad_mid + norm_back(grad_mixed, normed, scale, gain_one)
-        store(b)[1].start()
-
-        @pl.when(b == count // 2)
+        grad_zed[b] = grad_mid
+        slope_t[b] = (dot(tout_low, back, NN) * slope_t[b].astype(WIDE)).astype(LOW)
+        grad_tin[:, 0:hidden_tok] += dot(mixed[b], slope_t[b], NT)
+
+        reload_image(b).start()
+
+        @pl.when((b == 0) & (planes > 1))
         def _():
-            rs_three(planes - 1)
+            rs_four(planes - 2)
 
         return carry
 
+    def image_backward(b, carry):
+        grad_mixed = dot(tin_low, slope_t[b], NN)[0:patches]
+        reload_image(b).wait()
+        normed, scale = normalize(mid[b])
+        late[0, 0:1, :] += jnp.sum(grad_mixed * normed, axis=0, keepdims=True)
+        late[0, 1:2, :] += jnp.sum(grad_mixed, axis=0, keepdims=True)
+        grad_zed[b] += norm_back(grad_mixed, normed, scale, gain_one)
+
+        @pl.when(b == 1)
+        def _():
+            small_second()
+
+        @pl.when(b == count - 2)
+        def _():
+            small_third()
+
+        return carry
+
+    late[0] = jnp.zeros_like(late[0])
     lax.fori_loop(0, count, token_backward, 0)
 
     biases[0] = jnp.zeros_like(biases[0])
@@ -614,7 +643,7 @@
         high = lines[d * lines_in + first_lines : (d + 1) * lines_in, :]
         small_sum[far, k, 0:first_lines, 0:64] = low[:, 0:64]
         small_sum[far, k, 0 : lines_in - first_lines, 64:128] = high[:, 0:64]
-        small_sum[far, k, 24:29, 64 : 64 + own_vec] = grad_vecs[0:5, d * own_vec : (d + 1) * own_vec]
+        small_sum[far, k, 24:27, 64 : 64 + own_vec] = grad_vecs[0:3, d * own_vec : (d + 1) * own_vec]
         small_sum[far, k, 31:32, 0:shard] = grad_c_in[d]
         small_sum[far, k, 32 : 32 + lines_out, :] = grad_tout[d * lines_out : (d + 1) * lines_out, 0:128]
         small_sum[far, k, 48 : 48 + lines_out, 0 : patches - 128] = grad_tout[
@@ -628,26 +657,37 @@
     for far in range(4, PLANE):
         small_all[far] = small_sum[far].astype(LOW)
     small_reduce(0, 0).start()
-    rs_four(planes - 1)
-    bias_reduce(0, 0).wait_recv()
-    biases[1] = biases[0] + biases_in[0, 0]
-    small_reduce(0, 0).wait_recv()
-    for far in range(4):
-        small_sum[far] += small_core[far].astype(WIDE)
+    rs_three(planes - 1)
+
+    def small_second():
+        bias_reduce(0, 0).wait_recv()
+        biases[1] = biases[0] + biases_in[0, 0]
+        small_reduce(0, 0).wait_recv()
+        for far in range(4):
+            small_sum[far] += small_core[far].astype(WIDE)
+        for far in range(1, 4):
+            small_all[far] = small_sum[far].astype(LOW)
+            small_reduce(1, far).start()
+            bias_reduce(1, far).start()
+
+    def small_third():
+        for far in range(1, 4):
+            small_reduce(1, far).wait_recv()
+            bias_reduce(1, far).wait_recv()
+            small_sum[0] += small_plane[far].astype(WIDE)
+        biases[2] = (biases[1] + biases_in[1, 1]) + (biases_in[1, 2] + biases_in[1, 3])
+        for k in range(1, planes):
+            small_all[0, k] = small_sum[0, k].astype(LOW)
+            small_reduce(2, k).start()
+            bias_reduce(2, k).start()
+
+    lax.fori_loop(0, count, image_backward, 0)
+    late_reduce(0, 0).start()
+    rs_last()
+    late_reduce(0, 0).wait_recv()
+    late[1] = late[0] + late_in[0, 0]
     for far in range(1, 4):
-        small_all[far] = small_sum[far].astype(LOW)
-        small_reduce(1, far).start()
-        bias_reduce(1, far).start()
-    for far in range(1, 4):
-        small_reduce(1, far).wait_recv()
-        bias_reduce(1, far).wait_recv()
-        small_sum[0] += small_plane[far].astype(WIDE)
-    biases[2] = (biases[1] + biases_in[1, 1]) + (biases_in[1, 2] + biases_in[1, 3])
-    for k in range(1, planes):
-        small_all[0, k] = small_sum[0, k].astype(LOW)
-        small_reduce(2, k).start()
-        bias_reduce(2, k).start()
-    rs_last()
+        late_reduce(1, far).start()
     summed = small_sum[0, 0]
     tree = [biases[2]]
     for k in range(1, planes):
@@ -656,6 +696,18 @@
         summed = summed + small_z[k].astype(WIDE)
         tree.append(biases_in[2, k])
     small_out[...] = summed
+    late_sum = late[1]
+    for far in range(1, 4):
+        late_reduce(1, far).wait_recv()
+        late_sum = late_sum + late_in[1, far]
+    late[2] = late_sum
+    for k in range(1, planes):
+        late_reduce(2, k).start()
+    for k in range(1, planes):
+        late_reduce(2, k).wait_recv()
+        late_sum = late_sum + late_in[2, k]
+    late_sum = pltpu.roll(padded(late_sum, 8), width - own_vec * me, 1)
+    small_out[27:29, 64 : 64 + own_vec] = late_sum[0:2, 0:own_vec]
     while len(tree) > 1:
         tree = [tree[i] + tree[i + 1] for i in range(0, len(tree), 2)]
     biases_out[...] = tree[0]
@@ -667,8 +719,13 @@
                     ag(stage, k, mat).wait_send()
         for stage in range(3):
             rs(stage, planes - 1, mat).wait_send()
-        for k in range(max(1, planes - 2), planes):
-            rs(3, k, mat).wait_send()
+        for i in range(max(0, planes - 3), planes - 1):
+            rs(3, i, mat).wait_send()
+    late_reduce(0, 0).wait_send()
+    for far in range(1, 4):
+        late_reduce(1, far).wait_send()
+    for k in range(1, planes):
+        late_reduce(2, k).wait_send()
     small_reduce(0, 0).wait_send()
     bias_reduce(0, 0).wait_send()
     for far in range(1, 4):
@@ -677,9 +734,6 @@
     for k in range(1, planes):
         small_reduce(2, k).wait_send()
         bias_reduce(2, k).wait_send()
-    for b in range(count):
-        for copy in store(b):
-            copy.wait()
 
 
 def finish_kernel(
@@ -703,25 +757,39 @@
     c_in,
     c_one,
     c_two,
+    sem,
 ):
-    block_out[...] = block_in[...]
-    image_out[...] = image_in[...]
-    w_in_out[...] = w_in[...]
-    w_out_out[...] = w_out[...]
-    lines_in, unit = tin.shape
+    copies = [
+        pltpu.make_async_copy(block_in, block_out, sem.at[0]),
+        pltpu.make_async_copy(image_in, image_out, sem.at[1]),
+        pltpu.make_async_copy(w_in, w_in_out, sem.at[2]),
+        pltpu.make_async_copy(w_out, w_out_out, sem.at[3]),
+    ]
+    for copy in copies:
+        copy.start()
+    hidden_tok, patches = c_one.shape[0], c_two.shape[0]
+    unit = math.gcd(tin.shape[0], hidden_tok)
+    lines_in = tin.shape[0] // unit
     first_lines = (lines_in + 1) // 2
-    lines_out, patches = tout.shape
-    tin[0:first_lines, :] = small[0:first_lines, 0:unit]
-    tin[first_lines:lines_in, :] = small[0 : lines_in - first_lines, 64 : 64 + unit]
-    tout[:, 0:128] = small[32 : 32 + lines_out, :]
-    tout[:, 128:patches] = small[48 : 48 + lines_out, 0 : patches - 128]
-    for i, piece in enumerate((gain_one, shift_one, gain_two, shift_two, c_four)):
-        piece[...] = small[24 + i : 25 + i, 64 : 64 + piece.shape[1]]
-    c_in[...] = small[31:32, 0 : c_in.shape[1]]
-    for i in range(c_one.shape[1] // 128):
-        c_one[:, i * 128 : (i + 1) * 128] = biases[i : i + 1, :]
-    c_two[:, 0:128] = biases[3:4, :]
-    c_two[:, 128:patches] = biases[4:5, 0 : patches - 128]
+    for i in range(lines_in):
+        at, lane = (i, 0) if i < first_lines else (i - first_lines, 64)
+        tin[i * unit : (i + 1) * unit] = small[at : at + 1, lane : lane + unit].reshape(unit)
+    for i in range(tout.shape[0] // patches):
+        tout[i * patches : i * patches + 128] = small[32 + i : 33 + i, :].reshape(128)
+        tout[i * patches + 128 : (i + 1) * patches] = small[48 + i : 49 + i, 0 : patches - 128].reshape(
+            patches - 128
+        )
+    for i, piece in enumerate((gain_two, shift_two, c_four, gain_one, shift_one)):
+        own_vec = piece.shape[0]
+        piece[...] = small[24 + i : 25 + i, 64 : 64 + own_vec].reshape(own_vec)
+    shard = c_in.shape[0]
+    c_in[...] = small[31:32, 0:shard].reshape(shard)
+    for i in range(hidden_tok // 128):
+        c_one[i * 128 : (i + 1) * 128] = biases[i : i + 1, :].reshape(128)
+    c_two[0:128] = biases[3:4, :].reshape(128)
+    c_two[128:patches] = biases[4:5, 0 : patches - 128].reshape(patches - 128)
+    for copy in copies:
+        copy.wait()
 
 
 def fast_shards(
@@ -755,8 +823,6 @@
 
     unit = math.gcd(w_token_in.shape[0], hidden_tok)
     lines_in = w_token_in.shape[0] // unit
-    lines_out = w_token_out.shape[0] // patches
-    own_vec = gain_one.shape[0]
     hidden_pad = hidden_tok + 16
 
     vmem = pl.BlockSpec(memory_space=pltpu.VMEM)
@@ -765,23 +831,20 @@
     outs = pl.pallas_call(
         block_kernel,
         out_shape=(
-            shape(images.shape, WIDE),
-            shape(images.shape, WIDE),
-            shape(w_expand.shape, WIDE),
-            shape(w_reduce.shape, WIDE),
-            shape((64, 128), WIDE),
-            shape((8, 128), WIDE),
+            pltpu.VMEM(images.shape, WIDE),
+            pltpu.VMEM(images.shape, WIDE),
+            pltpu.VMEM(w_expand.shape, WIDE),
+            pltpu.VMEM(w_reduce.shape, WIDE),
+            pltpu.VMEM((64, 128), WIDE),
+            pltpu.VMEM((8, 128), WIDE),
         ),
         in_specs=[pl.BlockSpec(memory_space=pltpu.SMEM), hbm, hbm] + [vmem] * 12,
-        out_specs=[hbm, hbm] + [vmem] * 4,
+        out_specs=[vmem] * 6,
         scratch_shapes=[
-            pltpu.VMEM(images.shape, WIDE),
             pltpu.VMEM((2,) + images.shape[1:], WIDE),
             pltpu.VMEM((count, pad, width), LOW),
             pltpu.VMEM((count, hidden_pad, width), LOW),
             pltpu.VMEM((count, hidden_tok, width), LOW),
-            pltpu.VMEM(images.shape, WIDE),
-            pltpu.VMEM(images.shape, WIDE),
             pltpu.VMEM(images.shape, WIDE),
             pltpu.VMEM((blocks, pair, width), LOW),
             pltpu.VMEM((blocks, pair, width), LOW),
@@ -798,7 +861,7 @@
             pltpu.VMEM((2, shard, width), LOW),
             pltpu.VMEM((2, 2, shard, width), LOW),
             pltpu.VMEM((2, 2, shard, width), LOW),
-            pltpu.VMEM((planes, 2, shard, width), LOW),
+            pltpu.VMEM((planes - 1, 2, shard, width), LOW),
             pltpu.VMEM((pad, hidden_tok), WIDE),
             pltpu.VMEM((hidden_tok, pad), LOW),
             pltpu.VMEM((hidden_pad, pad), WIDE),
@@ -818,16 +881,17 @@
             pltpu.VMEM((planes, 64, 128), LOW),
             pltpu.VMEM((3, 8, 128), WIDE),
             pltpu.VMEM((3, max(4, planes), 8, 128), WIDE),
-            pltpu.SemaphoreType.DMA((3, count)),
-            pltpu.SemaphoreType.DMA((2, count)),
+            pltpu.VMEM((3, 2, width), WIDE),
+            pltpu.VMEM((3, max(4, planes), 2, width), WIDE),
+            pltpu.SemaphoreType.DMA((4, count)),
             pltpu.SemaphoreType.DMA((5, planes, 2)),
             pltpu.SemaphoreType.DMA((5, planes, 2)),
             pltpu.SemaphoreType.DMA((4, planes, 2)),
             pltpu.SemaphoreType.DMA((4, planes, 2)),
         ]
-        + [pltpu.SemaphoreType.DMA((3, max(4, planes)))] * 6,
+        + [pltpu.SemaphoreType.DMA((3, max(4, planes)))] * 8,
         compiler_params=pltpu.CompilerParams(
-            collective_id=0, has_side_effects=True, vmem_limit_bytes=63 * 2**20
+            collective_id=0, has_side_effects=True, vmem_limit_bytes=55 * 2**20
         ),
     )(
         mask,
@@ -835,18 +899,17 @@
         cotangent,
         w_expand,
         w_reduce,
-        w_token_in.reshape(lines_in, unit),
-        w_token_out.reshape(lines_out, patches),
-        gain_one.reshape(1, -1),
-        shift_one.reshape(1, -1),
-        gain_two.reshape(1, -1),
-        shift_two.reshape(1, -1),
-        bias_reduce.reshape(1, -1),
-        bias_expand.reshape(1, -1),
-        bias_token_in.reshape(1, -1),
-        bias_token_out.reshape(1, -1),
-    )
-    image = pl.BlockSpec((1, patches, width), lambda b: (b, 0, 0))
+        w_token_in,
+        w_token_out,
+        gain_one,
+        shift_one,
+        gain_two,
+        shift_two,
+        bias_reduce,
+        bias_expand,
+        bias_token_in,
+        bias_token_out,
+    )
     flat = pl.pallas_call(
         finish_kernel,
         out_shape=(
@@ -854,19 +917,20 @@
             shape(images.shape, WIDE),
             shape(w_expand.shape, WIDE),
             shape(w_reduce.shape, WIDE),
-            shape((lines_in, unit), WIDE),
-            shape((lines_out, patches), WIDE),
-            *[shape((1, own_vec), WIDE)] * 5,
-            shape((1, shard), WIDE),
-            shape((1, hidden_tok), WIDE),
-            shape((1, patches), WIDE),
+            shape(w_token_in.shape, WIDE),
+            shape(w_token_out.shape, WIDE),
+            *[shape(gain_one.shape, WIDE)] * 5,
+            shape(bias_expand.shape, WIDE),
+            shape(bias_token_in.shape, WIDE),
+            shape(bias_token_out.shape, WIDE),
         ),
-        grid=(count,),
-        in_specs=[image] * 2 + [vmem] * 4,
-        out_specs=[image] * 2 + [vmem] * 12,
+        in_specs=[vmem] * 6,
+        out_specs=[hbm] * 4 + [vmem] * 10,
+        scratch_shapes=[pltpu.SemaphoreType.DMA((4,))],
+        compiler_params=pltpu.CompilerParams(vmem_limit_bytes=16 * 2**20),
     )(*outs)
     block_output, image_grad, own_win, own_wout, *rest = flat
-    g_tin, g_tout, g_one, b_one, g_two, b_two, c_four, c_in, c_one, c_two = [part.reshape(-1) for part in rest]
+    g_tin, g_tout, g_one, b_one, g_two, b_two, c_four, c_in, c_one, c_two = rest
     return (
         block_output,
         image_grad,

time: 141 us -> 126 us (0.89)
  Pallas kernels: 132 us -> 125 us
  local copies, waits for them, and re-layouts: 6.87 us -> 0 us
    reshape x5 -> x0, local copies, waits for them, and re-layouts: 6.87 us -> none  [the longest x2 2.83 us: fast_shards(): part.reshape(-1)]
    pallas_call x1, Pallas kernels: 7.79 us -> 3.96 us  [fast_shards(): pl.pallas_call(finish_kernel, out_shape=(shape(images.shape, WIDE), shape...]
    pallas_call x1, Pallas kernels: 124 us -> 121 us  [fast_shards(): pl.pallas_call(block_kernel, out_shape=(pltpu.VMEM(images.shape, WIDE), p...]
where the time goes in v3:
time: 126 us
  Pallas kernels  125 us (99%)
    pallas_call x1, Pallas kernels, fast_shards(): pl.pallas_call(block_kernel, out_shape=(pltpu.VMEM(images.shape, WIDE), p...  121 us
    pallas_call x1, Pallas kernels, fast_shards(): pl.pallas_call(finish_kernel, out_shape=(shape(images.shape, WIDE), shape...  3.96 us

profile of v3, /device:TPU:0, one launch (start us, length us, event | category | flops | bytes accessed | tf_op | source)
XLA Modules:
  0.0 125.8 jit_solution(12977448889888889687)
XLA Ops:
  0.7 121.2 %shard_map.254 = (f32[6,196,768]{2,1,0:T(8,128)S(1)}, f32[6,196,768]{2,1,0:T(8,128)S(1)}, f32[96,768]{1,0:T(8,128)S(1)}, f32[96,768]{1,0:T(8,128)S(1)}, f32[64,128]{1,0:T(8,128)S(1)}, /*index=5*/f32[8,128]{1,0:T(8,128)S(1)}) custom-call(s32[6]{0:T(128)} %mask.1, f32[6,196,768]{2,1,0:T(8,128)} %images.1, f32[6,196,768]{2,1,0:T(8,128)} %cotangent.1, ...), custom_call_target="tpu_custom_call" | custom-call | tf_op jit(solution)/shard_map/pallas_call | solution.py:831
  121.9 4.0 %shard_map.255 = (f32[6,196,768]{2,1,0:T(8,128)}, f32[6,196,768]{2,1,0:T(8,128)}, f32[96,768]{1,0:T(8,128)}, f32[96,768]{1,0:T(8,128)}, f32[2352]{0:T(1024)}, /*...) custom-call(f32[6,196,768]{2,1,0:T(8,128)S(1)} %get-tuple-element.34, ...), custom_call_target="tpu_custom_call" | custom-call | tf_op jit(solution)/shard_map/pallas_call | solution.py:913

commit v4 on v3

--- a/solution.py
+++ b/solution.py
@@ -121,6 +121,7 @@
     biases_in,
     late,
     late_in,
+    scales,
     in_sem,
     ag_send,
     ag_recv,
@@ -175,7 +176,8 @@
                 1: (0, step * shard, shard, near),
                 2: (0, (3 - step) * shard, shard, far),
                 3: (step * shard, 3 * shard, shard, far),
-                4: (0, half, half, by_core),
+                4: (0, half, 3 * shard, by_core),
+                5: (3 * shard, half + 3 * shard, shard, by_core),
             }[stage]
             source = weights.at[mat, k, pl.ds(src, size)]
         return pltpu.make_async_remote_copy(
@@ -208,26 +210,26 @@
             device_id_type=MESH,
         )
 
-    def small_gather(stage, k):
+    def small_gather(stage, k, group):
         src, dst, to = [
-            lambda: (small_all.at[0, 0], small_all.at[0, k], by_z(k)),
-            lambda: (small_all.at[0], small_all.at[k], (me, by_x, by_y, by_both)[k]),
-            lambda: (small_all.at[pl.ds(0, 4)], small_all.at[pl.ds(4, 4)], by_core),
+            lambda: (small_all.at[group, 0, 0], small_all.at[group, 0, k], by_z(k)),
+            lambda: (small_all.at[group, 0], small_all.at[group, k], (me, by_x, by_y, by_both)[k]),
+            lambda: (small_all.at[group, pl.ds(0, 4)], small_all.at[group, pl.ds(4, 4)], by_core),
         ][stage]()
         return pltpu.make_async_remote_copy(
             src_ref=src,
             dst_ref=dst,
-            send_sem=sg_send.at[stage, k],
-            recv_sem=sg_recv.at[stage, k],
+            send_sem=sg_send.at[stage, k, group],
+            recv_sem=sg_recv.at[stage, k, group],
             device_id=(to,),
             device_id_type=MESH,
         )
 
     def small_reduce(stage, k):
         src, dst, to = [
-            lambda: (small_all.at[pl.ds(4, 4)], small_core, by_core),
-            lambda: (small_all.at[k], small_plane.at[k], (me, by_x, by_y, by_both)[k]),
-            lambda: (small_all.at[0, k], small_z.at[k], by_z(k)),
+            lambda: (small_all.at[:, pl.ds(4, 4)], small_core, by_core),
+            lambda: (small_all.at[:, k], small_plane.at[:, k], (me, by_x, by_y, by_both)[k]),
+            lambda: (small_all.at[:, 0, k], small_z.at[k], by_z(k)),
         ][stage]()
         return pltpu.make_async_remote_copy(
             src_ref=src,
@@ -305,7 +307,8 @@
         line = tout_own[i * patches : (i + 1) * patches].reshape(1, patches)
         small_own[32 + i : 33 + i, :] = line[:, 0:128]
         small_own[48 + i : 49 + i, 0 : patches - 128] = line[:, 128:patches]
-    small_all[0, 0] = small_own[...].astype(LOW)
+    for group in range(2):
+        small_all[group, 0, 0] = small_own[32 * group : 32 * (group + 1)].astype(LOW)
     weights[0, 0, 0:shard] = w_in[...].astype(LOW)
     weights[1, 0, 0:shard] = w_out[...].astype(LOW)
 
@@ -316,19 +319,60 @@
     pl.semaphore_wait(barrier, len(peers))
 
     mats = (0, 1)
-
-    def ag_planes(distance):
-        for k in range(1, planes):
-            away = plane_of(k) - z
-
-            @pl.when((away == distance) | (away == -distance))
+    row_of_four = planes == 4
+    inner = (z == 1) | (z == 2)
+
+    def ag_pass(which, mat):
+        src, dst, to = ((1, 2, by_z(3)), (3, 2, by_z(1)), (2, 3, by_z(1)))[which]
+        return pltpu.make_async_remote_copy(
+            src_ref=weights.at[mat, src, pl.ds(0, shard)],
+            dst_ref=weights.at[mat, dst, pl.ds(0, shard)],
+            send_sem=ag_send.at[6, which, mat],
+            recv_sem=ag_recv.at[0, dst, mat],
+            device_id=(to,),
+            device_id_type=MESH,
+        )
+
+    def ag_planes():
+        for mat in mats:
+            ag(0, 1, mat).start()
+        if row_of_four:
+
+            @pl.when(inner)
             def _():
                 for mat in mats:
-                    ag(0, k, mat).start()
+                    ag(0, 3, mat).start()
+
+    def ag_planes_pass():
+        if row_of_four:
+
+            @pl.when(inner)
+            def _():
+                for which, came in ((0, 1), (1, 3)):
+                    for mat in mats:
+                        ag(0, came, mat).wait_recv()
+                        ag_pass(which, mat).start()
+
+    def ag_planes_last():
+        if row_of_four:
+
+            @pl.when(inner)
+            def _():
+                for mat in mats:
+                    ag(0, 2, mat).wait_recv()
+                    ag_pass(2, mat).start()
 
     def ag_direct(k):
-        for mat in mats:
-            ag(0, k, mat).wait_recv()
+        if row_of_four:
+
+            @pl.when(jnp.logical_not(inner))
+            def _():
+                for mat in mats:
+                    ag(0, k, mat).wait_recv()
+
+        else:
+            for mat in mats:
+                ag(0, k, mat).wait_recv()
         for mat in mats:
             ag(1, k, mat).start()
         for mat in mats:
@@ -342,18 +386,24 @@
     def ag_core(k):
         for mat in mats:
             ag(2, k, mat).wait_recv()
+            ag(4, k, mat).start()
+
+    def ag_core_last(k):
+        for mat in mats:
             ag(3, k, mat).wait_recv()
-            ag(4, k, mat).start()
+            ag(5, k, mat).start()
 
     def ag_ready(k):
         for mat in mats:
             ag(4, k, mat).wait_recv()
-
-    for k in range(1, planes):
-        small_gather(0, k).start()
+            ag(5, k, mat).wait_recv()
+
+    for group in range(2):
+        for k in range(1, planes):
+            small_gather(0, k, group).start()
     for mat in mats:
         ag(1, 0, mat).start()
-    ag_planes(1)
+    ag_planes()
 
     grad_vecs[...] = jnp.zeros_like(grad_vecs)
     grad_tin[...] = jnp.zeros_like(grad_tin)
@@ -375,35 +425,52 @@
         return carry
 
     lax.fori_loop(0, blocks, channel_top, 0)
-    for k in range(1, planes):
-        small_gather(0, k).wait_recv()
-    for k in range(1, 4):
-        small_gather(1, k).start()
+    for group in range(2):
+        for k in range(1, planes):
+            small_gather(0, k, group).wait_recv()
+        for k in range(1, 4):
+            small_gather(1, k, group).start()
     for mat in mats:
         ag(2, 0, mat).start()
-    ag_planes(2)
     lax.fori_loop(0, count, first_norm, 0)
-    ag_forward(0)
-    for distance in range(3, planes):
-        ag_planes(distance)
     for k in range(1, 4):
-        small_gather(1, k).wait_recv()
-    small_gather(2, 0).start()
+        small_gather(1, k, 0).wait_recv()
+    small_gather(2, 0, 0).start()
+    ag_planes_pass()
     ag_direct(plane_at(0))
-    small_gather(2, 0).wait_recv()
 
     tin[...] = jnp.zeros_like(tin)
     tout[...] = jnp.zeros_like(tout)
-    for d in range(devices):
+
+    def unpack(d, group):
         far, k = place_of(d)
-        message = small_all[far, k].astype(WIDE)
-        lines[d * lines_in : d * lines_in + first_lines, :] = message[0:first_lines, :]
-        shifted = jnp.concatenate([message[0:24, 64:128], message[0:24, 0:64]], axis=1)
-        lines[d * lines_in + first_lines : (d + 1) * lines_in, :] = shifted[0 : lines_in - first_lines, :]
-        vecs[:, d * own_vec : (d + 1) * own_vec] = message[24:32, 64 : 64 + own_vec]
-        c_in[d] = message[31:32, 0:shard]
-        tout[d * lines_out : (d + 1) * lines_out, 0:128] = message[32 : 32 + lines_out, :]
-        tout[d * lines_out : (d + 1) * lines_out, 128:patches] = message[48 : 48 + lines_out, 0 : patches - 128]
+        message = small_all[group, far, k].astype(WIDE)
+        if group == 0:
+            lines[d * lines_in : d * lines_in + first_lines, :] = message[0:first_lines, :]
+            shifted = jnp.concatenate([message[0:24, 64:128], message[0:24, 0:64]], axis=1)
+            lines[d * lines_in + first_lines : (d + 1) * lines_in, :] = shifted[0 : lines_in - first_lines, :]
+            vecs[:, d * own_vec : (d + 1) * own_vec] = message[24:32, 64 : 64 + own_vec]
+            c_in[d] = message[31:32, 0:shard]
+        else:
+            tout[d * lines_out : (d + 1) * lines_out, 0:128] = message[0:lines_out, :]
+            tout[d * lines_out : (d + 1) * lines_out, 128:patches] = message[16 : 16 + lines_out, 0 : patches - 128]
+
+    def unpack_half(own, group):
+        for parity in range(2):
+
+            @pl.when((core == parity) == own)
+            def _():
+                for d in range(parity, devices, 2):
+                    unpack(d, group)
+
+    unpack_half(True, 0)
+    for k in range(1, 4):
+        small_gather(1, k, 1).wait_recv()
+    small_gather(2, 0, 1).start()
+    unpack_half(True, 1)
+    for group in range(2):
+        small_gather(2, 0, group).wait_recv()
+        unpack_half(False, group)
     for turn in range(turns):
         tin[0:patches, turn * unit : (turn + 1) * unit] = lines[pl.ds(turn, patches, stride=turns), :][:, 0:unit]
     for rest, into, at in ((c_one, tin, patches), (c_two, tout, hidden_tok)):
@@ -438,36 +505,37 @@
         parts = []
         for h in range(2):
             normed, _ = normalize(mid[2 * r + h])
+            total[2 * r + h] = mid[2 * r + h] + c_four
+            grad_zed[2 * r + h] = jnp.zeros((patches, width), WIDE)
             parts.append(padded(normed * gain_two + shift_two, lot))
         zed[r] = jnp.concatenate(parts, axis=0).astype(LOW)
         return carry
 
-    first, second = count // 3, 2 * count // 3
-    lax.fori_loop(0, first, token_forward, 0)
-    ag_core(0)
-    lax.fori_loop(first, second, token_forward, 0)
+    lax.fori_loop(0, count // 2, token_forward, 0)
     ag_forward(plane_at(0))
-    lax.fori_loop(second, count, token_forward, 0)
+    if planes > 1:
+        ag_forward(0)
+    lax.fori_loop(count // 2, count - 1, token_forward, 0)
+    ag_planes_last()
+    ag_core(plane_at(0))
+    lax.fori_loop(count - 1, count, token_forward, 0)
     if planes > 2:
         ag_direct(plane_at(1))
     lax.fori_loop(0, blocks, channel_inputs, 0)
-    ag_core(plane_at(0))
-    total[...] = jnp.zeros_like(total)
-    grad_zed[...] = jnp.zeros_like(grad_zed)
-
-    def rs_two(i):
-        for mat in mats:
-            rs(0, i, mat).wait_recv()
-            own_sum[mat] += recv_one[i % 2, mat].astype(WIDE)
-            first, second = (1, 3) if mat == 0 else (2, 3)
-
-            @pl.when(i > 0)
-            def _():
-                rs(1, i - 1, mat).wait_send()
-
-            send_two[mat, 0:shard] = own_sum[mat, first * shard : (first + 1) * shard].astype(LOW)
-            send_two[mat, shard : 2 * shard] = own_sum[mat, second * shard : (second + 1) * shard].astype(LOW)
-            rs(1, i, mat).start()
+    ag_core_last(plane_at(0))
+
+    def rs_two(i, mat):
+        rs(0, i, mat).wait_recv()
+        own_sum[mat] += recv_one[i % 2, mat].astype(WIDE)
+        first, second = (1, 3) if mat == 0 else (2, 3)
+
+        @pl.when(i > 0)
+        def _():
+            rs(1, i - 1, mat).wait_send()
+
+        send_two[mat, 0:shard] = own_sum[mat, first * shard : (first + 1) * shard].astype(LOW)
+        send_two[mat, shard : 2 * shard] = own_sum[mat, second * shard : (second + 1) * shard].astype(LOW)
+        rs(1, i, mat).start()
 
     def rs_three(i):
         for mat in mats:
@@ -527,13 +595,22 @@
                 total[2 * r + h] += up[h * lot : h * lot + patches]
                 grad_zed[2 * r + h] += down[h * lot : h * lot + patches]
 
-            @pl.when((r == 0) & (i + 2 < planes))
+            @pl.when((r == 0) & (i == 0) & (planes > 2))
             def _():
-                ag_forward(i + 2)
-
-            @pl.when((r == 1) & (i + 3 < planes))
+                ag_forward(2)
+
+            @pl.when((r == 0) & (i + 3 < planes))
             def _():
                 ag_direct(i + 3)
+
+            @pl.when((r == 1) & (i + 2 < planes))
+            def _():
+                ag_core(i + 2)
+
+            @pl.when((r == 1) & (i == 0))
+            def _():
+                ag_core(0)
+                ag_core_last(0)
 
             @pl.when((r == 1) & (i > 1))
             def _():
@@ -545,7 +622,8 @@
 
         @pl.when(i + 2 < planes)
         def _():
-            ag_core(i + 2)
+            ag_core_last(i + 2)
+
 
         back_sum = jnp.sum(grad_pre[...].astype(WIDE), axis=0, keepdims=True)
         for place in range(PLANE):
@@ -556,21 +634,28 @@
 
         flat_top = top[...].reshape(blocks * pair, width)
         flat_zed = zed[...].reshape(blocks * pair, width)
-        for mat, left, right in ((1, act, flat_top), (0, grad_pre, flat_zed)):
-            @pl.when(i > 0)
-            def _():
+        @pl.when(i > 0)
+        def _():
+            for mat in mats:
                 rs(0, i - 1, mat).wait_send()
 
-            send_one[mat] = dot(left[:, half:chunk], right, TN).astype(LOW)
+        send_one[1] = dot(act[:, half:chunk], flat_top, TN).astype(LOW)
+        send_one[0] = dot(grad_pre[:, half:chunk], flat_zed, TN).astype(LOW)
+        for mat in mats:
             rs(0, i, mat).start()
 
         @pl.when(i > 0)
         def _():
             rs_three(i - 1)
 
-        for mat, left, right in ((1, act, flat_top), (0, grad_pre, flat_zed)):
-            own_sum[mat] = dot(left[:, 0:half], right, TN)
-        rs_two(i)
+        @pl.when(i + 3 < planes)
+        def _():
+            ag_forward(i + 3)
+
+        own_sum[1] = dot(act[:, 0:half], flat_top, TN)
+        own_sum[0] = dot(grad_pre[:, 0:half], flat_zed, TN)
+        for mat in mats:
+            rs_two(i, mat)
         return carry
 
     for b in range(2):
@@ -582,7 +667,6 @@
 
     def token_backward(b, carry):
         keep = mask[b].astype(WIDE)
-        total[b] = (mid[b] + total[b] + c_four) * keep
         normed, scale = normalize(mid[b])
         down = grad_zed[b]
         grad_vecs[0:1, :] += jnp.sum(down * normed, axis=0, keepdims=True)
@@ -608,22 +692,25 @@
 
         return carry
 
-    def image_backward(b, carry):
-        grad_mixed = dot(tin_low, slope_t[b], NN)[0:patches]
+    def image_norm(b, carry):
         reload_image(b).wait()
         normed, scale = normalize(mid[b])
+        mid[b] = normed
+        scales[b] = scale
+        grad_mixed = dot(tin_low, slope_t[b], NN)[0:patches]
+        weights[b // planes, b % planes, 0:pad] = padded(grad_mixed, pad).astype(LOW)
         late[0, 0:1, :] += jnp.sum(grad_mixed * normed, axis=0, keepdims=True)
         late[0, 1:2, :] += jnp.sum(grad_mixed, axis=0, keepdims=True)
-        grad_zed[b] += norm_back(grad_mixed, normed, scale, gain_one)
 
         @pl.when(b == 1)
         def _():
             small_second()
 
-        @pl.when(b == count - 2)
-        def _():
-            small_third()
-
+        return carry
+
+    def image_backward(b, carry):
+        total[b] *= mask[b].astype(WIDE)
+        grad_zed[b] += norm_back(weights[b // planes, b % planes, 0:pad][0:patches].astype(WIDE), mid[b], scales[b], gain_one)
         return carry
 
     late[0] = jnp.zeros_like(late[0])
@@ -639,34 +726,35 @@
         lines[pl.ds(turn, patches, stride=turns), :] = grad_tin[0:patches, turn * unit : turn * unit + 128]
     for d in range(devices):
         far, k = place_of(d)
+        first, second = small_sum.at[0, far, k], small_sum.at[1, far, k]
         low = lines[d * lines_in : d * lines_in + first_lines, :]
         high = lines[d * lines_in + first_lines : (d + 1) * lines_in, :]
-        small_sum[far, k, 0:first_lines, 0:64] = low[:, 0:64]
-        small_sum[far, k, 0 : lines_in - first_lines, 64:128] = high[:, 0:64]
-        small_sum[far, k, 24:27, 64 : 64 + own_vec] = grad_vecs[0:3, d * own_vec : (d + 1) * own_vec]
-        small_sum[far, k, 31:32, 0:shard] = grad_c_in[d]
-        small_sum[far, k, 32 : 32 + lines_out, :] = grad_tout[d * lines_out : (d + 1) * lines_out, 0:128]
-        small_sum[far, k, 48 : 48 + lines_out, 0 : patches - 128] = grad_tout[
-            d * lines_out : (d + 1) * lines_out, 128:patches
-        ]
-    for k in range(1, planes):
-        small_gather(0, k).wait_send()
-    for far in range(1, 4):
-        small_gather(1, far).wait_send()
-    small_gather(2, 0).wait_send()
-    for far in range(4, PLANE):
-        small_all[far] = small_sum[far].astype(LOW)
+        first[0:first_lines, 0:64] = low[:, 0:64]
+        first[0 : lines_in - first_lines, 64:128] = high[:, 0:64]
+        first[24:27, 64 : 64 + own_vec] = grad_vecs[0:3, d * own_vec : (d + 1) * own_vec]
+        first[31:32, 0:shard] = grad_c_in[d]
+        second[0:lines_out, :] = grad_tout[d * lines_out : (d + 1) * lines_out, 0:128]
+        second[16 : 16 + lines_out, 0 : patches - 128] = grad_tout[d * lines_out : (d + 1) * lines_out, 128:patches]
+    for group in range(2):
+        for k in range(1, planes):
+            small_gather(0, k, group).wait_send()
+        for far in range(1, 4):
+            small_gather(1, far, group).wait_send()
+        small_gather(2, 0, group).wait_send()
+        for far in range(4, PLANE):
+            small_all[group, far] = small_sum[group, far].astype(LOW)
     small_reduce(0, 0).start()
-    rs_three(planes - 1)
 
     def small_second():
         bias_reduce(0, 0).wait_recv()
         biases[1] = biases[0] + biases_in[0, 0]
         small_reduce(0, 0).wait_recv()
         for far in range(4):
-            small_sum[far] += small_core[far].astype(WIDE)
+            for group in range(2):
+                small_sum[group, far] += small_core[group, far].astype(WIDE)
         for far in range(1, 4):
-            small_all[far] = small_sum[far].astype(LOW)
+            for group in range(2):
+                small_all[group, far] = small_sum[group, far].astype(LOW)
             small_reduce(1, far).start()
             bias_reduce(1, far).start()
 
@@ -674,28 +762,38 @@
         for far in range(1, 4):
             small_reduce(1, far).wait_recv()
             bias_reduce(1, far).wait_recv()
-            small_sum[0] += small_plane[far].astype(WIDE)
+            for group in range(2):
+                small_sum[group, 0] += small_plane[group, far].astype(WIDE)
         biases[2] = (biases[1] + biases_in[1, 1]) + (biases_in[1, 2] + biases_in[1, 3])
         for k in range(1, planes):
-            small_all[0, k] = small_sum[0, k].astype(LOW)
+            for group in range(2):
+                small_all[group, 0, k] = small_sum[group, 0, k].astype(LOW)
             small_reduce(2, k).start()
             bias_reduce(2, k).start()
 
-    lax.fori_loop(0, count, image_backward, 0)
+    for mat in mats:
+        for k in range(planes):
+            for stage in range(1, 6):
+                ag(stage, k, mat).wait_send()
+        ag(0, 1, mat).wait_send()
+        if row_of_four:
+
+            @pl.when(inner)
+            def _():
+                ag(0, 3, mat).wait_send()
+                for which in range(3):
+                    ag_pass(which, mat).wait_send()
+
+    lax.fori_loop(0, count, image_norm, 0)
     late_reduce(0, 0).start()
-    rs_last()
+    lax.fori_loop(0, 1, image_backward, 0)
     late_reduce(0, 0).wait_recv()
     late[1] = late[0] + late_in[0, 0]
     for far in range(1, 4):
         late_reduce(1, far).start()
-    summed = small_sum[0, 0]
-    tree = [biases[2]]
-    for k in range(1, planes):
-        small_reduce(2, k).wait_recv()
-        bias_reduce(2, k).wait_recv()
-        summed = summed + small_z[k].astype(WIDE)
-        tree.append(biases_in[2, k])
-    small_out[...] = summed
+    rs_three(planes - 1)
+    small_third()
+    lax.fori_loop(1, count // 2, image_backward, 0)
     late_sum = late[1]
     for far in range(1, 4):
         late_reduce(1, far).wait_recv()
@@ -703,6 +801,17 @@
     late[2] = late_sum
     for k in range(1, planes):
         late_reduce(2, k).start()
+    lax.fori_loop(count // 2, count, image_backward, 0)
+    rs_last()
+    summed = [small_sum[group, 0, 0] for group in range(2)]
+    tree = [biases[2]]
+    for k in range(1, planes):
+        small_reduce(2, k).wait_recv()
+        bias_reduce(2, k).wait_recv()
+        summed = [summed[group] + small_z[k, group].astype(WIDE) for group in range(2)]
+        tree.append(biases_in[2, k])
+    for group in range(2):
+        small_out[32 * group : 32 * (group + 1)] = summed[group]
     for k in range(1, planes):
         late_reduce(2, k).wait_recv()
         late_sum = late_sum + late_in[2, k]
@@ -713,10 +822,6 @@
     biases_out[...] = tree[0]
 
     for mat in mats:
-        for k in range(planes):
-            for stage in range(5):
-                if stage > 0 or k > 0:
-                    ag(stage, k, mat).wait_send()
         for stage in range(3):
             rs(stage, planes - 1, mat).wait_send()
         for i in range(max(0, planes - 3), planes - 1):
@@ -870,26 +975,28 @@
             pltpu.VMEM((devices, 1, shard), WIDE),
             pltpu.VMEM((devices * lines_in, 128), WIDE),
             pltpu.VMEM((64, 128), WIDE),
-            pltpu.VMEM((PLANE, planes, 64, 128), LOW),
+            pltpu.VMEM((2, PLANE, planes, 32, 128), LOW),
             pltpu.VMEM((pad, hidden_tok + 128), WIDE),
             pltpu.VMEM((hidden_pad, pad), WIDE),
             pltpu.VMEM((8, width), WIDE),
             pltpu.VMEM((devices, 1, shard), WIDE),
-            pltpu.VMEM((PLANE, planes, 64, 128), WIDE),
-            pltpu.VMEM((4, planes, 64, 128), LOW),
-            pltpu.VMEM((4, planes, 64, 128), LOW),
-            pltpu.VMEM((planes, 64, 128), LOW),
+            pltpu.VMEM((2, PLANE, planes, 32, 128), WIDE),
+            pltpu.VMEM((2, 4, planes, 32, 128), LOW),
+            pltpu.VMEM((2, 4, planes, 32, 128), LOW),
+            pltpu.VMEM((planes, 2, 32, 128), LOW),
             pltpu.VMEM((3, 8, 128), WIDE),
             pltpu.VMEM((3, max(4, planes), 8, 128), WIDE),
             pltpu.VMEM((3, 2, width), WIDE),
             pltpu.VMEM((3, max(4, planes), 2, width), WIDE),
+            pltpu.VMEM((count, patches, 1), WIDE),
             pltpu.SemaphoreType.DMA((4, count)),
-            pltpu.SemaphoreType.DMA((5, planes, 2)),
-            pltpu.SemaphoreType.DMA((5, planes, 2)),
+            pltpu.SemaphoreType.DMA((7, planes, 2)),
+            pltpu.SemaphoreType.DMA((7, planes, 2)),
             pltpu.SemaphoreType.DMA((4, planes, 2)),
             pltpu.SemaphoreType.DMA((4, planes, 2)),
         ]
-        + [pltpu.SemaphoreType.DMA((3, max(4, planes)))] * 8,
+        + [pltpu.SemaphoreType.DMA((3, max(4, planes), 2))] * 2
+        + [pltpu.SemaphoreType.DMA((3, max(4, planes)))] * 6,
         compiler_params=pltpu.CompilerParams(
             collective_id=0, has_side_effects=True, vmem_limit_bytes=55 * 2**20
         ),
@@ -957,9 +1064,9 @@
     unit = math.gcd(w_token_in.shape[0], hidden_tok)
     return (
         devices % PLANE == 0
-        and planes & (planes - 1) == 0
-        and planes >= 2
+        and planes in (2, 4)
         and images.shape[0] % 2 == 0
+        and images.shape[0] <= 2 * planes
         and shard % 16 == 0
         and shard <= 128
         and (4 * shard) % 128 == 0

time: 126 us -> 112 us (0.89)
  Pallas kernels: 125 us -> 111 us
    pallas_call x1, Pallas kernels: 121 us -> 107 us  [fast_shards(): pl.pallas_call(block_kernel, out_shape=(pltpu.VMEM(images.shape, WIDE), p...]
where the time goes in v4:
time: 112 us; the launch traced here: 111 us
  Pallas kernels  111 us (99%)
    pallas_call x1, Pallas kernels, fast_shards(): pl.pallas_call(block_kernel, out_shape=(pltpu.VMEM(images.shape, WIDE), p...  107 us
    pallas_call x1, Pallas kernels, fast_shards(): pl.pallas_call(finish_kernel, out_shape=(shape(images.shape, WIDE), shape...  3.96 us

profile of v4, /device:TPU:0, one launch (start us, length us, event | category | flops | bytes accessed | tf_op | source)
XLA Modules:
  0.0 111.4 jit_solution(13004776486103523812)
XLA Ops:
  0.7 106.7 %shard_map.254 = (f32[6,196,768]{2,1,0:T(8,128)S(1)}, f32[6,196,768]{2,1,0:T(8,128)S(1)}, f32[96,768]{1,0:T(8,128)S(1)}, f32[96,768]{1,0:T(8,128)S(1)}, f32[64,128]{1,0:T(8,128)S(1)}, /*index=5*/f32[8,128]{1,0:T(8,128)S(1)}) custom-call(s32[6]{0:T(128)} %mask.1, f32[6,196,768]{2,1,0:T(8,128)} %images.1, f32[6,196,768]{2,1,0:T(8,128)} %cotangent.1, ...), custom_call_target="tpu_custom_call" | custom-call | tf_op jit(solution)/shard_map/pallas_call | solution.py:936
  107.4 4.0 %shard_map.255 = (f32[6,196,768]{2,1,0:T(8,128)}, f32[6,196,768]{2,1,0:T(8,128)}, f32[96,768]{1,0:T(8,128)}, f32[96,768]{1,0:T(8,128)}, f32[2352]{0:T(1024)}, /*...) custom-call(f32[6,196,768]{2,1,0:T(8,128)S(1)} %get-tuple-element.34, ...), custom_call_target="tpu_custom_call" | custom-call | tf_op jit(solution)/shard_map/pallas_call | solution.py:1020

commit v5 on v4

--- a/solution.py
+++ b/solution.py
@@ -100,6 +100,8 @@
     recv_three,
     send_four,
     recv_four,
+    send_far,
+    recv_far,
     tin,
     tin_t,
     tout,
@@ -199,7 +201,8 @@
             lambda: (send_one.at[mat], recv_one.at[slot, mat], by_core),
             lambda: (send_two.at[mat], recv_two.at[slot, mat], near),
             lambda: (send_three.at[mat], recv_three.at[slot, mat], far),
-            lambda: (send_four.at[slot, mat], recv_four.at[i, mat], by_z(k)),
+            lambda: (send_four.at[slot, mat], recv_four.at[i - 1, mat], by_z(k)),
+            lambda: (send_far.at[mat], recv_far.at[mat], by_z(k)),
         ][stage]()
         return pltpu.make_async_remote_copy(
             src_ref=src,
@@ -319,7 +322,6 @@
     pl.semaphore_wait(barrier, len(peers))
 
     mats = (0, 1)
-    row_of_four = planes == 4
     inner = (z == 1) | (z == 2)
 
     def ag_pass(which, mat):
@@ -336,47 +338,36 @@
     def ag_planes():
         for mat in mats:
             ag(0, 1, mat).start()
-        if row_of_four:
-
-            @pl.when(inner)
-            def _():
+
+        @pl.when(inner)
+        def _():
+            for mat in mats:
+                ag(0, 3, mat).start()
+
+    def ag_planes_pass():
+        @pl.when(inner)
+        def _():
+            for which, came in ((0, 1), (1, 3)):
                 for mat in mats:
-                    ag(0, 3, mat).start()
-
-    def ag_planes_pass():
-        if row_of_four:
-
-            @pl.when(inner)
-            def _():
-                for which, came in ((0, 1), (1, 3)):
-                    for mat in mats:
-                        ag(0, came, mat).wait_recv()
-                        ag_pass(which, mat).start()
+                    ag(0, came, mat).wait_recv()
+                    ag_pass(which, mat).start()
 
     def ag_planes_last():
-        if row_of_four:
-
-            @pl.when(inner)
-            def _():
-                for mat in mats:
-                    ag(0, 2, mat).wait_recv()
-                    ag_pass(2, mat).start()
+        @pl.when(inner)
+        def _():
+            for mat in mats:
+                ag(0, 2, mat).wait_recv()
+                ag_pass(2, mat).start()
 
     def ag_direct(k):
-        if row_of_four:
-
-            @pl.when(jnp.logical_not(inner))
-            def _():
-                for mat in mats:
-                    ag(0, k, mat).wait_recv()
-
-        else:
+        @pl.when(jnp.logical_not(inner))
+        def _():
             for mat in mats:
                 ag(0, k, mat).wait_recv()
-        for mat in mats:
-            ag(1, k, mat).start()
-        for mat in mats:
-            ag(2, k, mat).start()
+
+        for stage in (1, 2):
+            for mat in mats:
+                ag(stage, k, mat).start()
 
     def ag_forward(k):
         for mat in mats:
@@ -430,14 +421,10 @@
             small_gather(0, k, group).wait_recv()
         for k in range(1, 4):
             small_gather(1, k, group).start()
-    for mat in mats:
-        ag(2, 0, mat).start()
     lax.fori_loop(0, count, first_norm, 0)
     for k in range(1, 4):
         small_gather(1, k, 0).wait_recv()
     small_gather(2, 0, 0).start()
-    ag_planes_pass()
-    ag_direct(plane_at(0))
 
     tin[...] = jnp.zeros_like(tin)
     tout[...] = jnp.zeros_like(tout)
@@ -468,6 +455,8 @@
         small_gather(1, k, 1).wait_recv()
     small_gather(2, 0, 1).start()
     unpack_half(True, 1)
+    ag_planes_pass()
+    ag_direct(plane_at(0))
     for group in range(2):
         small_gather(2, 0, group).wait_recv()
         unpack_half(False, group)
@@ -485,13 +474,6 @@
 
     gain_one, shift_one = vecs[0:1, :], vecs[1:2, :]
     gain_two, shift_two, c_four = vecs[2:3, :], vecs[3:4, :], vecs[4:5, :]
-    for k in range(planes):
-        for place in range(PLANE):
-            near = plane_of(k) * PLANE + (
-                (row + (place // 2) % 2) % 2 * 4 + (col + place % 2) % 2 * 2 + (core + place // 4) % 2
-            )
-            c_in_rel[k, :, place * shard : (place + 1) * shard] = c_in[near]
-
     def token_forward(b, carry):
         fed = mid[b] * gain_one + shift_one
         mixed[b] = padded(jnp.concatenate([fed, ones], axis=0), pad).astype(LOW)
@@ -511,38 +493,54 @@
         zed[r] = jnp.concatenate(parts, axis=0).astype(LOW)
         return carry
 
-    lax.fori_loop(0, count // 2, token_forward, 0)
+    first = 2 * count // 3
+    lax.fori_loop(0, first, token_forward, 0)
     ag_forward(plane_at(0))
-    if planes > 1:
-        ag_forward(0)
-    lax.fori_loop(count // 2, count - 1, token_forward, 0)
+    lax.fori_loop(first, count, token_forward, 0)
+    ag_core(plane_at(0))
     ag_planes_last()
-    ag_core(plane_at(0))
-    lax.fori_loop(count - 1, count, token_forward, 0)
-    if planes > 2:
-        ag_direct(plane_at(1))
     lax.fori_loop(0, blocks, channel_inputs, 0)
+    ag_direct(plane_at(1))
+    for k in range(planes):
+        for place in range(PLANE):
+            near = plane_of(k) * PLANE + (
+                (row + (place // 2) % 2) % 2 * 4 + (col + place % 2) % 2 * 2 + (core + place // 4) % 2
+            )
+            c_in_rel[k, :, place * shard : (place + 1) * shard] = c_in[near]
+
     ag_core_last(plane_at(0))
 
     def rs_two(i, mat):
         rs(0, i, mat).wait_recv()
         own_sum[mat] += recv_one[i % 2, mat].astype(WIDE)
-        first, second = (1, 3) if mat == 0 else (2, 3)
+
+        @pl.when(i == 0)
+        def _():
+            send_far[mat] = own_sum[mat].astype(LOW)
+            rs(4, 0, mat).start()
+
+        @pl.when(i == planes - 1)
+        def _():
+            rs(4, 0, mat).wait_recv()
+            own_sum[mat] += recv_far[mat].astype(WIDE)
+
+        @pl.when(i > 1)
+        def _():
+            rs(1, i - 1, mat).wait_send()
 
         @pl.when(i > 0)
         def _():
-            rs(1, i - 1, mat).wait_send()
-
-        send_two[mat, 0:shard] = own_sum[mat, first * shard : (first + 1) * shard].astype(LOW)
-        send_two[mat, shard : 2 * shard] = own_sum[mat, second * shard : (second + 1) * shard].astype(LOW)
-        rs(1, i, mat).start()
+            first, second = (1, 3) if mat == 0 else (2, 3)
+            send_two[mat, 0:shard] = own_sum[mat, first * shard : (first + 1) * shard].astype(LOW)
+            send_two[mat, shard : 2 * shard] = own_sum[mat, second * shard : (second + 1) * shard].astype(LOW)
+            rs(1, i, mat).start()
 
     def rs_three(i):
         for mat in mats:
             rs(1, i, mat).wait_recv()
             other = 2 if mat == 0 else 1
 
-            @pl.when(i > 0)
+            @pl.when(i > 1)
             def _():
                 rs(2, i - 1, mat).wait_send()
 
@@ -557,10 +555,6 @@
         for mat in mats:
             rs(2, i, mat).wait_recv()
 
-            @pl.when(i > 1)
-            def _():
-                rs(3, i - 2, mat).wait_send()
-
             send_four[i % 2, mat] = (keep_sum[mat] + recv_three[i % 2, mat].astype(WIDE)).astype(LOW)
             rs(3, i, mat).start()
 
@@ -570,9 +564,9 @@
             result = grad_in if mat == 0 else grad_out
             rs(2, last, mat).wait_recv()
             summed = keep_sum[mat] + recv_three[last % 2, mat].astype(WIDE)
-            for i in range(last):
+            for i in range(1, last):
                 rs(3, i, mat).wait_recv()
-                summed = summed + recv_four[i, mat].astype(WIDE)
+                summed = summed + recv_four[i - 1, mat].astype(WIDE)
             result[...] = summed
 
     tile = chunk // 3
@@ -595,34 +589,38 @@
                 total[2 * r + h] += up[h * lot : h * lot + patches]
                 grad_zed[2 * r + h] += down[h * lot : h * lot + patches]
 
-            @pl.when((r == 0) & (i == 0) & (planes > 2))
+            @pl.when((r == 0) & (i == 1))
             def _():
-                ag_forward(2)
-
-            @pl.when((r == 0) & (i + 3 < planes))
+                ag_forward(plane_at(2))
+
+            @pl.when((r == 0) & (i == 3))
             def _():
-                ag_direct(i + 3)
-
-            @pl.when((r == 1) & (i + 2 < planes))
+                rs_four(1)
+
+            @pl.when((r == 1) & (i == 0))
             def _():
-                ag_core(i + 2)
-
-            @pl.when((r == 1) & (i == 0))
+                ag_forward(plane_at(1))
+                ag_direct(plane_at(2))
+
+            @pl.when((r == 1) & (i == 1))
+            def _():
+                ag_core(plane_at(2))
+                for mat in mats:
+                    ag(2, 0, mat).start()
+                ag_forward(0)
+
+            @pl.when((r == 1) & (i == 2))
             def _():
                 ag_core(0)
                 ag_core_last(0)
 
-            @pl.when((r == 1) & (i > 1))
+            @pl.when((r == 2) & (i == 0))
             def _():
-                rs_four(i - 2)
+                ag_core(plane_at(1))
 
             return inner
 
         lax.fori_loop(0, blocks, rows, 0)
-
-        @pl.when(i + 2 < planes)
-        def _():
-            ag_core_last(i + 2)
 
 
         back_sum = jnp.sum(grad_pre[...].astype(WIDE), axis=0, keepdims=True)
@@ -644,13 +642,13 @@
         for mat in mats:
             rs(0, i, mat).start()
 
-        @pl.when(i > 0)
+        @pl.when(i < 2)
+        def _():
+            ag_core_last(plane_at(i + 1))
+
+        @pl.when(i > 1)
         def _():
             rs_three(i - 1)
-
-        @pl.when(i + 3 < planes)
-        def _():
-            ag_forward(i + 3)
 
         own_sum[1] = dot(act[:, 0:half], flat_top, TN)
         own_sum[0] = dot(grad_pre[:, 0:half], flat_zed, TN)
@@ -686,7 +684,7 @@
 
         reload_image(b).start()
 
-        @pl.when((b == 0) & (planes > 1))
+        @pl.when(b == 2)
         def _():
             rs_four(planes - 2)
 
@@ -776,13 +774,12 @@
             for stage in range(1, 6):
                 ag(stage, k, mat).wait_send()
         ag(0, 1, mat).wait_send()
-        if row_of_four:
-
-            @pl.when(inner)
-            def _():
-                ag(0, 3, mat).wait_send()
-                for which in range(3):
-                    ag_pass(which, mat).wait_send()
+
+        @pl.when(inner)
+        def _():
+            ag(0, 3, mat).wait_send()
+            for which in range(3):
+                ag_pass(which, mat).wait_send()
 
     lax.fori_loop(0, count, image_norm, 0)
     late_reduce(0, 0).start()
@@ -824,7 +821,8 @@
     for mat in mats:
         for stage in range(3):
             rs(stage, planes - 1, mat).wait_send()
-        for i in range(max(0, planes - 3), planes - 1):
+        rs(4, 0, mat).wait_send()
+        for i in range(1, planes - 1):
             rs(3, i, mat).wait_send()
     late_reduce(0, 0).wait_send()
     for far in range(1, 4):
@@ -966,7 +964,9 @@
             pltpu.VMEM((2, shard, width), LOW),
             pltpu.VMEM((2, 2, shard, width), LOW),
             pltpu.VMEM((2, 2, shard, width), LOW),
-            pltpu.VMEM((planes - 1, 2, shard, width), LOW),
+            pltpu.VMEM((planes - 2, 2, shard, width), LOW),
+            pltpu.VMEM((2, half, width), LOW),
+            pltpu.VMEM((2, half, width), LOW),
             pltpu.VMEM((pad, hidden_tok), WIDE),
             pltpu.VMEM((hidden_tok, pad), LOW),
             pltpu.VMEM((hidden_pad, pad), WIDE),
@@ -992,8 +992,8 @@
             pltpu.SemaphoreType.DMA((4, count)),
             pltpu.SemaphoreType.DMA((7, planes, 2)),
             pltpu.SemaphoreType.DMA((7, planes, 2)),
-            pltpu.SemaphoreType.DMA((4, planes, 2)),
-            pltpu.SemaphoreType.DMA((4, planes, 2)),
+            pltpu.SemaphoreType.DMA((5, planes, 2)),
+            pltpu.SemaphoreType.DMA((5, planes, 2)),
         ]
         + [pltpu.SemaphoreType.DMA((3, max(4, planes), 2))] * 2
         + [pltpu.SemaphoreType.DMA((3, max(4, planes)))] * 6,
@@ -1064,7 +1064,7 @@
     unit = math.gcd(w_token_in.shape[0], hidden_tok)
     return (
         devices % PLANE == 0
-        and planes in (2, 4)
+        and planes == 4
         and images.shape[0] % 2 == 0
         and images.shape[0] <= 2 * planes
         and shard % 16 == 0

time: 112 us -> 106 us (0.946)
  Pallas kernels: 111 us -> 105 us
    pallas_call x1, Pallas kernels: 107 us -> 101 us  [fast_shards(): pl.pallas_call(block_kernel, out_shape=(pltpu.VMEM(images.shape, WIDE), p...]
where the time goes in v5:
time: 106 us
  Pallas kernels  105 us (99%)
    pallas_call x1, Pallas kernels, fast_shards(): pl.pallas_call(block_kernel, out_shape=(pltpu.VMEM(images.shape, WIDE), p...  101 us
    pallas_call x1, Pallas kernels, fast_shards(): pl.pallas_call(finish_kernel, out_shape=(shape(images.shape, WIDE), shape...  3.96 us

profile of v5, /device:TPU:0, one launch (start us, length us, event | category | flops | bytes accessed | tf_op | source)
XLA Modules:
  0.0 105.5 jit_solution(7420905848125590322)
XLA Ops:
  0.7 100.9 %shard_map.254 = (f32[6,196,768]{2,1,0:T(8,128)S(1)}, f32[6,196,768]{2,1,0:T(8,128)S(1)}, f32[96,768]{1,0:T(8,128)S(1)}, f32[96,768]{1,0:T(8,128)S(1)}, f32[64,128]{1,0:T(8,128)S(1)}, /*index=5*/f32[8,128]{1,0:T(8,128)S(1)}) custom-call(s32[6]{0:T(128)} %mask.1, f32[6,196,768]{2,1,0:T(8,128)} %images.1, f32[6,196,768]{2,1,0:T(8,128)} %cotangent.1, ...), custom_call_target="tpu_custom_call" | custom-call | tf_op jit(solution)/shard_map/pallas_call | solution.py:934
  101.6 4.0 %shard_map.255 = (f32[6,196,768]{2,1,0:T(8,128)}, f32[6,196,768]{2,1,0:T(8,128)}, f32[96,768]{1,0:T(8,128)}, f32[96,768]{1,0:T(8,128)}, f32[2352]{0:T(1024)}, /*...) custom-call(f32[6,196,768]{2,1,0:T(8,128)S(1)} %get-tuple-element.34, ...), custom_call_target="tpu_custom_call" | custom-call | tf_op jit(solution)/shard_map/pallas_call | solution.py:1020

commit v6 on v5

--- a/solution.py
+++ b/solution.py
@@ -18,6 +18,13 @@
     return 0.5 * (1.0 + lax.erf(v * 0.7071067811865476)) + v * 0.3989422804014327 * jnp.exp(
         -0.5 * v * v
     )
+
+
+def norm_parts(v):
+    middle = jnp.mean(v, axis=-1, keepdims=True)
+    centered = v - middle
+    scale = lax.rsqrt(jnp.mean(centered * centered, axis=-1, keepdims=True) + EPS)
+    return (centered * scale, middle, scale)
 
 
 def normalize(v):
@@ -100,7 +107,6 @@
     recv_three,
     send_four,
     recv_four,
-    send_far,
     recv_far,
     tin,
     tin_t,
@@ -123,7 +129,7 @@
     biases_in,
     late,
     late_in,
-    scales,
+    figures,
     in_sem,
     ag_send,
     ag_recv,
@@ -144,9 +150,9 @@
     half = 4 * shard
     chunk = 8 * shard
     pad = mixed.shape[1]
-    pair = zed.shape[1]
+    blocks = count // 2
+    pair = zed.shape[0] // blocks
     lot = pair // 2
-    blocks = count // 2
     me = lax.axis_index("dp")
     core = me % 2
     col = (me // 2) % 2
@@ -191,8 +197,10 @@
             device_id_type=MESH,
         )
 
+    middle = ((z + 1) // 2) % 2
+
     def plane_at(i):
-        return (i + 1) % planes
+        return (1 - middle) * ((i + 1) % planes) + middle * (planes - 1 - i)
 
     def rs(stage, i, mat):
         slot, k = i % 2, plane_at(i)
@@ -201,17 +209,30 @@
             lambda: (send_one.at[mat], recv_one.at[slot, mat], by_core),
             lambda: (send_two.at[mat], recv_two.at[slot, mat], near),
             lambda: (send_three.at[mat], recv_three.at[slot, mat], far),
-            lambda: (send_four.at[slot, mat], recv_four.at[i - 1, mat], by_z(k)),
-            lambda: (send_far.at[mat], recv_far.at[mat], by_z(k)),
+            lambda: (send_four.at[slot, mat], recv_four.at[k - 1, mat], by_z(k)),
+            lambda: (weights.at[mat, k, pl.ds(0, half)], recv_far.at[(k - 1) // 2, mat], by_z(k)),
         ][stage]()
+        at = i if stage < 3 else k
         return pltpu.make_async_remote_copy(
             src_ref=src,
             dst_ref=dst,
-            send_sem=rs_send.at[stage, i, mat],
-            recv_sem=rs_recv.at[stage, i, mat],
+            send_sem=rs_send.at[stage, at, mat],
+            recv_sem=rs_recv.at[stage, at, mat],
             device_id=(to,),
             device_id_type=MESH,
         )
+
+    def came_from(stage, k, mat):
+        place = recv_four.at[k - 1, mat] if stage == 3 else recv_far.at[(k - 1) // 2, mat]
+        pltpu.make_async_remote_copy(
+            src_ref=place,
+            dst_ref=place,
+            send_sem=rs_send.at[stage, k, mat],
+            recv_sem=rs_recv.at[stage, k, mat],
+            device_id=(by_z(k),),
+            device_id_type=MESH,
+        ).wait_recv()
+        return place[...].astype(WIDE)
 
     def small_gather(stage, k, group):
         src, dst, to = [
@@ -228,17 +249,17 @@
             device_id_type=MESH,
         )
 
-    def small_reduce(stage, k):
+    def small_reduce(stage, k, group):
         src, dst, to = [
-            lambda: (small_all.at[:, pl.ds(4, 4)], small_core, by_core),
-            lambda: (small_all.at[:, k], small_plane.at[:, k], (me, by_x, by_y, by_both)[k]),
-            lambda: (small_all.at[:, 0, k], small_z.at[k], by_z(k)),
+            lambda: (small_all.at[group, pl.ds(4, 4)], small_core.at[group], by_core),
+            lambda: (small_all.at[group, k], small_plane.at[group, k], (me, by_x, by_y, by_both)[k]),
+            lambda: (small_all.at[group, 0, k], small_z.at[k, group], by_z(k)),
         ][stage]()
         return pltpu.make_async_remote_copy(
             src_ref=src,
             dst_ref=dst,
-            send_sem=ss_send.at[stage, k],
-            recv_sem=ss_recv.at[stage, k],
+            send_sem=ss_send.at[stage, k, group],
+            recv_sem=ss_recv.at[stage, k, group],
             device_id=(to,),
             device_id_type=MESH,
         )
@@ -322,7 +343,7 @@
     pl.semaphore_wait(barrier, len(peers))
 
     mats = (0, 1)
-    inner = (z == 1) | (z == 2)
+    inner = middle == 1
 
     def ag_pass(which, mat):
         src, dst, to = ((1, 2, by_z(3)), (3, 2, by_z(1)), (2, 3, by_z(1)))[which]
@@ -406,13 +427,14 @@
             b = 2 * r + h
             load_top(b).wait()
             tops.append(padded(total[b] * mask[b].astype(WIDE), lot))
-        top[r] = jnp.concatenate(tops, axis=0).astype(LOW)
-        grad_vecs[2:3, :] += jnp.sum(top[r].astype(WIDE), axis=0, keepdims=True)
+        rounded = jnp.concatenate(tops, axis=0).astype(LOW)
+        top[pl.ds(r * pair, pair), :] = rounded
+        grad_vecs[2:3, :] += jnp.sum(rounded.astype(WIDE), axis=0, keepdims=True)
         return carry
 
     def first_norm(b, carry):
         load(b).wait()
-        mid[b] = normalize(grad_zed[b])[0]
+        mid[b], figures[b, :, 0:1], figures[b, :, 1:2] = norm_parts(grad_zed[b])
         return carry
 
     lax.fori_loop(0, blocks, channel_top, 0)
@@ -474,29 +496,44 @@
 
     gain_one, shift_one = vecs[0:1, :], vecs[1:2, :]
     gain_two, shift_two, c_four = vecs[2:3, :], vecs[3:4, :], vecs[4:5, :]
-    def token_forward(b, carry):
+    def singles(work, start, stop):
+        def one(b, carry):
+            work(b)
+            return carry
+
+        lax.fori_loop(start, stop, one, 0)
+
+    def pairs(work, start, stop):
+        def two(r, carry):
+            for h in range(2):
+                work(2 * r + h)
+            return carry
+
+        lax.fori_loop(start // 2, stop // 2, two, 0)
+
+    def token_forward(b):
         fed = mid[b] * gain_one + shift_one
         mixed[b] = padded(jnp.concatenate([fed, ones], axis=0), pad).astype(LOW)
         value, slope = gelu_parts(dot(tin_t[...], mixed[b], NN))
         act_t[b] = padded(jnp.concatenate([value, ones], axis=0), act_t.shape[1]).astype(LOW)
         slope_t[b] = slope.astype(LOW)
         mid[b] = grad_zed[b] + dot(tout_t[...], act_t[b], NN)[0:patches]
-        return carry
 
     def channel_inputs(r, carry):
         parts = []
         for h in range(2):
-            normed, _ = normalize(mid[2 * r + h])
             total[2 * r + h] = mid[2 * r + h] + c_four
+            normed, _, figures[2 * r + h, :, 2:3] = norm_parts(mid[2 * r + h])
+            mid[2 * r + h] = normed
             grad_zed[2 * r + h] = jnp.zeros((patches, width), WIDE)
             parts.append(padded(normed * gain_two + shift_two, lot))
-        zed[r] = jnp.concatenate(parts, axis=0).astype(LOW)
+        zed[pl.ds(r * pair, pair), :] = jnp.concatenate(parts, axis=0).astype(LOW)
         return carry
 
-    first = 2 * count // 3
-    lax.fori_loop(0, first, token_forward, 0)
+    first = 4
+    singles(token_forward, 0, first)
     ag_forward(plane_at(0))
-    lax.fori_loop(first, count, token_forward, 0)
+    singles(token_forward, first, count)
     ag_core(plane_at(0))
     ag_planes_last()
     lax.fori_loop(0, blocks, channel_inputs, 0)
@@ -512,17 +549,20 @@
 
     def rs_two(i, mat):
         rs(0, i, mat).wait_recv()
-        own_sum[mat] += recv_one[i % 2, mat].astype(WIDE)
+        slot = i % 2
+        first, second = (1, 3) if mat == 0 else (2, 3)
+
+        def part(n):
+            return slice(n * shard, (n + 1) * shard)
 
         @pl.when(i == 0)
         def _():
-            send_far[mat] = own_sum[mat].astype(LOW)
+            weights[mat, plane_at(i), 0:half] = (own_sum[mat] + recv_one[slot, mat].astype(WIDE)).astype(LOW)
             rs(4, 0, mat).start()
 
-        @pl.when(i == planes - 1)
-        def _():
-            rs(4, 0, mat).wait_recv()
-            own_sum[mat] += recv_far[mat].astype(WIDE)
+        @pl.when((i == planes - 1) & inner)
+        def _():
+            own_sum[mat] += came_from(4, 1, mat) + came_from(4, 3, mat)
 
         @pl.when(i > 1)
         def _():
@@ -530,10 +570,11 @@
 
         @pl.when(i > 0)
         def _():
-            first, second = (1, 3) if mat == 0 else (2, 3)
-            send_two[mat, 0:shard] = own_sum[mat, first * shard : (first + 1) * shard].astype(LOW)
-            send_two[mat, shard : 2 * shard] = own_sum[mat, second * shard : (second + 1) * shard].astype(LOW)
+            for n, to in ((first, part(0)), (second, part(1))):
+                send_two[mat, to] = (own_sum[mat, part(n)] + recv_one[slot, mat, part(n)].astype(WIDE)).astype(LOW)
             rs(1, i, mat).start()
+            for n in (0, 3 - first):
+                own_sum[mat, part(n)] += recv_one[slot, mat, part(n)].astype(WIDE)
 
     def rs_three(i):
         for mat in mats:
@@ -564,10 +605,12 @@
             result = grad_in if mat == 0 else grad_out
             rs(2, last, mat).wait_recv()
             summed = keep_sum[mat] + recv_three[last % 2, mat].astype(WIDE)
-            for i in range(1, last):
-                rs(3, i, mat).wait_recv()
-                summed = summed + recv_four[i - 1, mat].astype(WIDE)
-            result[...] = summed
+            result[...] = summed + came_from(3, 2, mat)
+
+            @pl.when(jnp.logical_not(inner))
+            def _():
+                result[...] += came_from(3, 1, mat) + came_from(3, 3, mat)
+
 
     tile = chunk // 3
 
@@ -575,53 +618,53 @@
         k = plane_at(i)
         ag_ready(k)
 
-        def rows(r, inner):
+        def rows(r):
             for s in range(3):
                 part = slice(s * tile, (s + 1) * tile)
-                pre = dot(zed[r], weights[0, k, part], NT) + c_in_rel[k, :, part]
+                pre = dot(zed[r * pair : (r + 1) * pair, :], weights[0, k, part], NT) + c_in_rel[k, :, part]
                 value, slope = gelu_parts(pre)
-                act[pl.ds(r * pair, pair), part] = value.astype(LOW)
-                back = (dot(top[r], weights[1, k, part], NT) * slope).astype(LOW)
-                grad_pre[pl.ds(r * pair, pair), part] = back
-            up = dot(act[pl.ds(r * pair, pair), :], weights[1, k], NN)
-            down = dot(grad_pre[pl.ds(r * pair, pair), :], weights[0, k], NN)
+                act[r * pair : (r + 1) * pair, part] = value.astype(LOW)
+                back = (dot(top[r * pair : (r + 1) * pair, :], weights[1, k, part], NT) * slope).astype(LOW)
+                grad_pre[r * pair : (r + 1) * pair, part] = back
+            up = dot(act[r * pair : (r + 1) * pair, :], weights[1, k], NN)
+            down = dot(grad_pre[r * pair : (r + 1) * pair, :], weights[0, k], NN)
             for h in range(2):
                 total[2 * r + h] += up[h * lot : h * lot + patches]
                 grad_zed[2 * r + h] += down[h * lot : h * lot + patches]
 
-            @pl.when((r == 0) & (i == 1))
-            def _():
-                ag_forward(plane_at(2))
-
-            @pl.when((r == 0) & (i == 3))
-            def _():
-                rs_four(1)
-
-            @pl.when((r == 1) & (i == 0))
-            def _():
-                ag_forward(plane_at(1))
-                ag_direct(plane_at(2))
-
-            @pl.when((r == 1) & (i == 1))
-            def _():
-                ag_core(plane_at(2))
-                for mat in mats:
-                    ag(2, 0, mat).start()
-                ag_forward(0)
-
-            @pl.when((r == 1) & (i == 2))
-            def _():
-                ag_core(0)
-                ag_core_last(0)
-
-            @pl.when((r == 2) & (i == 0))
-            def _():
-                ag_core(plane_at(1))
-
-            return inner
-
-        lax.fori_loop(0, blocks, rows, 0)
-
+        rows(0)
+
+        @pl.when(i == 0)
+        def _():
+            ag_forward(plane_at(1))
+
+        @pl.when(i == 1)
+        def _():
+            ag_forward(plane_at(2))
+            ag_forward(0)
+
+        @pl.when(i == 3)
+        def _():
+            rs_four(1)
+
+        for r in range(1, blocks):
+            rows(r)
+
+        @pl.when(i == 0)
+        def _():
+            ag_core(plane_at(1))
+            ag_direct(plane_at(2))
+            for mat in mats:
+                ag(2, 0, mat).start()
+
+        @pl.when(i == 1)
+        def _():
+            ag_core(plane_at(2))
+
+        @pl.when(i == 2)
+        def _():
+            ag_core(0)
+            ag_core_last(0)
 
         back_sum = jnp.sum(grad_pre[...].astype(WIDE), axis=0, keepdims=True)
         for place in range(PLANE):
@@ -630,28 +673,36 @@
             )
             grad_c_in[near] = back_sum[:, place * shard : (place + 1) * shard]
 
-        flat_top = top[...].reshape(blocks * pair, width)
-        flat_zed = zed[...].reshape(blocks * pair, width)
         @pl.when(i > 0)
         def _():
             for mat in mats:
                 rs(0, i - 1, mat).wait_send()
 
-        send_one[1] = dot(act[:, half:chunk], flat_top, TN).astype(LOW)
-        send_one[0] = dot(grad_pre[:, half:chunk], flat_zed, TN).astype(LOW)
+        send_one[1] = dot(act[:, half:chunk], top[...], TN).astype(LOW)
+        send_one[0] = dot(grad_pre[:, half:chunk], zed[...], TN).astype(LOW)
         for mat in mats:
             rs(0, i, mat).start()
 
+        @pl.when(i > 1)
+        def _():
+            rs_three(i - 1)
+
+        @pl.when(i == 0)
+        def _():
+            for mat in mats:
+                for stage in range(1, 6):
+                    ag(stage, k, mat).wait_send()
+
+                @pl.when(inner)
+                def _():
+                    ag_pass(1, mat).wait_send()
+
+        own_sum[1] = dot(act[:, 0:half], top[...], TN)
+        own_sum[0] = dot(grad_pre[:, 0:half], zed[...], TN)
         @pl.when(i < 2)
         def _():
             ag_core_last(plane_at(i + 1))
 
-        @pl.when(i > 1)
-        def _():
-            rs_three(i - 1)
-
-        own_sum[1] = dot(act[:, 0:half], flat_top, TN)
-        own_sum[0] = dot(grad_pre[:, 0:half], flat_zed, TN)
         for mat in mats:
             rs_two(i, mat)
         return carry
@@ -663,134 +714,143 @@
     tin_low = tin[...].astype(LOW)
     tout_low = tout[0:hidden_tok, :].astype(LOW)
 
-    def token_backward(b, carry):
+    def kept(b):
+        return weights.at[b // planes, b % planes, 0:pad]
+
+    def middle_backward(b, carry):
         keep = mask[b].astype(WIDE)
-        normed, scale = normalize(mid[b])
+        reload(b).wait()
+        normed = mid[b]
         down = grad_zed[b]
         grad_vecs[0:1, :] += jnp.sum(down * normed, axis=0, keepdims=True)
         grad_vecs[1:2, :] += jnp.sum(down, axis=0, keepdims=True)
-        reload(b).wait()
-        grad_mid = cot[b % 2] * keep + norm_back(down, normed, scale, gain_two)
-
-        @pl.when(b + 2 < count)
-        def _():
-            reload(b + 2).start()
-
+        grad_mid = cot[b % 2] * keep + norm_back(down, normed, figures[b, :, 2:3], gain_two)
+        grad_zed[b] = grad_mid
         back = padded(grad_mid, pad).astype(LOW)
         grad_tout[...] += dot(act_t[b], back, NT)
-        grad_zed[b] = grad_mid
         slope_t[b] = (dot(tout_low, back, NN) * slope_t[b].astype(WIDE)).astype(LOW)
         grad_tin[:, 0:hidden_tok] += dot(mixed[b], slope_t[b], NT)
-
         reload_image(b).start()
 
-        @pl.when(b == 2)
-        def _():
-            rs_four(planes - 2)
+        @pl.when(b + 2 < count)
+        def _():
+            reload(b + 2).start()
 
         return carry
 
-    def image_norm(b, carry):
-        reload_image(b).wait()
-        normed, scale = normalize(mid[b])
+    def token_backward(b):
+        slope_t[b] = (dot(tout_low, kept(b)[...], NN) * slope_t[b].astype(WIDE)).astype(LOW)
+        grad_tin[:, 0:hidden_tok] += dot(mixed[b], slope_t[b], NT)
+
+    def image_norm(b):
+        normed = (mid[b] - figures[b, :, 0:1]) * figures[b, :, 1:2]
         mid[b] = normed
-        scales[b] = scale
-        grad_mixed = dot(tin_low, slope_t[b], NN)[0:patches]
-        weights[b // planes, b % planes, 0:pad] = padded(grad_mixed, pad).astype(LOW)
-        late[0, 0:1, :] += jnp.sum(grad_mixed * normed, axis=0, keepdims=True)
-        late[0, 1:2, :] += jnp.sum(grad_mixed, axis=0, keepdims=True)
-
-        @pl.when(b == 1)
-        def _():
-            small_second()
-
-        return carry
-
-    def image_backward(b, carry):
+        grad_mixed = dot(tin_low, slope_t[b], NN)
+        kept(b)[...] = grad_mixed.astype(LOW)
+        late[0, 0:1, :] += jnp.sum(grad_mixed[0:patches] * normed, axis=0, keepdims=True)
+        late[0, 1:2, :] += jnp.sum(grad_mixed[0:patches], axis=0, keepdims=True)
+
+    def image_backward(b):
         total[b] *= mask[b].astype(WIDE)
-        grad_zed[b] += norm_back(weights[b // planes, b % planes, 0:pad][0:patches].astype(WIDE), mid[b], scales[b], gain_one)
-        return carry
-
-    late[0] = jnp.zeros_like(late[0])
-    lax.fori_loop(0, count, token_backward, 0)
-
-    biases[0] = jnp.zeros_like(biases[0])
-    for i in range(hidden_tok // 128):
-        biases[0, i : i + 1, :] = grad_tin[patches : patches + 1, i * 128 : (i + 1) * 128]
-    biases[0, 3:4, :] = grad_tout[hidden_tok : hidden_tok + 1, 0:128]
-    biases[0, 4:5, 0 : patches - 128] = grad_tout[hidden_tok : hidden_tok + 1, 128:patches]
-    bias_reduce(0, 0).start()
-    for turn in range(turns):
-        lines[pl.ds(turn, patches, stride=turns), :] = grad_tin[0:patches, turn * unit : turn * unit + 128]
-    for d in range(devices):
-        far, k = place_of(d)
-        first, second = small_sum.at[0, far, k], small_sum.at[1, far, k]
-        low = lines[d * lines_in : d * lines_in + first_lines, :]
-        high = lines[d * lines_in + first_lines : (d + 1) * lines_in, :]
-        first[0:first_lines, 0:64] = low[:, 0:64]
-        first[0 : lines_in - first_lines, 64:128] = high[:, 0:64]
-        first[24:27, 64 : 64 + own_vec] = grad_vecs[0:3, d * own_vec : (d + 1) * own_vec]
-        first[31:32, 0:shard] = grad_c_in[d]
-        second[0:lines_out, :] = grad_tout[d * lines_out : (d + 1) * lines_out, 0:128]
-        second[16 : 16 + lines_out, 0 : patches - 128] = grad_tout[d * lines_out : (d + 1) * lines_out, 128:patches]
-    for group in range(2):
+        grad_zed[b] += norm_back(kept(b)[...][0:patches].astype(WIDE), mid[b], figures[b, :, 1:2], gain_one)
+
+    def small_first(group):
         for k in range(1, planes):
             small_gather(0, k, group).wait_send()
         for far in range(1, 4):
             small_gather(1, far, group).wait_send()
         small_gather(2, 0, group).wait_send()
+        if group == 0:
+            for turn in range(turns):
+                lines[pl.ds(turn, patches, stride=turns), :] = grad_tin[0:patches, turn * unit : turn * unit + 128]
+        for d in range(devices):
+            far, k = place_of(d)
+            message = small_sum.at[group, far, k]
+            if group == 0:
+                low = lines[d * lines_in : d * lines_in + first_lines, :]
+                high = lines[d * lines_in + first_lines : (d + 1) * lines_in, :]
+                message[0:first_lines, 0:64] = low[:, 0:64]
+                message[0 : lines_in - first_lines, 64:128] = high[:, 0:64]
+                message[24:27, 64 : 64 + own_vec] = grad_vecs[0:3, d * own_vec : (d + 1) * own_vec]
+                message[31:32, 0:shard] = grad_c_in[d]
+            else:
+                message[0:lines_out, :] = grad_tout[d * lines_out : (d + 1) * lines_out, 0:128]
+                message[16 : 16 + lines_out, 0 : patches - 128] = grad_tout[
+                    d * lines_out : (d + 1) * lines_out, 128:patches
+                ]
         for far in range(4, PLANE):
             small_all[group, far] = small_sum[group, far].astype(LOW)
-    small_reduce(0, 0).start()
-
-    def small_second():
-        bias_reduce(0, 0).wait_recv()
-        biases[1] = biases[0] + biases_in[0, 0]
-        small_reduce(0, 0).wait_recv()
+        small_reduce(0, 0, group).start()
+        if group == 0:
+            biases[0] = jnp.zeros_like(biases[0])
+            for i in range(hidden_tok // 128):
+                biases[0, i : i + 1, :] = grad_tin[patches : patches + 1, i * 128 : (i + 1) * 128]
+            biases[0, 3:4, :] = grad_tout[hidden_tok : hidden_tok + 1, 0:128]
+            biases[0, 4:5, 0 : patches - 128] = grad_tout[hidden_tok : hidden_tok + 1, 128:patches]
+            bias_reduce(0, 0).start()
+
+    def small_second(group):
+        small_reduce(0, 0, group).wait_recv()
         for far in range(4):
-            for group in range(2):
-                small_sum[group, far] += small_core[group, far].astype(WIDE)
+            small_sum[group, far] += small_core[group, far].astype(WIDE)
         for far in range(1, 4):
-            for group in range(2):
-                small_all[group, far] = small_sum[group, far].astype(LOW)
-            small_reduce(1, far).start()
-            bias_reduce(1, far).start()
-
-    def small_third():
+            small_all[group, far] = small_sum[group, far].astype(LOW)
+            small_reduce(1, far, group).start()
+        if group == 0:
+            bias_reduce(0, 0).wait_recv()
+            biases[1] = biases[0] + biases_in[0, 0]
+            for far in range(1, 4):
+                bias_reduce(1, far).start()
+
+    def small_third(group):
         for far in range(1, 4):
-            small_reduce(1, far).wait_recv()
-            bias_reduce(1, far).wait_recv()
-            for group in range(2):
-                small_sum[group, 0] += small_plane[group, far].astype(WIDE)
-        biases[2] = (biases[1] + biases_in[1, 1]) + (biases_in[1, 2] + biases_in[1, 3])
+            small_reduce(1, far, group).wait_recv()
+            small_sum[group, 0] += small_plane[group, far].astype(WIDE)
         for k in range(1, planes):
-            for group in range(2):
-                small_all[group, 0, k] = small_sum[group, 0, k].astype(LOW)
-            small_reduce(2, k).start()
-            bias_reduce(2, k).start()
+            small_all[group, 0, k] = small_sum[group, 0, k].astype(LOW)
+            small_reduce(2, k, group).start()
+        if group == 0:
+            for far in range(1, 4):
+                bias_reduce(1, far).wait_recv()
+            biases[2] = (biases[1] + biases_in[1, 1]) + (biases_in[1, 2] + biases_in[1, 3])
+            for k in range(1, planes):
+                bias_reduce(2, k).start()
 
     for mat in mats:
-        for k in range(planes):
+        for i in range(1, planes):
             for stage in range(1, 6):
-                ag(stage, k, mat).wait_send()
+                ag(stage, plane_at(i), mat).wait_send()
         ag(0, 1, mat).wait_send()
+        rs(4, 0, mat).wait_send()
 
         @pl.when(inner)
         def _():
             ag(0, 3, mat).wait_send()
-            for which in range(3):
+            for which in (0, 2):
                 ag_pass(which, mat).wait_send()
 
-    lax.fori_loop(0, count, image_norm, 0)
+    late[0] = jnp.zeros_like(late[0])
+    lax.fori_loop(0, 2, middle_backward, 0)
+    rs_four(planes - 2)
+    lax.fori_loop(2, count, middle_backward, 0)
+    small_first(1)
+    small_first(0)
+    for b in range(count):
+        reload_image(b).wait()
+    pairs(image_norm, 0, 2)
+    small_second(1)
+    pairs(image_norm, 2, count)
+    small_second(0)
     late_reduce(0, 0).start()
-    lax.fori_loop(0, 1, image_backward, 0)
+    pairs(image_backward, 0, 2)
     late_reduce(0, 0).wait_recv()
     late[1] = late[0] + late_in[0, 0]
     for far in range(1, 4):
         late_reduce(1, far).start()
     rs_three(planes - 1)
-    small_third()
-    lax.fori_loop(1, count // 2, image_backward, 0)
+    small_third(1)
+    pairs(image_backward, 2, count)
+    small_third(0)
     late_sum = late[1]
     for far in range(1, 4):
         late_reduce(1, far).wait_recv()
@@ -798,12 +858,12 @@
     late[2] = late_sum
     for k in range(1, planes):
         late_reduce(2, k).start()
-    lax.fori_loop(count // 2, count, image_backward, 0)
     rs_last()
     summed = [small_sum[group, 0, 0] for group in range(2)]
     tree = [biases[2]]
     for k in range(1, planes):
-        small_reduce(2, k).wait_recv()
+        for group in range(2):
+            small_reduce(2, k, group).wait_recv()
         bias_reduce(2, k).wait_recv()
         summed = [summed[group] + small_z[k, group].astype(WIDE) for group in range(2)]
         tree.append(biases_in[2, k])
@@ -821,7 +881,6 @@
     for mat in mats:
         for stage in range(3):
             rs(stage, planes - 1, mat).wait_send()
-        rs(4, 0, mat).wait_send()
         for i in range(1, planes - 1):
             rs(3, i, mat).wait_send()
     late_reduce(0, 0).wait_send()
@@ -829,14 +888,17 @@
         late_reduce(1, far).wait_send()
     for k in range(1, planes):
         late_reduce(2, k).wait_send()
-    small_reduce(0, 0).wait_send()
     bias_reduce(0, 0).wait_send()
     for far in range(1, 4):
-        small_reduce(1, far).wait_send()
         bias_reduce(1, far).wait_send()
     for k in range(1, planes):
-        small_reduce(2, k).wait_send()
         bias_reduce(2, k).wait_send()
+    for group in range(2):
+        small_reduce(0, 0, group).wait_send()
+        for far in range(1, 4):
+            small_reduce(1, far, group).wait_send()
+        for k in range(1, planes):
+            small_reduce(2, k, group).wait_send()
 
 
 def finish_kernel(
@@ -928,6 +990,20 @@
     lines_in = w_token_in.shape[0] // unit
     hidden_pad = hidden_tok + 16
 
+    owned = (
+        w_expand,
+        w_reduce,
+        w_token_in,
+        w_token_out,
+        gain_one,
+        shift_one,
+        gain_two,
+        shift_two,
+        bias_reduce,
+        bias_expand,
+        bias_token_in,
+        bias_token_out,
+    )
     vmem = pl.BlockSpec(memory_space=pltpu.VMEM)
     hbm = pl.BlockSpec(memory_space=pl.ANY)
     shape = jax.ShapeDtypeStruct
@@ -949,8 +1025,8 @@
             pltpu.VMEM((count, hidden_pad, width), LOW),
             pltpu.VMEM((count, hidden_tok, width), LOW),
             pltpu.VMEM(images.shape, WIDE),
-            pltpu.VMEM((blocks, pair, width), LOW),
-            pltpu.VMEM((blocks, pair, width), LOW),
+            pltpu.VMEM((blocks * pair, width), LOW),
+            pltpu.VMEM((blocks * pair, width), LOW),
             pltpu.VMEM((2, planes, chunk, width), LOW),
             pltpu.VMEM((blocks * pair, chunk), LOW),
             pltpu.VMEM((blocks * pair, chunk), LOW),
@@ -964,9 +1040,8 @@
             pltpu.VMEM((2, shard, width), LOW),
             pltpu.VMEM((2, 2, shard, width), LOW),
             pltpu.VMEM((2, 2, shard, width), LOW),
-            pltpu.VMEM((planes - 2, 2, shard, width), LOW),
-            pltpu.VMEM((2, half, width), LOW),
-            pltpu.VMEM((2, half, width), LOW),
+            pltpu.VMEM((planes - 1, 2, shard, width), LOW),
+            pltpu.VMEM((2, 2, half, width), LOW),
             pltpu.VMEM((pad, hidden_tok), WIDE),
             pltpu.VMEM((hidden_tok, pad), LOW),
             pltpu.VMEM((hidden_pad, pad), WIDE),
@@ -988,34 +1063,23 @@
             pltpu.VMEM((3, max(4, planes), 8, 128), WIDE),
             pltpu.VMEM((3, 2, width), WIDE),
             pltpu.VMEM((3, max(4, planes), 2, width), WIDE),
-            pltpu.VMEM((count, patches, 1), WIDE),
+            pltpu.VMEM((count, patches, 4), WIDE),
             pltpu.SemaphoreType.DMA((4, count)),
             pltpu.SemaphoreType.DMA((7, planes, 2)),
             pltpu.SemaphoreType.DMA((7, planes, 2)),
             pltpu.SemaphoreType.DMA((5, planes, 2)),
             pltpu.SemaphoreType.DMA((5, planes, 2)),
         ]
-        + [pltpu.SemaphoreType.DMA((3, max(4, planes), 2))] * 2
-        + [pltpu.SemaphoreType.DMA((3, max(4, planes)))] * 6,
+        + [pltpu.SemaphoreType.DMA((3, max(4, planes), 2))] * 4
+        + [pltpu.SemaphoreType.DMA((3, max(4, planes)))] * 4,
         compiler_params=pltpu.CompilerParams(
-            collective_id=0, has_side_effects=True, vmem_limit_bytes=55 * 2**20
+            collective_id=0, has_side_effects=True, vmem_limit_bytes=56 * 2**20
         ),
     )(
         mask,
         images,
         cotangent,
-        w_expand,
-        w_reduce,
-        w_token_in,
-        w_token_out,
-        gain_one,
-        shift_one,
-        gain_two,
-        shift_two,
-        bias_reduce,
-        bias_expand,
-        bias_token_in,
-        bias_token_out,
+        *owned,
     )
     flat = pl.pallas_call(
         finish_kernel,
@@ -1066,7 +1130,7 @@
         devices % PLANE == 0
         and planes == 4
         and images.shape[0] % 2 == 0
-        and images.shape[0] <= 2 * planes
+        and 6 <= images.shape[0] <= 2 * planes
         and shard % 16 == 0
         and shard <= 128
         and (4 * shard) % 128 == 0

time: 106 us -> 103 us (0.972)
  Pallas kernels: 105 us -> 102 us
    pallas_call x1, Pallas kernels: 101 us -> 98.3 us  [fast_shards(): pl.pallas_call(block_kernel, out_shape=(pltpu.VMEM(images.shape, WIDE), p...]
where the time goes in v6:
time: 103 us
  Pallas kernels  102 us (99%)
    pallas_call x1, Pallas kernels, fast_shards(): pl.pallas_call(block_kernel, out_shape=(pltpu.VMEM(images.shape, WIDE), p...  98.3 us
    pallas_call x1, Pallas kernels, fast_shards(): pl.pallas_call(finish_kernel, out_shape=(shape(images.shape, WIDE), shape...  3.96 us

profile of v6, /device:TPU:0, one launch (start us, length us, event | category | flops | bytes accessed | tf_op | source)
XLA Modules:
  0.0 103.1 jit_solution(18427296628743065253)
XLA Ops:
  0.7 98.3 %shard_map.254 = (f32[6,196,768]{2,1,0:T(8,128)S(1)}, f32[6,196,768]{2,1,0:T(8,128)S(1)}, f32[96,768]{1,0:T(8,128)S(1)}, f32[96,768]{1,0:T(8,128)S(1)}, f32[64,128]{1,0:T(8,128)S(1)}, /*index=5*/f32[8,128]{1,0:T(8,128)S(1)}) custom-call(s32[6]{0:T(128)} %mask.1, f32[6,196,768]{2,1,0:T(8,128)} %images.1, f32[6,196,768]{2,1,0:T(8,128)} %cotangent.1, ...), custom_call_target="tpu_custom_call" | custom-call | tf_op jit(solution)/shard_map/pallas_call | solution.py:1010
  98.9 4.0 %shard_map.255 = (f32[6,196,768]{2,1,0:T(8,128)}, f32[6,196,768]{2,1,0:T(8,128)}, f32[96,768]{1,0:T(8,128)}, f32[96,768]{1,0:T(8,128)}, f32[2352]{0:T(1024)}, /*...) custom-call(f32[6,196,768]{2,1,0:T(8,128)S(1)} %get-tuple-element.34, ...), custom_call_target="tpu_custom_call" | custom-call | tf_op jit(solution)/shard_map/pallas_call | solution.py:1084

commit v7 on v6

--- a/solution.py
+++ b/solution.py
@@ -86,7 +86,6 @@
     grad_out,
     small_out,
     biases_out,
-    cot,
     mixed,
     act_t,
     slope_t,
@@ -207,12 +206,17 @@
         near, far = (by_x, by_y) if mat == 0 else (by_y, by_x)
         src, dst, to = [
             lambda: (send_one.at[mat], recv_one.at[slot, mat], by_core),
-            lambda: (send_two.at[mat], recv_two.at[slot, mat], near),
+            lambda: (
+                send_two.at[mat, pl.ds(shard, shard)],
+                recv_two.at[slot, mat, pl.ds(shard, shard)],
+                near,
+            ),
             lambda: (send_three.at[mat], recv_three.at[slot, mat], far),
             lambda: (send_four.at[slot, mat], recv_four.at[k - 1, mat], by_z(k)),
             lambda: (weights.at[mat, k, pl.ds(0, half)], recv_far.at[(k - 1) // 2, mat], by_z(k)),
+            lambda: (send_two.at[mat, pl.ds(0, shard)], recv_two.at[slot, mat, pl.ds(0, shard)], near),
         ][stage]()
-        at = i if stage < 3 else k
+        at = k if stage in (3, 4) else i
         return pltpu.make_async_remote_copy(
             src_ref=src,
             dst_ref=dst,
@@ -312,9 +316,6 @@
 
     def reload_image(b):
         return pltpu.make_async_copy(images.at[b], mid.at[b], in_sem.at[3, b])
-
-    def reload(b):
-        return pltpu.make_async_copy(cotangent.at[b], cot.at[b % 2], in_sem.at[2, b])
 
     for b in range(count):
         load_top(b).start()
@@ -566,13 +567,14 @@
 
         @pl.when(i > 1)
         def _():
-            rs(1, i - 1, mat).wait_send()
+            for stage in (1, 5):
+                rs(stage, i - 1, mat).wait_send()
 
         @pl.when(i > 0)
         def _():
-            for n, to in ((first, part(0)), (second, part(1))):
+            for n, to, stage in ((second, part(1), 1), (first, part(0), 5)):
                 send_two[mat, to] = (own_sum[mat, part(n)] + recv_one[slot, mat, part(n)].astype(WIDE)).astype(LOW)
-            rs(1, i, mat).start()
+                rs(stage, i, mat).start()
             for n in (0, 3 - first):
                 own_sum[mat, part(n)] += recv_one[slot, mat, part(n)].astype(WIDE)
 
@@ -585,12 +587,16 @@
             def _():
                 rs(2, i - 1, mat).wait_send()
 
-            keep_sum[mat] = own_sum[mat, 0:shard] + recv_two[i % 2, mat, 0:shard].astype(WIDE)
             send_three[mat] = (
                 own_sum[mat, other * shard : (other + 1) * shard]
                 + recv_two[i % 2, mat, shard : 2 * shard].astype(WIDE)
             ).astype(LOW)
             rs(2, i, mat).start()
+
+    def rs_keep(i):
+        for mat in mats:
+            rs(5, i, mat).wait_recv()
+            keep_sum[mat] = own_sum[mat, 0:shard] + recv_two[i % 2, mat, 0:shard].astype(WIDE)
 
     def rs_four(i):
         for mat in mats:
@@ -616,6 +622,11 @@
 
     def channel_chunk(i, carry):
         k = plane_at(i)
+
+        @pl.when(i == planes - 1)
+        def _():
+            rs_four(1)
+
         ag_ready(k)
 
         def rows(r):
@@ -643,10 +654,6 @@
             ag_forward(plane_at(2))
             ag_forward(0)
 
-        @pl.when(i == 3)
-        def _():
-            rs_four(1)
-
         for r in range(1, blocks):
             rows(r)
 
@@ -665,6 +672,10 @@
         def _():
             ag_core(0)
             ag_core_last(0)
+
+        @pl.when(i > 1)
+        def _():
+            rs_three(i - 1)
 
         back_sum = jnp.sum(grad_pre[...].astype(WIDE), axis=0, keepdims=True)
         for place in range(PLANE):
@@ -685,7 +696,7 @@
 
         @pl.when(i > 1)
         def _():
-            rs_three(i - 1)
+            rs_keep(i - 1)
 
         @pl.when(i == 0)
         def _():
@@ -707,8 +718,6 @@
             rs_two(i, mat)
         return carry
 
-    for b in range(2):
-        reload(b).start()
     lax.fori_loop(0, planes, channel_chunk, 0)
 
     tin_low = tin[...].astype(LOW)
@@ -717,30 +726,25 @@
     def kept(b):
         return weights.at[b // planes, b % planes, 0:pad]
 
-    def middle_backward(b, carry):
-        keep = mask[b].astype(WIDE)
-        reload(b).wait()
+    def middle_backward(b, above):
         normed = mid[b]
         down = grad_zed[b]
         grad_vecs[0:1, :] += jnp.sum(down * normed, axis=0, keepdims=True)
         grad_vecs[1:2, :] += jnp.sum(down, axis=0, keepdims=True)
-        grad_mid = cot[b % 2] * keep + norm_back(down, normed, figures[b, :, 2:3], gain_two)
+        grad_mid = above + norm_back(down, normed, figures[b, :, 2:3], gain_two)
         grad_zed[b] = grad_mid
         back = padded(grad_mid, pad).astype(LOW)
         grad_tout[...] += dot(act_t[b], back, NT)
         slope_t[b] = (dot(tout_low, back, NN) * slope_t[b].astype(WIDE)).astype(LOW)
         grad_tin[:, 0:hidden_tok] += dot(mixed[b], slope_t[b], NT)
-        reload_image(b).start()
-
-        @pl.when(b + 2 < count)
-        def _():
-            reload(b + 2).start()
-
+
+    def middle_pair(r, carry):
+        above = top[pl.ds(r * pair, pair), :].astype(WIDE)
+        for h in range(2):
+            middle_backward(2 * r + h, above[h * lot : h * lot + patches])
+        for h in range(2):
+            reload_image(2 * r + h).start()
         return carry
-
-    def token_backward(b):
-        slope_t[b] = (dot(tout_low, kept(b)[...], NN) * slope_t[b].astype(WIDE)).astype(LOW)
-        grad_tin[:, 0:hidden_tok] += dot(mixed[b], slope_t[b], NT)
 
     def image_norm(b):
         normed = (mid[b] - figures[b, :, 0:1]) * figures[b, :, 1:2]
@@ -830,9 +834,8 @@
                 ag_pass(which, mat).wait_send()
 
     late[0] = jnp.zeros_like(late[0])
-    lax.fori_loop(0, 2, middle_backward, 0)
     rs_four(planes - 2)
-    lax.fori_loop(2, count, middle_backward, 0)
+    lax.fori_loop(0, blocks, middle_pair, 0)
     small_first(1)
     small_first(0)
     for b in range(count):
@@ -848,6 +851,7 @@
     for far in range(1, 4):
         late_reduce(1, far).start()
     rs_three(planes - 1)
+    rs_keep(planes - 1)
     small_third(1)
     pairs(image_backward, 2, count)
     small_third(0)
@@ -879,7 +883,7 @@
     biases_out[...] = tree[0]
 
     for mat in mats:
-        for stage in range(3):
+        for stage in (0, 1, 2, 5):
             rs(stage, planes - 1, mat).wait_send()
         for i in range(1, planes - 1):
             rs(3, i, mat).wait_send()
@@ -924,12 +928,10 @@
     c_two,
     sem,
 ):
-    copies = [
-        pltpu.make_async_copy(block_in, block_out, sem.at[0]),
-        pltpu.make_async_copy(image_in, image_out, sem.at[1]),
-        pltpu.make_async_copy(w_in, w_in_out, sem.at[2]),
-        pltpu.make_async_copy(w_out, w_out_out, sem.at[3]),
-    ]
+    pieces = [(block_in.at[b], block_out.at[b]) for b in range(block_in.shape[0])]
+    pieces += [(image_in.at[b], image_out.at[b]) for b in range(image_in.shape[0])]
+    pieces += [(w_in, w_in_out), (w_out, w_out_out)]
+    copies = [pltpu.make_async_copy(a, b, sem.at[i]) for i, (a, b) in enumerate(pieces)]
     for copy in copies:
         copy.start()
     hidden_tok, patches = c_one.shape[0], c_two.shape[0]
@@ -1020,7 +1022,6 @@
         in_specs=[pl.BlockSpec(memory_space=pltpu.SMEM), hbm, hbm] + [vmem] * 12,
         out_specs=[vmem] * 6,
         scratch_shapes=[
-            pltpu.VMEM((2,) + images.shape[1:], WIDE),
             pltpu.VMEM((count, pad, width), LOW),
             pltpu.VMEM((count, hidden_pad, width), LOW),
             pltpu.VMEM((count, hidden_tok, width), LOW),
@@ -1067,8 +1068,8 @@
             pltpu.SemaphoreType.DMA((4, count)),
             pltpu.SemaphoreType.DMA((7, planes, 2)),
             pltpu.SemaphoreType.DMA((7, planes, 2)),
-            pltpu.SemaphoreType.DMA((5, planes, 2)),
-            pltpu.SemaphoreType.DMA((5, planes, 2)),
+            pltpu.SemaphoreType.DMA((6, planes, 2)),
+            pltpu.SemaphoreType.DMA((6, planes, 2)),
         ]
         + [pltpu.SemaphoreType.DMA((3, max(4, planes), 2))] * 4
         + [pltpu.SemaphoreType.DMA((3, max(4, planes)))] * 4,
@@ -1097,7 +1098,7 @@
         ),
         in_specs=[vmem] * 6,
         out_specs=[hbm] * 4 + [vmem] * 10,
-        scratch_shapes=[pltpu.SemaphoreType.DMA((4,))],
+        scratch_shapes=[pltpu.SemaphoreType.DMA((2 * count + 2,))],
         compiler_params=pltpu.CompilerParams(vmem_limit_bytes=16 * 2**20),
     )(*outs)
     block_output, image_grad, own_win, own_wout, *rest = flat

time: 103 us -> 102 us (level)
  no operation moved by 1% of the time
where the time goes in v7:
time: 102 us
  Pallas kernels  101 us (99%)
    pallas_call x1, Pallas kernels, fast_shards(): pl.pallas_call(block_kernel, out_shape=(pltpu.VMEM(images.shape, WIDE), p...  97.3 us
    pallas_call x1, Pallas kernels, fast_shards(): pl.pallas_call(finish_kernel, out_shape=(shape(images.shape, WIDE), shape...  3.95 us

profile of v7, /device:TPU:0, one launch (start us, length us, event | category | flops | bytes accessed | tf_op | source)
XLA Modules:
  0.0 102.1 jit_solution(7060026468817551177)
XLA Ops:
  0.7 97.3 %shard_map.254 = (f32[6,196,768]{2,1,0:T(8,128)S(1)}, f32[6,196,768]{2,1,0:T(8,128)S(1)}, f32[96,768]{1,0:T(8,128)S(1)}, f32[96,768]{1,0:T(8,128)S(1)}, f32[64,128]{1,0:T(8,128)S(1)}, /*index=5*/f32[8,128]{1,0:T(8,128)S(1)}) custom-call(s32[6]{0:T(128)} %mask.1, f32[6,196,768]{2,1,0:T(8,128)} %images.1, f32[6,196,768]{2,1,0:T(8,128)} %cotangent.1, ...), custom_call_target="tpu_custom_call" | custom-call | tf_op jit(solution)/shard_map/pallas_call | solution.py:1012
  98.0 4.0 %shard_map.255 = (f32[6,196,768]{2,1,0:T(8,128)}, f32[6,196,768]{2,1,0:T(8,128)}, f32[96,768]{1,0:T(8,128)}, f32[96,768]{1,0:T(8,128)}, f32[2352]{0:T(1024)}, /*...) custom-call(f32[6,196,768]{2,1,0:T(8,128)S(1)} %get-tuple-element.34, ...), custom_call_target="tpu_custom_call" | custom-call | tf_op jit(solution)/shard_map/pallas_call | solution.py:1085

commit v8 on v7

--- a/solution.py
+++ b/solution.py
@@ -199,7 +199,8 @@
     middle = ((z + 1) // 2) % 2
 
     def plane_at(i):
-        return (1 - middle) * ((i + 1) % planes) + middle * (planes - 1 - i)
+        last = planes - 1
+        return (1 - middle) * ((i + 1) % planes) + middle * (i % last + last * ((last - i) // last))
 
     def rs(stage, i, mat):
         slot, k = i % 2, plane_at(i)

time: 102 us -> 101 us (level)
  Pallas kernels: 101 us -> 99.6 us
    pallas_call x1, Pallas kernels: 97.3 us -> 95.7 us  [fast_shards(): pl.pallas_call(block_kernel, out_shape=(pltpu.VMEM(images.shape, WIDE), p...]
where the time goes in v8:
time: 101 us; the launch traced here: 100 us
  Pallas kernels  99.6 us (99%)
    pallas_call x1, Pallas kernels, fast_shards(): pl.pallas_call(block_kernel, out_shape=(pltpu.VMEM(images.shape, WIDE), p...  95.7 us
    pallas_call x1, Pallas kernels, fast_shards(): pl.pallas_call(finish_kernel, out_shape=(shape(images.shape, WIDE), shape...  3.95 us

profile of v8, /device:TPU:0, one launch (start us, length us, event | category | flops | bytes accessed | tf_op | source)
XLA Modules:
  0.0 100.5 jit_solution(5343008136868964250)
XLA Ops:
  0.7 95.7 %shard_map.254 = (f32[6,196,768]{2,1,0:T(8,128)S(1)}, f32[6,196,768]{2,1,0:T(8,128)S(1)}, f32[96,768]{1,0:T(8,128)S(1)}, f32[96,768]{1,0:T(8,128)S(1)}, f32[64,128]{1,0:T(8,128)S(1)}, /*index=5*/f32[8,128]{1,0:T(8,128)S(1)}) custom-call(s32[6]{0:T(128)} %mask.1, f32[6,196,768]{2,1,0:T(8,128)} %images.1, f32[6,196,768]{2,1,0:T(8,128)} %cotangent.1, ...), custom_call_target="tpu_custom_call" | custom-call | tf_op jit(solution)/shard_map/pallas_call | solution.py:1013
  96.3 4.0 %shard_map.255 = (f32[6,196,768]{2,1,0:T(8,128)}, f32[6,196,768]{2,1,0:T(8,128)}, f32[96,768]{1,0:T(8,128)}, f32[96,768]{1,0:T(8,128)}, f32[2352]{0:T(1024)}, /*...) custom-call(f32[6,196,768]{2,1,0:T(8,128)S(1)} %get-tuple-element.34, ...), custom_call_target="tpu_custom_call" | custom-call | tf_op jit(solution)/shard_map/pallas_call | solution.py:1086

commit v9 on v8

--- a/solution.py
+++ b/solution.py
@@ -132,6 +132,8 @@
     in_sem,
     ag_send,
     ag_recv,
+    ah_send,
+    ah_recv,
     rs_send,
     rs_recv,
     sg_send,
@@ -347,6 +349,55 @@
     mats = (0, 1)
     inner = middle == 1
 
+    def ag_half(stage, k, part, mat):
+        near, far = (by_x, by_y) if mat == 0 else (by_y, by_x)
+        step = 1 if mat == 0 else 2
+        if stage == 0:
+            src, dst, to = 0, 0, by_z(k)
+        else:
+            src, dst, to = ((0, step, near), (0, 3 - step, far), (step, 3, far))[stage - 1]
+        rows = shard // 2
+        first = part * rows
+        at = (k - 1) // 2 if stage == 0 else 1 + stage
+        return pltpu.make_async_remote_copy(
+            src_ref=weights.at[mat, 0 if stage == 0 else k, pl.ds(src * shard + first, rows)],
+            dst_ref=weights.at[mat, k, pl.ds(dst * shard + first, rows)],
+            send_sem=ah_send.at[at, part, mat],
+            recv_sem=ah_recv.at[at, part, mat],
+            device_id=(to,),
+            device_id_type=MESH,
+        )
+
+    def first_direct(part):
+        k = plane_at(0)
+        for mat in mats:
+            ag_half(0, k, part, mat).wait_recv()
+        for mat in mats:
+            ag_half(1, k, part, mat).start()
+
+    def first_far(part):
+        for mat in mats:
+            ag_half(2, plane_at(0), part, mat).start()
+
+    def first_forward(part):
+        for mat in mats:
+            ag_half(1, plane_at(0), part, mat).wait_recv()
+            ag_half(3, plane_at(0), part, mat).start()
+
+    def first_core():
+        k = plane_at(0)
+        for mat in mats:
+            for part in range(2):
+                ag_half(2, k, part, mat).wait_recv()
+            ag(4, k, mat).start()
+
+    def first_core_last():
+        k = plane_at(0)
+        for mat in mats:
+            for part in range(2):
+                ag_half(3, k, part, mat).wait_recv()
+            ag(5, k, mat).start()
+
     def ag_pass(which, mat):
         src, dst, to = ((1, 2, by_z(3)), (3, 2, by_z(1)), (2, 3, by_z(1)))[which]
         return pltpu.make_async_remote_copy(
@@ -359,21 +410,24 @@
         )
 
     def ag_planes():
-        for mat in mats:
-            ag(0, 1, mat).start()
-
-        @pl.when(inner)
-        def _():
+        for part in range(2):
             for mat in mats:
-                ag(0, 3, mat).start()
+                ag_half(0, 1, part, mat).start()
+
+            @pl.when(inner)
+            def _():
+                for mat in mats:
+                    ag_half(0, 3, part, mat).start()
 
     def ag_planes_pass():
         @pl.when(inner)
         def _():
-            for which, came in ((0, 1), (1, 3)):
-                for mat in mats:
-                    ag(0, came, mat).wait_recv()
-                    ag_pass(which, mat).start()
+            for mat in mats:
+                for part in range(2):
+                    ag_half(0, 1, part, mat).wait_recv()
+                ag_pass(0, mat).start()
+            for mat in mats:
+                ag_pass(1, mat).start()
 
     def ag_planes_last():
         @pl.when(inner)
@@ -449,6 +503,8 @@
     for k in range(1, 4):
         small_gather(1, k, 0).wait_recv()
     small_gather(2, 0, 0).start()
+    first_direct(0)
+    first_far(0)
 
     tin[...] = jnp.zeros_like(tin)
     tout[...] = jnp.zeros_like(tout)
@@ -479,8 +535,8 @@
         small_gather(1, k, 1).wait_recv()
     small_gather(2, 0, 1).start()
     unpack_half(True, 1)
+    first_direct(1)
     ag_planes_pass()
-    ag_direct(plane_at(0))
     for group in range(2):
         small_gather(2, 0, group).wait_recv()
         unpack_half(False, group)
@@ -532,14 +588,17 @@
         zed[pl.ds(r * pair, pair), :] = jnp.concatenate(parts, axis=0).astype(LOW)
         return carry
 
-    first = 4
+    first = 3
+    first_forward(0)
+    first_far(1)
     singles(token_forward, 0, first)
-    ag_forward(plane_at(0))
+    first_forward(1)
     singles(token_forward, first, count)
-    ag_core(plane_at(0))
+    first_core()
     ag_planes_last()
+    ag_direct(plane_at(1))
     lax.fori_loop(0, blocks, channel_inputs, 0)
-    ag_direct(plane_at(1))
+    first_core_last()
     for k in range(planes):
         for place in range(PLANE):
             near = plane_of(k) * PLANE + (
@@ -547,7 +606,6 @@
             )
             c_in_rel[k, :, place * shard : (place + 1) * shard] = c_in[near]
 
-    ag_core_last(plane_at(0))
 
     def rs_two(i, mat):
         rs(0, i, mat).wait_recv()
@@ -678,18 +736,17 @@
         def _():
             rs_three(i - 1)
 
+        @pl.when(i > 0)
+        def _():
+            for mat in mats:
+                rs(0, i - 1, mat).wait_send()
+
         back_sum = jnp.sum(grad_pre[...].astype(WIDE), axis=0, keepdims=True)
         for place in range(PLANE):
             near = plane_of(k) * PLANE + (
                 (row + (place // 2) % 2) % 2 * 4 + (col + place % 2) % 2 * 2 + (core + place // 4) % 2
             )
             grad_c_in[near] = back_sum[:, place * shard : (place + 1) * shard]
-
-        @pl.when(i > 0)
-        def _():
-            for mat in mats:
-                rs(0, i - 1, mat).wait_send()
-
         send_one[1] = dot(act[:, half:chunk], top[...], TN).astype(LOW)
         send_one[0] = dot(grad_pre[:, half:chunk], zed[...], TN).astype(LOW)
         for mat in mats:
@@ -702,8 +759,11 @@
         @pl.when(i == 0)
         def _():
             for mat in mats:
-                for stage in range(1, 6):
+                for stage in (4, 5):
                     ag(stage, k, mat).wait_send()
+                for stage in range(1, 4):
+                    for part in range(2):
+                        ag_half(stage, k, part, mat).wait_send()
 
                 @pl.when(inner)
                 def _():
@@ -825,12 +885,14 @@
         for i in range(1, planes):
             for stage in range(1, 6):
                 ag(stage, plane_at(i), mat).wait_send()
-        ag(0, 1, mat).wait_send()
+        for part in range(2):
+            ag_half(0, 1, part, mat).wait_send()
         rs(4, 0, mat).wait_send()
 
         @pl.when(inner)
         def _():
-            ag(0, 3, mat).wait_send()
+            for part in range(2):
+                ag_half(0, 3, part, mat).wait_send()
             for which in (0, 2):
                 ag_pass(which, mat).wait_send()
 
@@ -1069,6 +1131,8 @@
             pltpu.SemaphoreType.DMA((4, count)),
             pltpu.SemaphoreType.DMA((7, planes, 2)),
             pltpu.SemaphoreType.DMA((7, planes, 2)),
+            pltpu.SemaphoreType.DMA((5, 2, 2)),
+            pltpu.SemaphoreType.DMA((5, 2, 2)),
             pltpu.SemaphoreType.DMA((6, planes, 2)),
             pltpu.SemaphoreType.DMA((6, planes, 2)),
         ]
@@ -1133,7 +1197,7 @@
         and planes == 4
         and images.shape[0] % 2 == 0
         and 6 <= images.shape[0] <= 2 * planes
-        and shard % 16 == 0
+        and shard % 32 == 0
         and shard <= 128
         and (4 * shard) % 128 == 0
         and 128 < patches <= 205

time: 101 us -> 99.6 us (0.986)
    pallas_call x1, Pallas kernels: 95.7 us -> 94.7 us  [fast_shards(): pl.pallas_call(block_kernel, out_shape=(pltpu.VMEM(images.shape, WIDE), p...]
where the time goes in v9:
time: 99.6 us; the launch traced here: 99.4 us
  Pallas kernels  98.6 us (99%)
    pallas_call x1, Pallas kernels, fast_shards(): pl.pallas_call(block_kernel, out_shape=(pltpu.VMEM(images.shape, WIDE), p...  94.7 us
    pallas_call x1, Pallas kernels, fast_shards(): pl.pallas_call(finish_kernel, out_shape=(shape(images.shape, WIDE), shape...  3.95 us

profile of v9, /device:TPU:0, one launch (start us, length us, event | category | flops | bytes accessed | tf_op | source)
XLA Modules:
  0.0 99.4 jit_solution(9137974133248314578)
XLA Ops:
  0.7 94.7 %shard_map.254 = (f32[6,196,768]{2,1,0:T(8,128)S(1)}, f32[6,196,768]{2,1,0:T(8,128)S(1)}, f32[96,768]{1,0:T(8,128)S(1)}, f32[96,768]{1,0:T(8,128)S(1)}, f32[64,128]{1,0:T(8,128)S(1)}, /*index=5*/f32[8,128]{1,0:T(8,128)S(1)}) custom-call(s32[6]{0:T(128)} %mask.1, f32[6,196,768]{2,1,0:T(8,128)} %images.1, f32[6,196,768]{2,1,0:T(8,128)} %cotangent.1, ...), custom_call_target="tpu_custom_call" | custom-call | tf_op jit(solution)/shard_map/pallas_call | solution.py:1075
  95.3 4.0 %shard_map.255 = (f32[6,196,768]{2,1,0:T(8,128)}, f32[6,196,768]{2,1,0:T(8,128)}, f32[96,768]{1,0:T(8,128)}, f32[96,768]{1,0:T(8,128)}, f32[2352]{0:T(1024)}, /*...) custom-call(f32[6,196,768]{2,1,0:T(8,128)S(1)} %get-tuple-element.34, ...), custom_call_target="tpu_custom_call" | custom-call | tf_op jit(solution)/shard_map/pallas_call | solution.py:1150

commit v10 on v9

--- a/solution.py
+++ b/solution.py
@@ -57,7 +57,7 @@
 
 def gelu_parts(v):
     cdf = 0.5 * (1.0 + lax.erf(v * 0.7071067811865476))
-    return v * cdf, cdf + v * 0.3989422804014327 * jnp.exp(-0.5 * v * v)
+    return v * cdf, cdf + v * 0.3989422804014327 * jnp.exp2(v * v * -0.7213475204444817)
 
 
 def padded(v, rows):
@@ -710,6 +710,8 @@
 
         @pl.when(i == 1)
         def _():
+            for mat in mats:
+                rs_two(i - 1, mat)
             ag_forward(plane_at(2))
             ag_forward(0)
 
@@ -775,8 +777,11 @@
         def _():
             ag_core_last(plane_at(i + 1))
 
-        for mat in mats:
-            rs_two(i, mat)
+        @pl.when(i > 0)
+        def _():
+            for mat in mats:
+                rs_two(i, mat)
+
         return carry
 
     lax.fori_loop(0, planes, channel_chunk, 0)

time: 99.6 us -> 99.2 us (level)
  no operation moved by 1% of the time
where the time goes in v10:
time: 99.2 us; the launch traced here: 99 us
  Pallas kernels  98.2 us (99%)
    pallas_call x1, Pallas kernels, fast_shards(): pl.pallas_call(block_kernel, out_shape=(pltpu.VMEM(images.shape, WIDE), p...  94.2 us
    pallas_call x1, Pallas kernels, fast_shards(): pl.pallas_call(finish_kernel, out_shape=(shape(images.shape, WIDE), shape...  3.95 us

profile of v10, /device:TPU:0, one launch (start us, length us, event | category | flops | bytes accessed | tf_op | source)
XLA Modules:
  0.0 99.0 jit_solution(16339528434795364413)
XLA Ops:
  0.7 94.2 %shard_map.254 = (f32[6,196,768]{2,1,0:T(8,128)S(1)}, f32[6,196,768]{2,1,0:T(8,128)S(1)}, f32[96,768]{1,0:T(8,128)S(1)}, f32[96,768]{1,0:T(8,128)S(1)}, f32[64,128]{1,0:T(8,128)S(1)}, /*index=5*/f32[8,128]{1,0:T(8,128)S(1)}) custom-call(s32[6]{0:T(128)} %mask.1, f32[6,196,768]{2,1,0:T(8,128)} %images.1, f32[6,196,768]{2,1,0:T(8,128)} %cotangent.1, ...), custom_call_target="tpu_custom_call" | custom-call | tf_op jit(solution)/shard_map/pallas_call | solution.py:1080
  94.9 4.0 %shard_map.255 = (f32[6,196,768]{2,1,0:T(8,128)}, f32[6,196,768]{2,1,0:T(8,128)}, f32[96,768]{1,0:T(8,128)}, f32[96,768]{1,0:T(8,128)}, f32[2352]{0:T(1024)}, /*...) custom-call(f32[6,196,768]{2,1,0:T(8,128)S(1)} %get-tuple-element.34, ...), custom_call_target="tpu_custom_call" | custom-call | tf_op jit(solution)/shard_map/pallas_call | solution.py:1155
